TPU v7x, 512 devices: a whole 4x8x8 slice. The times are simulated.
512 devices in a mesh: dp: 8 (over y), row: 8 (over z_lo, core), col: 8 (over z_hi, x).
Axes of the slice: x: 4, y: 8, z: 8 (z_hi: 2, z_lo: 4; z = z_hi * 4 + z_lo), core: 2. Of those that a mesh axis runs over, the one named last changes fastest.
Arguments:
- block_input: bfloat16 [8, 128, 256, 192], P('dp', 'row', 'col'), may hold values from -6 to 6
- grad_out: bfloat16 [8, 128, 256, 192], P('dp', 'row', 'col'), may hold values from -6 to 6
- region_ids: int32 [128, 256], P('row', 'col'), may hold values from 0 to 9, as said below
- layernorm_scale: float32 [192], replicated, may hold values from 0.25 to 1.75
- layernorm_bias: float32 [192], replicated, may hold values from -3 to 3
- qkv_weight: bfloat16 [192, 576], replicated, may hold values from -0.4375 to 0.4375
- qkv_bias: float32 [576], replicated, may hold values from -3 to 3
- proj_weight: bfloat16 [192, 192], replicated, may hold values from -0.4375 to 0.4375
- bias_table: float32 [225, 6], replicated, may hold values from -4 to 4
- position_index: int32 [64, 64], replicated, may hold values from 0 to 224, as said below
Outputs:
- grad_x: bfloat16 [8, 128, 256, 192], P('dp', 'row', 'col')
- grad_qkv_weight: float32 [192, 576], replicated
- grad_qkv_bias: float32 [576], replicated
- grad_proj_weight: float32 [192, 192], replicated
- grad_proj_bias: float32 [192], replicated
- gradient_norm_scale: float32 [192], replicated
- grad_norm_bias: float32 [192], replicated
- grad_table: float32 [225, 6], replicated
Inputs may be any that keep to these rules, and one draw needn't show every extreme that they name: `region_ids`: each id marks one region of the shifted image. The regions are the three row bands split at 120 and 124, crossed with the three column bands split at 248 and 252, plus one region of padded pixels. The padded pixels are 1 to 3 rows just before row 124 and 1 to 3 columns just before column 252. Every window outside the last window row and column of the image holds a single id. `position_index`: pixel pairs of a window with the same row offset and the same column offset share an entry; distinct offset pairs have distinct entries.
All inputs are finite; a program needn't handle non-finite values.
Results may differ from a plain program's by a relative error of at most 0.011.
Values may be sent and summed in bfloat16 or wider, within the bound.
No kernel may reach another device: no remote copies, remote signals or barrier semaphores. Data moves between devices by JAX's collectives and lax.ppermute only.
A program may use at most 64 MiB of HBM per device.

v0:
```python
import jax
import jax.numpy as jnp
from jax import lax
from jax.sharding import PartitionSpec as P

WIN = 8
SHIFT = 4


def shifted(block, axis, distance):
    devices = range(lax.axis_size(axis))
    route = [((i - distance) % len(devices), i) for i in devices]
    return lax.ppermute(block, axis, route)


def windows(a):
    frames, height, width, chan = a.shape
    a = a.reshape(frames, height // WIN, WIN, width // WIN, WIN, chan)
    return a.transpose(0, 1, 3, 2, 4, 5).reshape(-1, WIN * WIN, chan)


def unwindows(a, frames, height, width):
    chan = a.shape[-1]
    a = a.reshape(frames, height // WIN, width // WIN, WIN, WIN, chan)
    return a.transpose(0, 1, 3, 2, 4, 5).reshape(frames, height, width, chan)


def roll_ahead(field, first_dim, move_rows, move_cols):
    for dim_now, mover in ((first_dim, move_rows), (first_dim + 1, move_cols)):
        length = field.shape[dim_now]
        leading = lax.slice_in_dim(field, 0, SHIFT, axis=dim_now)
        remainder = lax.slice_in_dim(field, SHIFT, length, axis=dim_now)
        field = jnp.concatenate([remainder, mover(leading)], axis=dim_now)
    return field


def roll_behind(field, first_dim, move_rows, move_cols):
    for dim_now, mover in ((first_dim, move_rows), (first_dim + 1, move_cols)):
        length = field.shape[dim_now]
        trailing = lax.slice_in_dim(field, length - SHIFT, length, axis=dim_now)
        remainder = lax.slice_in_dim(field, 0, length - SHIFT, axis=dim_now)
        field = jnp.concatenate([mover(trailing), remainder], axis=dim_now)
    return field


def local_grads(
    shifted_x,
    shifted_grad,
    region_ids,
    layernorm_scale,
    layernorm_bias,
    qkv_weight,
    qkv_bias,
    proj_weight,
    bias_table,
    position_index,
):
    frames, height, width, chan = shifted_x.shape
    heads = bias_table.shape[1]
    head_dim = chan // heads
    count = position_index.shape[0]
    scale = head_dim ** (-0.5)
    wide_type = jnp.float32
    input_float = shifted_x.astype(wide_type)
    mean_x = jnp.mean(input_float, -1, keepdims=True)
    centered_input = input_float - mean_x
    reciprocal_deviation = lax.rsqrt(
        jnp.mean(centered_input * centered_input, -1, keepdims=True) + 1e-05
    )
    standardized_input = centered_input * reciprocal_deviation
    normalized_rows = (standardized_input * layernorm_scale + layernorm_bias).astype(jnp.bfloat16)
    normed_rows = windows(normalized_rows).reshape(-1, chan)
    grad_rows = windows(shifted_grad).reshape(-1, chan)
    qkv = jnp.dot(normed_rows, qkv_weight, preferred_element_type=wide_type) + qkv_bias
    qkv = qkv.reshape(-1, count, 3, heads, head_dim)
    query = (qkv[:, :, 0] * scale).astype(jnp.bfloat16).transpose(0, 2, 1, 3)
    key = qkv[:, :, 1].astype(jnp.bfloat16).transpose(0, 2, 1, 3)
    value = qkv[:, :, 2].astype(jnp.bfloat16).transpose(0, 2, 1, 3)
    onehot = (
        position_index.reshape(-1)[:, None]
        == jnp.arange(bias_table.shape[0], dtype=jnp.int32)[None, :]
    ).astype(wide_type)
    bias = (
        jnp.dot(onehot, bias_table, precision=lax.Precision.HIGHEST)
        .reshape(count, count, heads)
        .transpose(2, 0, 1)
    )
    ids = windows(region_ids[None, :, :, None]).reshape(-1, count)
    ids = jnp.tile(ids, (frames, 1))
    mask = jnp.where(ids[:, :, None] == ids[:, None, :], 0.0, -100.0).astype(wide_type)
    scores = jnp.einsum("whqd,whkd->whqk", query, key, preferred_element_type=wide_type)
    scores = scores + bias[None] + mask[:, None]
    probs = jax.nn.softmax(scores, axis=-1)
    probs_b = probs.astype(jnp.bfloat16)
    attn = jnp.einsum("whqk,whkd->whqd", probs_b, value, preferred_element_type=wide_type).astype(
        jnp.bfloat16
    )
    attn_rows = attn.transpose(0, 2, 1, 3).reshape(-1, chan)
    grad_proj_weight = jnp.einsum(
        "tc,tk->ck", attn_rows, grad_rows, preferred_element_type=wide_type
    )
    grad_proj_bias = jnp.sum(grad_rows.astype(wide_type), 0)
    d_attn = jnp.einsum(
        "tk,ck->tc", grad_rows, proj_weight, preferred_element_type=wide_type
    ).astype(jnp.bfloat16)
    d_attn = d_attn.reshape(-1, count, heads, head_dim).transpose(0, 2, 1, 3)
    d_p = jnp.einsum("whqd,whkd->whqk", d_attn, value, preferred_element_type=wide_type)
    d_v = jnp.einsum("whqk,whqd->whkd", probs_b, d_attn, preferred_element_type=wide_type).astype(
        jnp.bfloat16
    )
    d_s = probs * (d_p - jnp.sum(d_p * probs, -1, keepdims=True))
    d_bias = jnp.sum(d_s, 0).transpose(1, 2, 0).reshape(count * count, heads)
    grad_table = jnp.dot(onehot.T, d_bias, precision=lax.Precision.HIGHEST)
    d_sb = d_s.astype(jnp.bfloat16)
    d_q = (
        jnp.einsum("whqk,whkd->whqd", d_sb, key, preferred_element_type=wide_type) * scale
    ).astype(jnp.bfloat16)
    d_k = jnp.einsum("whqk,whqd->whkd", d_sb, query, preferred_element_type=wide_type).astype(
        jnp.bfloat16
    )
    d_qkv = jnp.stack([d_q, d_k, d_v]).transpose(1, 3, 0, 2, 4).reshape(-1, 3 * chan)
    grad_qkv_weight = jnp.einsum("tc,tk->ck", normed_rows, d_qkv, preferred_element_type=wide_type)
    grad_qkv_bias = jnp.sum(d_qkv.astype(wide_type), 0)
    grad_normalized = jnp.einsum("tk,ck->tc", d_qkv, qkv_weight, preferred_element_type=wide_type)
    grad_normalized = unwindows(grad_normalized.reshape(-1, count, chan), frames, height, width)
    gradient_norm_scale = jnp.sum(grad_normalized * standardized_input, (0, 1, 2))
    grad_norm_bias = jnp.sum(grad_normalized, (0, 1, 2))
    grad_standardized = grad_normalized * layernorm_scale
    grad_displaced = reciprocal_deviation * (
        grad_standardized
        - jnp.mean(grad_standardized, -1, keepdims=True)
        - standardized_input * jnp.mean(grad_standardized * standardized_input, -1, keepdims=True)
    )
    return (
        grad_displaced,
        (
            grad_qkv_weight,
            grad_qkv_bias,
            grad_proj_weight,
            grad_proj_bias,
            gradient_norm_scale,
            grad_norm_bias,
            grad_table,
        ),
    )


def on_device(
    block_input,
    grad_out,
    region_ids,
    layernorm_scale,
    layernorm_bias,
    qkv_weight,
    qkv_bias,
    proj_weight,
    bias_table,
    position_index,
):
    shifted_x = roll_ahead(
        block_input,
        1,
        lambda piece: shifted(piece, "row", -1),
        lambda piece: shifted(piece, "col", -1),
    )
    shifted_grad = roll_ahead(
        grad_out,
        1,
        lambda piece: shifted(piece, "row", -1),
        lambda piece: shifted(piece, "col", -1),
    )
    grad_displaced, grads = local_grads(
        shifted_x,
        shifted_grad,
        region_ids,
        layernorm_scale,
        layernorm_bias,
        qkv_weight,
        qkv_bias,
        proj_weight,
        bias_table,
        position_index,
    )
    back = roll_behind(
        grad_displaced,
        1,
        lambda piece: shifted(piece.astype(jnp.bfloat16), "row", 1).astype(piece.dtype),
        lambda piece: shifted(piece.astype(jnp.bfloat16), "col", 1).astype(piece.dtype),
    )
    grad_x = (grad_out.astype(jnp.float32) + back).astype(jnp.bfloat16)
    totals = lax.psum(
        (grads[0], grads[1], grads[2], grads[3], grads[4], grads[5], grads[6]), ("dp", "row", "col")
    )
    return (grad_x, totals[0], totals[1], totals[2], totals[3], totals[4], totals[5], totals[6])


def solution(mesh):
    return jax.shard_map(
        on_device,
        mesh=mesh,
        in_specs=(
            P("dp", "row", "col", None),
            P("dp", "row", "col", None),
            P("row", "col"),
            P(),
            P(),
            P(),
            P(),
            P(),
            P(),
            P(),
        ),
        out_specs=(P("dp", "row", "col", None), P(), P(), P(), P(), P(), P(), P()),
        check_vma=False,
    )
```

profile of v0, /device:TPU:1, one launch (start us, length us, event | category | flops | bytes accessed | tf_op | source)
XLA Modules:
  0.0 377.0 jit_solution(11532303623661506735)
XLA Ops:
  7.3 0.9 slice.56
  8.2 8.8 %collective-permute-start.2 = (bf16[1,4,32,192]{3,2,1,0:T(8,128)(2,1)S(1)}, bf16[1,4,32,192]{3,2,1,0:T(8,128)(2,1)S(1)}, u32[]{:S(2)}, u32[]{:S(2)}) collective-permute-start(bf16[1,4,32,192]{3,2,1,0:T(8,128)(2,1)S(1)} %slice.56), channel_id=1, source_target_pairs={{8,0},{16,8},{24,16},{32,24},{40,32},{48,40},{56,48},{0,56},{9,1},... | collective-permute-start | bytes 147464 | tf_op jit(solution)/shard_map/ppermute | solution.py:13
  17.0 0.8 slice.50
  17.8 2.0 collective-permute-start
  19.8 0.8 eq.34
  20.6 0.8 reshape_broadcast_in_dim.3
  21.5 0.8 compare_select_fusion
  22.3 3.2 fusion.2
  25.7 0.8 copy.65
  26.6 10.1 %collective-permute-start.1 = (bf16[1,16,4,192]{3,2,1,0:T(4,128)(2,1)S(1)}, bf16[1,16,4,192]{3,2,1,0:T(4,128)(2,1)S(1)}, u32[]{:S(2)}, u32[]{:S(2)}) collective-permute-start(bf16[1,16,4,192]{3,2,1,0:T(4,128)(2,1)S(1)} %pad_maximum_fusion.4), channel_id=1, source_target_pairs={{1,0},{2,1},{3,2},{4,3},{5,4},{6,5},{7,6},{0,7},{9,8},{10,9},{11,1... | collective-permute-start | bytes 73736 | tf_op jit(solution)/shard_map/ppermute | solution.py:13
  36.8 2.5 collective-permute-start.3
  40.4 0.5 copy-done.8
  41.1 1.4 convolution_add_fusion
  42.5 1.6 reshape.297
  44.1 1.5 copy.105
  45.6 1.8 copy.63
  47.5 0.7 copy-done.4
  48.2 0.7 copy-done.7
  49.2 1.0 reshape.300
  50.2 1.6 add_add_fusion
  51.8 2.4 fusion.36
  54.2 2.2 fusion.11
  56.4 2.3 fusion.10
  58.7 1.6 multiply_reduce_fusion
  60.4 1.2 fusion.13
  61.5 1.7 fusion.9
  63.2 1.3 fusion.8
  64.6 0.5 convert_reduce_fusion
  65.0 1.0 copy-done.1
  66.1 1.8 copy.76
  67.8 3.3 copy.72
  71.1 2.0 copy.78
  73.1 1.9 reshape.304
  75.1 1.9 fusion.38
  77.0 1.7 copy.79
  78.7 1.7 reshape.305
  80.4 2.6 reshape.303
  83.1 2.3 fusion.37
  85.4 2.5 reshape.301
  87.9 1.8 multiply_reduce_fusion.1
  90.4 2.2 collective-permute-start.4
  92.6 1.4 fusion.1
  94.4 2.8 collective-permute-start.5
  97.5 103.8 %all-reduce = (f32[576]{0:T(1024)}, f32[192]{0:T(256)}, f32[192]{0:T(256)}, f32[192]{0:T(256)}, f32[225,6]{0,1:T(8,128)}) all-reduce(f32[576]{0:T(1024)S(1)} %reduce_sum.108, f32[192]{0:T(256)S(1)} %convert_reduce_fusion.1, f32[192]{0:T(256)S(1)} %get-tuple-element.8, ...), channel_id=1, replica_groups=mesh['dp'=8,'row'=8,'col'=8] {'dp','row','col'}, use_global_device_ids=true, to_apply=%region_9.10 | all-reduce | flops 2502 | bytes 20016 | tf_op jit(solution)/shard_map/psum | solution.py:191
  201.4 0.8 fusion.17
  202.2 164.5 %all-reduce.4.cloned.1.call-done = (f32[192,576]{1,0:T(8,128)}, f32[192,192]{1,0:T(8,128)}) async-done(((f32[192,576]{1,0:T(8,128)}, f32[192,192]{1,0:T(8,128)}), (f32[192,576]{1,0:T(8,128)}, f32[192,192]{1,0:T(8,128)})) %all-reduce.4.cloned.1.call-update) | async-done | bytes 589840 | tf_op jit(solution)/shard_map/psum | solution.py:191
  366.7 1.8 copy.111
  368.5 1.6 copy.112
  (85 shorter events, 3.2 us)
Async XLA Ops:
  7.2 34.0 %copy-start = (bf16[192,576]{1,0:T(8,128)(2,1)S(1)}, bf16[192,576]{1,0:T(8,128)(2,1)}, u32[]{:S(2)}) copy-start(bf16[192,576]{1,0:T(8,128)(2,1)} %param.15) | copy-start | bytes 663556
  7.2 18.4 %copy-start.9 = (bf16[1,16,32,192]{3,2,1,0:T(8,128)(2,1)S(1)}, bf16[1,16,32,192]{3,2,1,0:T(8,128)(2,1)}, u32[]{:S(2)}) copy-start(bf16[1,16,32,192]{3,2,1,0:T(8,128)(2,1)} %param.11) | copy-start | bytes 589828
  7.2 18.4 %copy-start.14 = (bf16[1,16,32,192]{3,2,1,0:T(8,128)(2,1)S(1)}, bf16[1,16,32,192]{3,2,1,0:T(8,128)(2,1)}, u32[]{:S(2)}) copy-start(bf16[1,16,32,192]{3,2,1,0:T(8,128)(2,1)} %param.10) | copy-start | bytes 589828
  7.2 359.4 %all-reduce.4.cloned.1.call-start = ((), (), s32[]{:S(2)}) async-start(), calls=%async_computation | async-start | bytes 1376256 | tf_op jit(solution)/shard_map/psum | solution.py:191
  8.2 28.5 %collective-permute-start.2 = (bf16[1,4,32,192]{3,2,1,0:T(8,128)(2,1)S(1)}, bf16[1,4,32,192]{3,2,1,0:T(8,128)(2,1)S(1)}, u32[]{:S(2)}, u32[]{:S(2)}) collective-permute-start(bf16[1,4,32,192]{3,2,1,0:T(8,128)(2,1)S(1)} %slice.56), channel_id=1, source_target_pairs={{8,0},{16,8},{24,16},{32,24},{40,32},{48,40},{56,48},{0,56},{9,1},... | collective-permute-start | bytes 147464 | tf_op jit(solution)/shard_map/ppermute | solution.py:13
  17.8 8.7 %collective-permute-start = (bf16[1,4,32,192]{3,2,1,0:T(8,128)(2,1)S(1)}, bf16[1,4,32,192]{3,2,1,0:T(8,128)(2,1)S(1)}, u32[]{:S(2)}, u32[]{:S(2)}) collective-permute-start(bf16[1,4,32,192]{3,2,1,0:T(8,128)(2,1)S(1)} %slice.50), channel_id=1, source_target_pairs={{8,0},{16,8},{24,16},{32,24},{40,32},{48,40},{56,48},{0,56},{9,1},... | collective-permute-start | bytes 147464 | tf_op jit(solution)/shard_map/ppermute | solution.py:13
  20.6 5.0 %copy-start.17 = (s32[4096]{0:T(1024)}, s32[4096]{0:T(1024)S(1)}, u32[]{:S(2)}) copy-start(s32[4096]{0:T(1024)S(1)} %eq.34) | copy-start | bytes 49156
  26.6 13.6 %copy-start.20 = (f32[192]{0:T(256)S(1)}, f32[192]{0:T(256)}, u32[]{:S(2)}) copy-start(f32[192]{0:T(256)} %param.13) | copy-start | bytes 2308
  26.6 13.6 %copy-start.21 = (f32[192]{0:T(256)S(1)}, f32[192]{0:T(256)}, u32[]{:S(2)}) copy-start(f32[192]{0:T(256)} %param.14) | copy-start | bytes 2308
  26.6 12.8 %collective-permute-start.1 = (bf16[1,16,4,192]{3,2,1,0:T(4,128)(2,1)S(1)}, bf16[1,16,4,192]{3,2,1,0:T(4,128)(2,1)S(1)}, u32[]{:S(2)}, u32[]{:S(2)}) collective-permute-start(bf16[1,16,4,192]{3,2,1,0:T(4,128)(2,1)S(1)} %pad_maximum_fusion.4), channel_id=1, source_target_pairs={{1,0},{2,1},{3,2},{4,3},{5,4},{6,5},{7,6},{0,7},{9,8},{10,9},{11,1... | collective-permute-start | bytes 73736 | tf_op jit(solution)/shard_map/ppermute | solution.py:13
  36.8 10.7 %collective-permute-start.3 = (bf16[1,16,4,192]{3,2,1,0:T(4,128)(2,1)S(1)}, bf16[1,16,4,192]{3,2,1,0:T(4,128)(2,1)S(1)}, u32[]{:S(2)}, u32[]{:S(2)}) collective-permute-start(bf16[1,16,4,192]{3,2,1,0:T(4,128)(2,1)S(1)} %pad_maximum_fusion.3), channel_id=1, source_target_pairs={{1,0},{2,1},{3,2},{4,3},{5,4},{6,5},{7,6},{0,7},{9,8},{10,9},{11,1... | collective-permute-start | bytes 73736 | tf_op jit(solution)/shard_map/ppermute | solution.py:13
  39.3 1.1 copy-start.2
  39.3 1.8 copy-start.19
  40.2 0.8 copy-start.8
  40.4 0.7 copy-start.6
  45.6 3.3 copy-start.16
  47.4 2.8 copy-start.11
  47.4 2.8 copy-start.12
  47.5 0.7 copy-start.4
  48.2 0.7 copy-start.7
  61.5 3.0 copy-start.13
  65.0 1.1 copy-start.1
  87.9 2.1 copy-start.3
  89.7 2.9 copy-start.15
  89.7 2.9 copy-start.18
  90.4 6.9 %copy-start.5 = (bf16[1,16,32,192]{3,2,1,0:T(8,128)(2,1)S(1)}, bf16[1,16,32,192]{3,2,1,0:T(8,128)(2,1)}, u32[]{:S(2)}) copy-start(bf16[1,16,32,192]{3,2,1,0:T(8,128)(2,1)} %copy-done.4) | copy-start | bytes 589828
  90.4 4.0 %collective-permute-start.4 = (bf16[1,4,32,192]{3,2,1,0:T(8,128)(2,1)S(1)}, bf16[1,4,32,192]{3,2,1,0:T(8,128)(2,1)S(1)}, u32[]{:S(2)}, u32[]{:S(2)}) collective-permute-start(bf16[1,4,32,192]{3,2,1,0:T(8,128)(2,1)S(1)} %slice.101), channel_id=1, source_target_pairs={{56,0},{0,8},{8,16},{16,24},{24,32},{32,40},{40,48},{48,56},{57,1}... | collective-permute-start | bytes 147464 | tf_op jit(solution)/shard_map/ppermute | solution.py:13
  94.0 107.3 %copy-start.10 = (bf16[1,16,32,192]{3,2,1,0:T(8,128)(2,1)S(1)}, bf16[1,16,32,192]{3,2,1,0:T(8,128)(2,1)}, u32[]{:S(2)}) copy-start(bf16[1,16,32,192]{3,2,1,0:T(8,128)(2,1)} %param.11) | copy-start | bytes 589828
  94.4 106.9 %collective-permute-start.5 = (bf16[1,16,4,192]{3,2,1,0:T(4,128)(2,1)S(1)}, bf16[1,16,4,192]{3,2,1,0:T(4,128)(2,1)S(1)}, u32[]{:S(2)}, u32[]{:S(2)}) collective-permute-start(bf16[1,16,4,192]{3,2,1,0:T(4,128)(2,1)S(1)} %fusion.32), channel_id=1, source_target_pairs={{7,0},{0,1},{1,2},{2,3},{3,4},{4,5},{5,6},{6,7},{15,8},{8,9},{9,10... | collective-permute-start | bytes 73736 | tf_op jit(solution)/shard_map/ppermute | solution.py:13
Sparse Core Ops, SparseCore 0:
  94.2 272.3 all-reduce.3
where the time goes:
time: 378 us; the launch traced here: 377 us
  waiting for transfers between devices  165 us (44%)
  blocking collectives  104 us (28%)
  local copies, waits for them, and re-layouts  35 us (9%)
  starting transfers between devices  28.4 us (8%)
  matrix products  23.2 us (6%)
  between operations  14.6 us (4%)
  other arithmetic  7.18 us (2%)
    psum x1, waiting for transfers between devices, on_device(): lax.psum((grads[0], grads[1], grads[2], grads[3], grads[4], grads[5], gra...  164 us
    psum x1, blocking collectives, on_device(): lax.psum((grads[0], grads[1], grads[2], grads[3], grads[4], grads[5], gra...  104 us
    ppermute x6, starting transfers between devices, shifted(): return lax.ppermute(block, axis, route)  28.4 us
  transfers between devices with their start and end apart: 7, of which 2 were waited for; matrix products, arithmetic and copies ran while one was open for 5% of the time, Pallas kernels for 0%

commit v1 on v0

v1 whole, which is shorter than its diff:
```python
import jax
import jax.numpy as jnp
from jax import lax
from jax.experimental import pallas as pl
from jax.experimental.pallas import tpu as pltpu
from jax.sharding import Mesh, PartitionSpec as P

WIN = 8
SHIFT = 4
TOK = 64
HEADS = 6
CHAN = 192
DIM = 32
ROWS = 16
COLS = 32
TABLE = 225
OFF = 256
CHUNKS = 32
PACK = 40
BF = jnp.bfloat16
F32 = jnp.float32
HIGH = lax.Precision.HIGHEST

FIRST = ("y", "x")
SECOND = ("zl", "c", "zh")
ROW = ("zl", "c")
COL = ("zh", "x")


def nn(a, b, precision=None):
    return lax.dot_general(a, b, (((1,), (0,)), ((), ())), precision=precision, preferred_element_type=F32)


def nt(a, b, precision=None):
    return lax.dot_general(a, b, (((1,), (1,)), ((), ())), precision=precision, preferred_element_type=F32)


def tn(a, b, precision=None):
    return lax.dot_general(a, b, (((0,), (0,)), ((), ())), precision=precision, preferred_element_type=F32)


def iota(shape, dim):
    return lax.broadcasted_iota(jnp.int32, shape, dim)


def spread_reversed():
    a, lane = iota((TOK, 128), 0), iota((TOK, 128), 1)
    return (lane == 127 - (16 * (a // WIN) + a % WIN)).astype(F32)


def squeeze_pair():
    source, lane = iota((256, 128), 0), iota((256, 128), 1)
    head, a = lane // TOK, lane % TOK
    return (source == 128 * head + 16 * (a // WIN) + a % WIN).astype(F32)


def offset_sums(spread):
    wide = jnp.concatenate([spread, jnp.zeros((TOK, 128), F32)], axis=1)
    total = jnp.zeros((WIN, OFF), F32)
    for i in range(WIN):
        total += pltpu.roll(wide[WIN * i : WIN * i + WIN], 16 * i, 1, stride=1, stride_axis=0)
    return jnp.sum(total, 0, keepdims=True)


def prepare_kernel(pos_ref, table_ref, bias_ref, perm_ref, pad_ref):
    pos = pos_ref[...].astype(F32)
    rev = spread_reversed()
    count = offset_sums(nn(jnp.ones((TOK, TOK), F32), rev))
    entry_ahead = offset_sums(nn(pos, rev, HIGH))
    entry_back = offset_sums(nn(pos.T, rev, HIGH))

    def entry(total):
        whole = jnp.floor(total / jnp.maximum(count, 1.0) + 0.5).astype(jnp.int32)
        return jnp.where(count > 0.5, whole, -1)

    t = iota((OFF, OFF), 0)
    perm_ref[...] = (t == entry(entry_back)).astype(F32)
    perm_ahead = (t == entry(entry_ahead)).astype(F32)
    pad_ref[...] = jnp.zeros_like(pad_ref)
    pad_ref[0:TABLE, 0:HEADS] = table_ref[...]
    by_offset = nn(pad_ref[...].T[0:8], perm_ahead, HIGH)
    squeeze = squeeze_pair()
    for pair in range(HEADS // 2):
        halves = []
        for h in (2 * pair, 2 * pair + 1):
            line = jnp.broadcast_to(by_offset[h : h + 1], (WIN, OFF))
            halves.append(
                jnp.concatenate(
                    [
                        pltpu.roll(line, 16 * i + 129, 1, stride=1, stride_axis=0)[:, 0:128]
                        for i in range(WIN)
                    ],
                    axis=0,
                )
            )
        bias_ref[:, 128 * pair : 128 * pair + 128] = nn(
            jnp.concatenate(halves, axis=1), squeeze, HIGH
        )


def main_kernel(
    x_ref,
    g_ref,
    row_ref,
    col_ref,
    corner_ref,
    ids_ref,
    ls_ref,
    lb_ref,
    w_ref,
    qb_ref,
    wp_ref,
    bias_ref,
    perm_ref,
    ds_ref,
    edge_ref,
    pack_ref,
    ext_ref,
    xhat_ref,
    rstd_ref,
    normed_ref,
    grad_ref,
    q_ref,
    k_ref,
    v_ref,
    da_ref,
    attn_ref,
    dq_ref,
    dk_ref,
    dv_ref,
):
    scale = DIM ** (-0.5)

    def windowed(tile_ref, which):
        ext_ref[0:ROWS, 0:COLS, :] = tile_ref[...].astype(F32)
        ext_ref[ROWS : ROWS + SHIFT, 0:COLS, :] = row_ref[which].astype(F32)
        ext_ref[0:ROWS, COLS : COLS + SHIFT, :] = col_ref[which].astype(F32)
        ext_ref[ROWS : ROWS + SHIFT, COLS : COLS + SHIFT, :] = corner_ref[which].astype(F32)
        pieces = []
        for wr in range(ROWS // WIN):
            for wc in range(COLS // WIN):
                r, c = WIN * wr + SHIFT, WIN * wc + SHIFT
                pieces.append(ext_ref[r : r + WIN, c : c + WIN, :].reshape(TOK, CHAN))
        return jnp.concatenate(pieces, axis=0)

    grad = windowed(g_ref, 1)
    grad_ref[...] = grad.astype(BF)
    grad_proj_bias = jnp.sum(grad, 0, keepdims=True)
    x = windowed(x_ref, 0)
    mean = jnp.sum(x, -1, keepdims=True) * (1.0 / CHAN)
    centered = x - mean
    rstd = lax.rsqrt(jnp.sum(centered * centered, -1, keepdims=True) * (1.0 / CHAN) + 1e-05)
    xhat = centered * rstd
    xhat_ref[...] = xhat
    rstd_ref[...] = rstd
    normed = (xhat * ls_ref[...] + lb_ref[...]).astype(BF)
    normed_ref[...] = normed
    w = w_ref[...]
    w_q, w_k, w_v = w[:, 0:CHAN], w[:, CHAN : 2 * CHAN], w[:, 2 * CHAN : 3 * CHAN]
    qb = qb_ref[...]
    q_ref[...] = ((nn(normed, w_q) + qb[:, 0:CHAN]) * scale).astype(BF)
    k_ref[...] = (nn(normed, w_k) + qb[:, CHAN : 2 * CHAN]).astype(BF)
    v_ref[...] = (nn(normed, w_v) + qb[:, 2 * CHAN : 3 * CHAN]).astype(BF)
    da_ref[...] = nt(grad_ref[...], wp_ref[...]).astype(BF)

    token, tile_row = iota((8 * TOK, ROWS), 0), iota((8 * TOK, ROWS), 1)
    window, inside = token // TOK, token % TOK
    pick_row = (tile_row == WIN * (window // 4) + inside // WIN).astype(BF)
    spread_ids = nn(pick_row, ids_ref[...].astype(F32).astype(BF))
    token, tile_col = iota((8 * TOK, COLS), 0), iota((8 * TOK, COLS), 1)
    window, inside = token // TOK, token % TOK
    pick_col = tile_col == WIN * (window % 4) + inside % WIN
    ids = jnp.sum(jnp.where(pick_col, spread_ids, 0.0), -1, keepdims=True)
    region = (ids == iota((8 * TOK, 16), 1).astype(F32)).astype(BF)

    head_of = iota((TOK, CHAN), 1) // DIM

    def by_head(a):
        zero = jnp.zeros_like(a)
        return jnp.concatenate([jnp.where(head_of == h, a, zero) for h in range(HEADS)], axis=0)

    def own_head(a):
        total = jnp.where(head_of == 0, a[0:TOK], 0.0)
        for h in range(1, HEADS):
            total = jnp.where(head_of == h, a[TOK * h : TOK * h + TOK], total)
        return total

    d_sum = jnp.zeros((TOK, HEADS * TOK), F32)
    for win in range(8):
        s = slice(TOK * win, TOK * win + TOK)
        q_heads = by_head(q_ref[s])
        key = k_ref[s]
        value = v_ref[s]
        same = nt(region[s], jnp.concatenate([region[s]] * HEADS, axis=0))
        scores = nt(key, q_heads) + bias_ref[...] + (same - 1.0) * 100.0
        top = jnp.max(scores, 0, keepdims=True)
        e = jnp.exp(scores - top)
        p = e * (1.0 / jnp.sum(e, 0, keepdims=True))
        pb = p.astype(BF)
        attn_ref[s] = own_head(tn(pb, value)).astype(BF)
        da_heads = by_head(da_ref[s])
        d_p = nt(value, da_heads)
        dv_ref[s] = nn(pb, da_heads).astype(BF)
        d_s = p * (d_p - jnp.sum(d_p * p, 0, keepdims=True))
        d_sum += d_s
        d_sb = d_s.astype(BF)
        dq_ref[s] = (own_head(tn(d_sb, key)) * scale).astype(BF)
        dk_ref[s] = nn(d_sb, q_heads).astype(BF)

    rev = spread_reversed()
    lines = [
        offset_sums(nn(d_sum[:, TOK * h : TOK * h + TOK], rev, HIGH)) for h in range(HEADS)
    ]
    lines += [jnp.zeros((1, OFF), F32)] * 2
    by_entry = nt(jnp.concatenate(lines, axis=0), perm_ref[...], HIGH)

    dq, dk, dv = dq_ref[...], dk_ref[...], dv_ref[...]
    d_normed = nt(dq, w_q) + nt(dk, w_k) + nt(dv, w_v)
    xhat = xhat_ref[...]
    norm_scale = jnp.sum(d_normed * xhat, 0, keepdims=True)
    norm_bias = jnp.sum(d_normed, 0, keepdims=True)
    d_hat = d_normed * ls_ref[...]
    mean_hat = jnp.sum(d_hat, -1, keepdims=True) * (1.0 / CHAN)
    mean_mix = jnp.sum(d_hat * xhat, -1, keepdims=True) * (1.0 / CHAN)
    d_shifted = rstd_ref[...] * (d_hat - mean_hat - xhat * mean_mix)
    for win in range(8):
        wr, wc = win // 4, win % 4
        block = d_shifted[TOK * win : TOK * win + TOK].reshape(WIN, WIN, CHAN)
        ds_ref[WIN * wr : WIN * wr + WIN, WIN * wc : WIN * wc + WIN, :] = block
    edge_ref[...] = ds_ref[ROWS - SHIFT : ROWS].astype(BF)

    normed = normed_ref[...]
    weights = jnp.concatenate(
        [tn(normed, dq), tn(normed, dk), tn(normed, dv), tn(attn_ref[...], grad_ref[...])], axis=1
    )
    sums = [jnp.sum(a.astype(F32), 0, keepdims=True) for a in (dq, dk, dv)] + [grad_proj_bias]
    small = jnp.concatenate(
        [
            jnp.concatenate(sums, axis=1),
            jnp.concatenate([norm_scale, norm_bias, jnp.zeros((1, 2 * CHAN), F32)], axis=1),
            jnp.concatenate([by_entry[0:1], by_entry[1:2], by_entry[2:3]], axis=1),
            jnp.concatenate([by_entry[3:4], by_entry[4:5], by_entry[5:6]], axis=1),
        ],
        axis=0,
    )
    high = small.astype(BF).astype(F32)
    small = jnp.concatenate([high, small - high], axis=0)
    packed = jnp.concatenate([weights, small], axis=0)
    for chunk in range(CHUNKS):
        tiles = []
        for tile in range(5 * chunk, 5 * chunk + 5):
            r, c = tile // 6, tile % 6
            if r < 25:
                tiles.append(packed[8 * r : 8 * r + 8, 128 * c : 128 * c + 128])
            else:
                tiles.append(jnp.zeros((8, 128), F32))
        pack_ref[chunk] = jnp.concatenate(tiles, axis=0).astype(BF)


def add_up(ref, count):
    total = ref[0].astype(F32)
    for i in range(1, count):
        total += ref[i].astype(F32)
    return total


def sum_kernel(got_ref, out_ref):
    total = add_up(got_ref, got_ref.shape[0]).astype(BF)
    for i in range(out_ref.shape[0]):
        out_ref[i] = total


def unpack_kernel(got_ref, w_ref, wb_ref, p_ref, pb_ref, ns_ref, nb_ref, table_ref, all_ref):
    for tile in range(150):
        r, c = tile // 6, tile % 6
        if tile % 5 == 0:
            chunk = got_ref[tile // 5].astype(F32)
        part = 8 * (tile % 5)
        all_ref[8 * r : 8 * r + 8, 128 * c : 128 * c + 128] = chunk[part : part + 8]
    w_ref[...] = all_ref[0:CHAN, 0 : 3 * CHAN]
    p_ref[...] = all_ref[0:CHAN, 3 * CHAN : 4 * CHAN]
    small = all_ref[CHAN : CHAN + 4, :] + all_ref[CHAN + 4 : CHAN + 8, :]
    wb_ref[...] = small[0:1, 0 : 3 * CHAN]
    pb_ref[...] = small[0:1, 3 * CHAN : 4 * CHAN]
    ns_ref[...] = small[1:2, 0:CHAN]
    nb_ref[...] = small[1:2, CHAN : 2 * CHAN]
    lines = [small[2 + h // 3 : 3 + h // 3, OFF * (h % 3) : OFF * (h % 3) + OFF] for h in range(HEADS)]
    lines += [jnp.zeros((1, OFF), F32)] * 2
    table = jnp.concatenate(lines, axis=0).T
    table_ref[...] = table[0:TABLE, 0:HEADS]


def kernel_call(kernel, out_shape, scratch=(), flops=10**7):
    return pl.pallas_call(
        kernel,
        out_shape=out_shape,
        scratch_shapes=scratch,
        cost_estimate=pl.CostEstimate(flops=flops, bytes_accessed=10**6, transcendentals=0),
        compiler_params=pltpu.CompilerParams(vmem_limit_bytes=40 * 2**20),
    )


def shape(dims, kind=F32):
    return jax.ShapeDtypeStruct(dims, kind)


def moved(block, axes, distance):
    sizes = [lax.axis_size(a) for a in axes]
    count = sizes[0] * sizes[1]
    return lax.ppermute(block, axes, [((i - distance) % count, i) for i in range(count)])


def moved_corner(block):
    pairs = [
        (8 * ((r + 1) % 8) + (c + 1) % 8, 8 * r + c) for r in range(8) for c in range(8)
    ]
    return lax.ppermute(block, ROW + COL, pairs)


def prepare(position_index, bias_table):
    return kernel_call(
        prepare_kernel,
        (shape((TOK, HEADS * TOK)), shape((OFF, OFF))),
        [pltpu.VMEM((OFF, 128), F32)],
    )(position_index, bias_table)


def main(*args):
    tokens = 8 * TOK
    return kernel_call(
        main_kernel,
        (
            shape((ROWS, COLS, CHAN)),
            shape((SHIFT, COLS, CHAN), BF),
            shape((CHUNKS, PACK, 128), BF),
        ),
        [
            pltpu.VMEM((ROWS + 8, COLS + 8, CHAN), F32),
            pltpu.VMEM((tokens, CHAN), F32),
            pltpu.VMEM((tokens, 1), F32),
        ]
        + [pltpu.VMEM((tokens, CHAN), BF)] * 10,
        flops=10**9,
    )(*args)


def unpack(gathered):
    return kernel_call(
        unpack_kernel,
        (
            shape((CHAN, 3 * CHAN)),
            shape((1, 3 * CHAN)),
            shape((CHAN, CHAN)),
            shape((1, CHAN)),
            shape((1, CHAN)),
            shape((1, CHAN)),
            shape((TABLE, HEADS)),
        ),
        [pltpu.VMEM((CHAN + 8, 4 * CHAN), F32)],
    )(gathered)


def on_device(
    block_input,
    grad_out,
    region_ids,
    layernorm_scale,
    layernorm_bias,
    qkv_weight,
    qkv_bias,
    proj_weight,
    bias_table,
    position_index,
):
    x, g = block_input[0], grad_out[0]
    row = moved(jnp.stack([x[:SHIFT], g[:SHIFT]]), ROW, -1)
    col = moved(jnp.stack([x[:, :SHIFT], g[:, :SHIFT]]), COL, -1)
    corner = moved_corner(jnp.stack([x[:SHIFT, :SHIFT], g[:SHIFT, :SHIFT]]))
    bias, perm = prepare(position_index, bias_table)
    d_shifted, edge, packed = main(
        x,
        g,
        row,
        col,
        corner,
        region_ids,
        layernorm_scale[None],
        layernorm_bias[None],
        qkv_weight,
        qkv_bias[None],
        proj_weight,
        bias,
        perm,
    )
    above = moved(edge, ROW, 1)
    got = lax.all_to_all(packed, FIRST, 0, 0, tiled=True)
    part = kernel_call(sum_kernel, shape((16, PACK, 128), BF))(got)
    back = jnp.concatenate([above.astype(F32), d_shifted[: ROWS - SHIFT]], axis=0)
    left = moved(back[:, COLS - SHIFT :].astype(BF), COL, 1)
    got = lax.all_to_all(part, SECOND, 0, 0, tiled=True)
    whole = kernel_call(sum_kernel, shape((CHUNKS, PACK, 128), BF))(got)
    back = jnp.concatenate([left.astype(F32), back[:, : COLS - SHIFT]], axis=1)
    grad_x = (g.astype(F32) + back).astype(BF)[None]
    gathered = lax.all_to_all(whole, FIRST, 0, 0, tiled=True)
    w, wb, p, pb, ns, nb, table = unpack(gathered)
    return (grad_x, w, wb[0], p, pb[0], ns[0], nb[0], table)


def solution(mesh):
    fine = Mesh(mesh.devices.reshape(8, 4, 2, 2, 4), ("y", "zl", "c", "zh", "x"))
    tiles = P("y", ROW, COL, None)
    return jax.shard_map(
        on_device,
        mesh=fine,
        in_specs=(tiles, tiles, P(ROW, COL), P(), P(), P(), P(), P(), P(), P()),
        out_specs=(tiles, P(), P(), P(), P(), P(), P(), P()),
        check_vma=False,
    )
```

time: 378 us -> 94 us (0.25)
  waiting for transfers between devices: 165 us -> 14.2 us
  blocking collectives: 104 us -> 20.2 us
  local copies, waits for them, and re-layouts: 35 us -> 3.93 us
  matrix products: 23.2 us -> 0 us
  between operations: 14.6 us -> 0.91 us
  starting transfers between devices: 28.4 us -> 41.1 us
  Pallas kernels: 0 us -> 10.4 us
  other arithmetic: 7.18 us -> 1.61 us
    psum x1 -> x0, waiting for transfers between devices: 164 us -> none  [on_device(): lax.psum((grads[0], grads[1], grads[2], grads[3], grads[4], grads[5], gra...]
    psum x1 -> x0, blocking collectives: 104 us -> none  [on_device(): lax.psum((grads[0], grads[1], grads[2], grads[3], grads[4], grads[5], gra...]
    dot_general x13 -> x0, matrix products: 23.2 us -> none  [the longest x1 3.25 us: local_grads(): jnp.dot(onehot, bias_table, precision=lax.Precision.HIGHEST)]
    all_to_all x0 -> x1, blocking collectives: none -> 20.2 us  [on_device(): got = lax.all_to_all(packed, FIRST, 0, 0, tiled=True)]
    reshape x10 -> x0, local copies, waits for them, and re-layouts: 13.1 us -> none  [the longest x3 4.91 us: local_grads(): qkv = qkv.reshape(-1, count, 3, heads, head_dim)]
    all_to_all x0 -> x2, starting transfers between devices: none -> 12.9 us  [the longest x1 8.48 us: on_device(): got = lax.all_to_all(part, SECOND, 0, 0, tiled=True)]
    pallas_call x0 -> x5, Pallas kernels: none -> 10.4 us  [the longest x1 6.79 us: main(): kernel_call(main_kernel, (shape((ROWS, COLS, CHAN)), shape((SHIFT, COLS,...]
    ppermute x6 -> x5, waiting for transfers between devices: 0.28 us -> 9.95 us  [the longest x4 9.95 us: moved(): lax.ppermute(block, axes, [((i - distance) % count, i) for i in range(cou...]
  transfers between devices with their start and end apart: 7 -> 7, of which waited for: 2 -> 4; matrix products, arithmetic and copies ran while one was open for 5% -> 2% of each run, Pallas kernels for 0% -> 1%
where the time goes in v1:
time: 94 us; the launch traced here: 92.4 us
  starting transfers between devices  41.1 us (44%)
  blocking collectives  20.2 us (21%)
  waiting for transfers between devices  14.2 us (15%)
  Pallas kernels  10.4 us (11%)
  local copies, waits for them, and re-layouts  3.93 us (4%)
  other arithmetic  1.61 us (2%)
    ppermute x4, starting transfers between devices, moved(): lax.ppermute(block, axes, [((i - distance) % count, i) for i in range(cou...  23.5 us
    all_to_all x1, blocking collectives, on_device(): got = lax.all_to_all(packed, FIRST, 0, 0, tiled=True)  20.2 us
    ppermute x4, waiting for transfers between devices, moved(): lax.ppermute(block, axes, [((i - distance) % count, i) for i in range(cou...  9.95 us
    all_to_all x1, starting transfers between devices, on_device(): got = lax.all_to_all(part, SECOND, 0, 0, tiled=True)  8.48 us
    pallas_call x1, Pallas kernels, main(): kernel_call(main_kernel, (shape((ROWS, COLS, CHAN)), shape((SHIFT, COLS,...  6.79 us
    ppermute x1, starting transfers between devices, moved_corner(): return lax.ppermute(block, ROW + COL, pairs)  4.79 us
    all_to_all x1, starting transfers between devices, on_device(): gathered = lax.all_to_all(whole, FIRST, 0, 0, tiled=True)  4.39 us
    all_to_all x1, waiting for transfers between devices, on_device(): got = lax.all_to_all(part, SECOND, 0, 0, tiled=True)  4.19 us
  transfers between devices with their start and end apart: 7, of which 4 were waited for; matrix products, arithmetic and copies ran while one was open for 2% of the time, Pallas kernels for 1%

profile of v1, /device:TPU:1, one launch (start us, length us, event | category | flops | bytes accessed | tf_op | source)
XLA Modules:
  0.0 92.4 jit_solution(3737782247962470460)
XLA Ops:
  0.6 0.0 copy-start
  0.6 0.9 %slice_bitcast_fusion = (bf16[1,16,4,192]{3,2,1,0:T(4,128)(2,1)S(1)}, bf16[1,16,4,192]{3,2,1,0:T(4,128)(2,1)S(1)}) fusion(bf16[16,32,192]{2,1,0:T(8,128)(2,1)} %bitcast.20, bf16[16,32,192]{2,1,0:T(8,128)(2,1)} %bitcast.23), kind=kLoop, calls=%fused_computation.10 | loop fusion | bytes 98304 | tf_op jit(solution)/shard_map/stack | solution.py:377
  1.6 0.1 pad_maximum_fusion.2
  1.6 0.0 copy-start.1
  1.7 13.8 %collective-permute-start.1 = (bf16[2,16,4,192]{3,2,1,0:T(4,128)(2,1)S(1)}, bf16[2,16,4,192]{3,2,1,0:T(4,128)(2,1)S(1)}, u32[]{:S(2)}, u32[]{:S(2)}) collective-permute-start(bf16[2,16,4,192]{3,2,1,0:T(4,128)(2,1)S(1)} %pad_maximum_fusion.2), channel_id=1, source_target_pairs={{1,0},{2,1},{3,2},{4,3},{5,4},{6,5},{7,6},{0,7},{9,8},{10,9},{11,1... | collective-permute-start | bytes 147464 | tf_op jit(solution)/shard_map/ppermute | solution.py:310
  15.5 0.8 slice.30
  16.3 0.0 copy-done
  16.3 0.0 copy-start.3
  16.4 3.0 %collective-permute-start = (bf16[2,4,32,192]{3,2,1,0:T(8,128)(2,1)S(1)}, bf16[2,4,32,192]{3,2,1,0:T(8,128)(2,1)S(1)}, u32[]{:S(2)}, u32[]{:S(2)}) collective-permute-start(bf16[2,4,32,192]{3,2,1,0:T(8,128)(2,1)S(1)} %pad_maximum_fusion.1), channel_id=1, source_target_pairs={{8,0},{16,8},{24,16},{32,24},{40,32},{48,40},{56,48},{0,56},{9,1},... | collective-permute-start | bytes 294920 | tf_op jit(solution)/shard_map/ppermute | solution.py:310
  19.4 0.0 copy-done.1
  19.4 0.0 copy-start.9
  19.4 0.0 copy-start.8
  19.4 4.8 %collective-permute-start.2 = (bf16[2,4,4,192]{3,2,1,0:T(4,128)(2,1)S(1)}, bf16[2,4,4,192]{3,2,1,0:T(4,128)(2,1)S(1)}, u32[]{:S(2)}, u32[]{:S(2)}) collective-permute-start(bf16[2,4,4,192]{3,2,1,0:T(4,128)(2,1)S(1)} %pad_maximum_fusion.3), channel_id=1, source_target_pairs={{9,0},{10,1},{11,2},{12,3},{13,4},{14,5},{15,6},{8,7},{17,8},{18,9... | collective-permute-start | bytes 36872 | tf_op jit(solution)/shard_map/ppermute | solution.py:317
  24.2 0.0 copy-done.9
  24.3 0.0 copy-done.8
  24.3 0.0 copy-start.2
  24.3 0.1 copy.18.table_ref
  24.4 0.6 copy-done.2
  25.0 0.0 copy-start.4
  25.0 0.0 copy-start.5
  25.0 0.0 copy-start.7
  25.0 1.1 %shard_map.161 = (f32[64,384]{1,0:T(8,128)S(1)}, f32[256,256]{1,0:T(8,128)S(1)}) custom-call(s32[64,64]{1,0:T(8,128)S(1)} %copy-done.2, f32[225,6]{1,0:T(8,128)S(1)} %copy.18.table_ref), custom_call_target="tpu_custom_call" | custom-call | flops 10000000 | bytes 1000000 | tf_op jit(solution)/shard_map/pallas_call | solution.py:321
  26.2 0.0 collective-permute-done.2.corner_ref
  26.2 0.0 collective-permute-done.1.col_ref
  26.2 0.0 collective-permute-done.row_ref
  26.2 0.0 copy-start.6
  26.2 0.0 copy-done.3
  26.2 0.0 copy-done.4
  26.2 0.0 copy-done.5
  26.2 0.0 copy-done.7
  26.2 0.6 copy-done.6
  26.9 6.8 %shard_map.162 = (f32[16,32,192]{2,1,0:T(8,128)S(1)}, bf16[4,32,192]{2,1,0:T(8,128)(2,1)S(1)}, bf16[32,40,128]{2,1,0:T(8,128)(2,1)S(1)}) custom-call(bf16[16,32,192]{2,1,0:T(8,128)(2,1)S(1)} %bitcast.25, bf16[16,32,192]{2,1,0:T(8,128)(2,1)S(1)} %bitcast.22, bf16[2,4,32,192]{3,2,1,0:T(8,128)(2,1)S(1)} %collective-permute-done.row_ref, ...), custom_call_target="tpu_custom_call" | custom-call | flops 1000000000 | bytes 1000000 | tf_op jit(solution)/shard_map/pallas_call | solution.py:330
  33.7 20.2 %all_to_all.15.got_ref = bf16[32,40,128]{2,1,0:T(8,128)(2,1)S(1)} all-to-all(bf16[32,40,128]{2,1,0:T(8,128)(2,1)S(1)} %get-tuple-element.24), channel_id=1, replica_groups=mesh['y'=8,'zl'=4,'c'=2,'zh'=2,'x'=4] {'y','x'}, dimensions={0} | all-to-all | bytes 655360 | tf_op jit(solution)/shard_map/all_to_all | solution.py:396
  53.9 0.7 shard_map.163
  54.6 8.5 %all-to-all-start.1 = ((bf16[16,40,128]{2,1,0:T(8,128)(2,1)}), bf16[16,40,128]{2,1,0:T(8,128)(2,1)S(1)}, u32[]{:S(2)}, u32[]{:S(2)}) async-start(bf16[16,40,128]{2,1,0:T(8,128)(2,1)} %shard_map.163), calls=%async_computation.1 | async-start | bytes 327680 | tf_op jit(solution)/shard_map/all_to_all | solution.py:400
  63.1 3.5 %collective-permute-start.3 = (bf16[4,32,192]{2,1,0:T(8,128)(2,1)S(1)}, bf16[4,32,192]{2,1,0:T(8,128)(2,1)S(1)}, u32[]{:S(2)}, u32[]{:S(2)}) collective-permute-start(bf16[4,32,192]{2,1,0:T(8,128)(2,1)S(1)} %get-tuple-element.22), channel_id=1, source_target_pairs={{56,0},{0,8},{8,16},{16,24},{24,32},{32,40},{40,48},{48,56},{57,1}... | collective-permute-start | bytes 147464 | tf_op jit(solution)/shard_map/ppermute | solution.py:310
  66.7 2.0 %collective-permute-done.3 = bf16[4,32,192]{2,1,0:T(8,128)(2,1)S(1)} collective-permute-done((bf16[4,32,192]{2,1,0:T(8,128)(2,1)S(1)}, bf16[4,32,192]{2,1,0:T(8,128)(2,1)S(1)}, u32[]{:S(2)}, u32[]{:S(2)}) %collective-permute-start.3) | collective-permute-done | bytes 49184 | tf_op jit(solution)/shard_map/ppermute | solution.py:310
  68.7 4.2 %all-to-all-done.1.got_ref = bf16[16,40,128]{2,1,0:T(8,128)(2,1)S(1)} async-done(((bf16[16,40,128]{2,1,0:T(8,128)(2,1)}), bf16[16,40,128]{2,1,0:T(8,128)(2,1)S(1)}, u32[]{:S(2)}, u32[]{:S(2)}) %all-to-all-start.1) | async-done | bytes 163872 | tf_op jit(solution)/shard_map/all_to_all | solution.py:400
  72.9 0.8 shard_map.164
  73.7 4.4 %all-to-all-start.2 = ((bf16[32,40,128]{2,1,0:T(8,128)(2,1)}), bf16[32,40,128]{2,1,0:T(8,128)(2,1)S(1)}, u32[]{:S(2)}, u32[]{:S(2)}) async-start(bf16[32,40,128]{2,1,0:T(8,128)(2,1)} %shard_map.164), calls=%async_computation.2 | async-start | bytes 655360 | tf_op jit(solution)/shard_map/all_to_all | solution.py:404
  78.1 3.1 %collective-permute-start.4 = (bf16[16,4,192]{2,1,0:T(4,128)(2,1)S(1)}, bf16[16,4,192]{2,1,0:T(4,128)(2,1)S(1)}, u32[]{:S(2)}, u32[]{:S(2)}) collective-permute-start(bf16[16,4,192]{2,1,0:T(4,128)(2,1)S(1)} %fusion.3), channel_id=1, source_target_pairs={{7,0},{0,1},{1,2},{2,3},{3,4},{4,5},{5,6},{6,7},{15,8},{8,9},{9,10... | collective-permute-start | bytes 73736 | tf_op jit(solution)/shard_map/ppermute | solution.py:310
  81.3 7.9 %collective-permute-done.4 = bf16[16,4,192]{2,1,0:T(4,128)(2,1)S(1)} collective-permute-done((bf16[16,4,192]{2,1,0:T(4,128)(2,1)S(1)}, bf16[16,4,192]{2,1,0:T(4,128)(2,1)S(1)}, u32[]{:S(2)}, u32[]{:S(2)}) %collective-permute-start.4) | collective-permute-done | bytes 24608 | tf_op jit(solution)/shard_map/ppermute | solution.py:310
  89.2 0.8 fusion.1
  90.1 0.1 all-to-all-done.2.got_ref
  90.1 0.9 %shard_map.165 = (f32[192,576]{1,0:T(8,128)}, f32[1,576]{1,0:T(1,128)S(1)}, f32[192,192]{1,0:T(8,128)}, f32[1,192]{1,0:T(1,128)}, f32[1,192]{1,0:T(1,128)}, /*index=5*/f32[1,192]{1,0:T(1,128)}, f32[225,6]{1,0:T(8,128)S(1)}) custom-call(bf16[32,40,128]{2,1,0:T(8,128)(2,1)S(1)} %all-to-all-done.2.got_ref), custom_call_target="tpu_custom_call" | custom-call | flops 10000000 | bytes 1000000 | tf_op jit(solution)/shard_map/pallas_call | solution.py:348
  91.1 0.7 copy.19
  91.8 0.6 reduce
  (10 shorter events, 0.2 us)
Async XLA Ops:
  0.6 15.7 %copy-start = (bf16[1,16,32,192]{3,2,1,0:T(8,128)(2,1)S(1)}, bf16[1,16,32,192]{3,2,1,0:T(8,128)(2,1)}, u32[]{:S(2)}) copy-start(bf16[1,16,32,192]{3,2,1,0:T(8,128)(2,1)} %param.11) | copy-start | bytes 589828
  1.6 17.7 %copy-start.1 = (bf16[1,16,32,192]{3,2,1,0:T(8,128)(2,1)S(1)}, bf16[1,16,32,192]{3,2,1,0:T(8,128)(2,1)}, u32[]{:S(2)}) copy-start(bf16[1,16,32,192]{3,2,1,0:T(8,128)(2,1)} %param.10) | copy-start | bytes 589828
  1.7 24.5 %collective-permute-start.1 = (bf16[2,16,4,192]{3,2,1,0:T(4,128)(2,1)S(1)}, bf16[2,16,4,192]{3,2,1,0:T(4,128)(2,1)S(1)}, u32[]{:S(2)}, u32[]{:S(2)}) collective-permute-start(bf16[2,16,4,192]{3,2,1,0:T(4,128)(2,1)S(1)} %pad_maximum_fusion.2), channel_id=1, source_target_pairs={{1,0},{2,1},{3,2},{4,3},{5,4},{6,5},{7,6},{0,7},{9,8},{10,9},{11,1... | collective-permute-start | bytes 147464 | tf_op jit(solution)/shard_map/ppermute | solution.py:310
  16.3 9.9 %copy-start.3 = (bf16[192,576]{1,0:T(8,128)(2,1)S(1)}, bf16[192,576]{1,0:T(8,128)(2,1)}, u32[]{:S(2)}) copy-start(bf16[192,576]{1,0:T(8,128)(2,1)} %w_ref.1) | copy-start | bytes 663556
  16.4 9.8 %collective-permute-start = (bf16[2,4,32,192]{3,2,1,0:T(8,128)(2,1)S(1)}, bf16[2,4,32,192]{3,2,1,0:T(8,128)(2,1)S(1)}, u32[]{:S(2)}, u32[]{:S(2)}) collective-permute-start(bf16[2,4,32,192]{3,2,1,0:T(8,128)(2,1)S(1)} %pad_maximum_fusion.1), channel_id=1, source_target_pairs={{8,0},{16,8},{24,16},{32,24},{40,32},{48,40},{56,48},{0,56},{9,1},... | collective-permute-start | bytes 294920 | tf_op jit(solution)/shard_map/ppermute | solution.py:310
  19.4 4.9 %copy-start.9 = (f32[576]{0:T(1024)S(1)}, f32[576]{0:T(1024)}, u32[]{:S(2)}) copy-start(f32[576]{0:T(1024)} %param.16) | copy-start | bytes 6916
  19.4 4.9 %copy-start.8 = (f32[225,6]{0,1:T(8,128)S(1)}, f32[225,6]{0,1:T(8,128)}, u32[]{:S(2)}) copy-start(f32[225,6]{0,1:T(8,128)} %param.18) | copy-start | bytes 16204
  19.4 6.7 %collective-permute-start.2 = (bf16[2,4,4,192]{3,2,1,0:T(4,128)(2,1)S(1)}, bf16[2,4,4,192]{3,2,1,0:T(4,128)(2,1)S(1)}, u32[]{:S(2)}, u32[]{:S(2)}) collective-permute-start(bf16[2,4,4,192]{3,2,1,0:T(4,128)(2,1)S(1)} %pad_maximum_fusion.3), channel_id=1, source_target_pairs={{9,0},{10,1},{11,2},{12,3},{13,4},{14,5},{15,6},{8,7},{17,8},{18,9... | collective-permute-start | bytes 36872 | tf_op jit(solution)/shard_map/ppermute | solution.py:317
  24.3 0.8 copy-start.2
  25.0 1.2 %copy-start.4 = (bf16[192,192]{1,0:T(8,128)(2,1)S(1)}, bf16[192,192]{1,0:T(8,128)(2,1)}, u32[]{:S(2)}) copy-start(bf16[192,192]{1,0:T(8,128)(2,1)} %wp_ref.1) | copy-start | bytes 221188
  25.0 1.2 %copy-start.5 = (s32[16,32]{1,0:T(8,128)S(1)}, s32[16,32]{1,0:T(8,128)}, u32[]{:S(2)}) copy-start(s32[16,32]{1,0:T(8,128)} %ids_ref.1) | copy-start | bytes 6148
  25.0 1.2 %copy-start.7 = (f32[192]{0:T(256)S(1)}, f32[192]{0:T(256)}, u32[]{:S(2)}) copy-start(f32[192]{0:T(256)} %param.14) | copy-start | bytes 2308
  26.2 0.7 copy-start.6
  54.6 18.3 %all-to-all-start.1 = ((bf16[16,40,128]{2,1,0:T(8,128)(2,1)}), bf16[16,40,128]{2,1,0:T(8,128)(2,1)S(1)}, u32[]{:S(2)}, u32[]{:S(2)}) async-start(bf16[16,40,128]{2,1,0:T(8,128)(2,1)} %shard_map.163), calls=%async_computation.1 | async-start | bytes 327680 | tf_op jit(solution)/shard_map/all_to_all | solution.py:400
  63.1 5.6 %collective-permute-start.3 = (bf16[4,32,192]{2,1,0:T(8,128)(2,1)S(1)}, bf16[4,32,192]{2,1,0:T(8,128)(2,1)S(1)}, u32[]{:S(2)}, u32[]{:S(2)}) collective-permute-start(bf16[4,32,192]{2,1,0:T(8,128)(2,1)S(1)} %get-tuple-element.22), channel_id=1, source_target_pairs={{56,0},{0,8},{8,16},{16,24},{24,32},{32,40},{40,48},{48,56},{57,1}... | collective-permute-start | bytes 147464 | tf_op jit(solution)/shard_map/ppermute | solution.py:310
  73.7 16.5 %all-to-all-start.2 = ((bf16[32,40,128]{2,1,0:T(8,128)(2,1)}), bf16[32,40,128]{2,1,0:T(8,128)(2,1)S(1)}, u32[]{:S(2)}, u32[]{:S(2)}) async-start(bf16[32,40,128]{2,1,0:T(8,128)(2,1)} %shard_map.164), calls=%async_computation.2 | async-start | bytes 655360 | tf_op jit(solution)/shard_map/all_to_all | solution.py:404
  78.1 11.1 %collective-permute-start.4 = (bf16[16,4,192]{2,1,0:T(4,128)(2,1)S(1)}, bf16[16,4,192]{2,1,0:T(4,128)(2,1)S(1)}, u32[]{:S(2)}, u32[]{:S(2)}) collective-permute-start(bf16[16,4,192]{2,1,0:T(4,128)(2,1)S(1)} %fusion.3), channel_id=1, source_target_pairs={{7,0},{0,1},{1,2},{2,3},{3,4},{4,5},{5,6},{6,7},{15,8},{8,9},{9,10... | collective-permute-start | bytes 73736 | tf_op jit(solution)/shard_map/ppermute | solution.py:310

commit v2 on v1

--- a/solution.py
+++ b/solution.py
@@ -16,13 +16,13 @@
 TABLE = 225
 OFF = 256
 CHUNKS = 32
-PACK = 40
+PACK = 24
 BF = jnp.bfloat16
 F32 = jnp.float32
 HIGH = lax.Precision.HIGHEST
 
 FIRST = ("y", "x")
-SECOND = ("zl", "c", "zh")
+SECOND = ("zl", "zh")
 ROW = ("zl", "c")
 COL = ("zh", "x")
 
@@ -43,9 +43,15 @@
     return lax.broadcasted_iota(jnp.int32, shape, dim)
 
 
-def spread_reversed():
-    a, lane = iota((TOK, 128), 0), iota((TOK, 128), 1)
-    return (lane == 127 - (16 * (a // WIN) + a % WIN)).astype(F32)
+def split(a):
+    high = a.astype(BF)
+    return high, (a - high.astype(F32)).astype(BF)
+
+
+def spread_pair():
+    source, lane = iota((128, 256), 0), iota((128, 256), 1)
+    head, a = source // TOK, source % TOK
+    return (lane == 128 * head + 127 - (16 * (a // WIN) + a % WIN)).astype(BF)
 
 
 def squeeze_pair():
@@ -55,47 +61,53 @@
 
 
 def offset_sums(spread):
-    wide = jnp.concatenate([spread, jnp.zeros((TOK, 128), F32)], axis=1)
+    blank = jnp.zeros((WIN, 128), F32)
     total = jnp.zeros((WIN, OFF), F32)
     for i in range(WIN):
-        total += pltpu.roll(wide[WIN * i : WIN * i + WIN], 16 * i, 1, stride=1, stride_axis=0)
-    return jnp.sum(total, 0, keepdims=True)
-
-
-def prepare_kernel(pos_ref, table_ref, bias_ref, perm_ref, pad_ref):
-    pos = pos_ref[...].astype(F32)
-    rev = spread_reversed()
-    count = offset_sums(nn(jnp.ones((TOK, TOK), F32), rev))
-    entry_ahead = offset_sums(nn(pos, rev, HIGH))
-    entry_back = offset_sums(nn(pos.T, rev, HIGH))
+        wide = jnp.concatenate([spread[WIN * i : WIN * i + WIN], blank], axis=1)
+        total += pltpu.roll(wide, 16 * i, 1) if i else wide
+    return jnp.sum(pltpu.roll(total, 0, 1, stride=1, stride_axis=0), 0, keepdims=True)
+
+
+def prepare_kernel(pos_ref, table_ref, ls_ref, lb_ref, qb_ref, bias_ref, perm_ref, rows_ref):
+    rows_ref[0, 0:CHAN] = ls_ref[...]
+    rows_ref[1, 0:CHAN] = lb_ref[...]
+    rows_ref[2, :] = qb_ref[...]
+    pos = pos_ref[...]
+    both = jnp.concatenate([pos, jnp.ones_like(pos)], axis=1).astype(F32).astype(BF)
+    spread = nn(both, spread_pair())
+    count = offset_sums(spread[:, 128:256])
+    entry_ahead = offset_sums(spread[:, 0:128])
+    back = pos.astype(F32).T
+    back = jnp.concatenate([back, back], axis=1).astype(BF)
+    entry_back = offset_sums(nn(back, spread_pair())[:, 0:128])
 
     def entry(total):
         whole = jnp.floor(total / jnp.maximum(count, 1.0) + 0.5).astype(jnp.int32)
         return jnp.where(count > 0.5, whole, -1)
 
     t = iota((OFF, OFF), 0)
-    perm_ref[...] = (t == entry(entry_back)).astype(F32)
-    perm_ahead = (t == entry(entry_ahead)).astype(F32)
-    pad_ref[...] = jnp.zeros_like(pad_ref)
-    pad_ref[0:TABLE, 0:HEADS] = table_ref[...]
-    by_offset = nn(pad_ref[...].T[0:8], perm_ahead, HIGH)
+    perm_ref[...] = (t == entry(entry_back)).astype(BF)
+    perm_ahead = (iota((TABLE, OFF), 0) == entry(entry_ahead)).astype(F32)
+    by_offset = nn(table_ref[...], perm_ahead, HIGH)
     squeeze = squeeze_pair()
     for pair in range(HEADS // 2):
         halves = []
         for h in (2 * pair, 2 * pair + 1):
             line = jnp.broadcast_to(by_offset[h : h + 1], (WIN, OFF))
-            halves.append(
-                jnp.concatenate(
-                    [
-                        pltpu.roll(line, 16 * i + 129, 1, stride=1, stride_axis=0)[:, 0:128]
-                        for i in range(WIN)
-                    ],
-                    axis=0,
-                )
-            )
+            line = pltpu.roll(line, 129, 1, stride=1, stride_axis=0)
+            shifts = [line] + [pltpu.roll(line, 16 * i, 1) for i in range(1, WIN)]
+            halves.append(jnp.concatenate([a[:, 0:128] for a in shifts], axis=0))
         bias_ref[:, 128 * pair : 128 * pair + 128] = nn(
             jnp.concatenate(halves, axis=1), squeeze, HIGH
         )
+
+
+def halo_kernel(x_ref, g_ref, row_ref, corner_ref):
+    for i, ref in enumerate((x_ref, g_ref)):
+        tile = ref[0:SHIFT]
+        row_ref[i] = tile
+        corner_ref[i] = tile[:, 0:SHIFT]
 
 
 def main_kernel(
@@ -105,15 +117,16 @@
     col_ref,
     corner_ref,
     ids_ref,
-    ls_ref,
-    lb_ref,
     w_ref,
-    qb_ref,
     wp_ref,
     bias_ref,
     perm_ref,
+    rows_ref,
+    core_ref,
     ds_ref,
     edge_ref,
+    mine_ref,
+    other_ref,
     pack_ref,
     ext_ref,
     xhat_ref,
@@ -153,11 +166,11 @@
     xhat = centered * rstd
     xhat_ref[...] = xhat
     rstd_ref[...] = rstd
-    normed = (xhat * ls_ref[...] + lb_ref[...]).astype(BF)
+    ls, lb, qb = rows_ref[0:1, 0:CHAN], rows_ref[1:2, 0:CHAN], rows_ref[2:3, :]
+    normed = (xhat * ls + lb).astype(BF)
     normed_ref[...] = normed
     w = w_ref[...]
     w_q, w_k, w_v = w[:, 0:CHAN], w[:, CHAN : 2 * CHAN], w[:, 2 * CHAN : 3 * CHAN]
-    qb = qb_ref[...]
     q_ref[...] = ((nn(normed, w_q) + qb[:, 0:CHAN]) * scale).astype(BF)
     k_ref[...] = (nn(normed, w_k) + qb[:, CHAN : 2 * CHAN]).astype(BF)
     v_ref[...] = (nn(normed, w_v) + qb[:, 2 * CHAN : 3 * CHAN]).astype(BF)
@@ -191,8 +204,8 @@
         q_heads = by_head(q_ref[s])
         key = k_ref[s]
         value = v_ref[s]
-        same = nt(region[s], jnp.concatenate([region[s]] * HEADS, axis=0))
-        scores = nt(key, q_heads) + bias_ref[...] + (same - 1.0) * 100.0
+        apart = nt(region[s], jnp.concatenate([region[s]] * 2, axis=0)) * 100.0 - 100.0
+        scores = nt(key, q_heads) + bias_ref[...] + jnp.concatenate([apart] * 3, axis=1)
         top = jnp.max(scores, 0, keepdims=True)
         e = jnp.exp(scores - top)
         p = e * (1.0 / jnp.sum(e, 0, keepdims=True))
@@ -207,19 +220,23 @@
         dq_ref[s] = (own_head(tn(d_sb, key)) * scale).astype(BF)
         dk_ref[s] = nn(d_sb, q_heads).astype(BF)
 
-    rev = spread_reversed()
-    lines = [
-        offset_sums(nn(d_sum[:, TOK * h : TOK * h + TOK], rev, HIGH)) for h in range(HEADS)
-    ]
-    lines += [jnp.zeros((1, OFF), F32)] * 2
-    by_entry = nt(jnp.concatenate(lines, axis=0), perm_ref[...], HIGH)
+    parts = [a for pair in range(3) for a in split(d_sum[:, 128 * pair : 128 * pair + 128])]
+    spread = nn(jnp.concatenate(parts, axis=0), spread_pair())
+    lines = []
+    for pair in range(3):
+        both = spread[128 * pair : 128 * pair + TOK] + spread[128 * pair + TOK : 128 * pair + 128]
+        lines += [offset_sums(both[:, 0:128]), offset_sums(both[:, 128:256])]
+    lines = jnp.concatenate(lines + [jnp.zeros((2, OFF), F32)], axis=0)
+    high, low = split(lines)
+    by_entry = nt(jnp.concatenate([high, low], axis=0), perm_ref[...])
+    by_entry = by_entry[0:8] + by_entry[8:16]
 
     dq, dk, dv = dq_ref[...], dk_ref[...], dv_ref[...]
     d_normed = nt(dq, w_q) + nt(dk, w_k) + nt(dv, w_v)
     xhat = xhat_ref[...]
     norm_scale = jnp.sum(d_normed * xhat, 0, keepdims=True)
     norm_bias = jnp.sum(d_normed, 0, keepdims=True)
-    d_hat = d_normed * ls_ref[...]
+    d_hat = d_normed * ls
     mean_hat = jnp.sum(d_hat, -1, keepdims=True) * (1.0 / CHAN)
     mean_mix = jnp.sum(d_hat * xhat, -1, keepdims=True) * (1.0 / CHAN)
     d_shifted = rstd_ref[...] * (d_hat - mean_hat - xhat * mean_mix)
@@ -229,9 +246,9 @@
         ds_ref[WIN * wr : WIN * wr + WIN, WIN * wc : WIN * wc + WIN, :] = block
     edge_ref[...] = ds_ref[ROWS - SHIFT : ROWS].astype(BF)
 
-    normed = normed_ref[...]
+    normed = normed_ref[...].T
     weights = jnp.concatenate(
-        [tn(normed, dq), tn(normed, dk), tn(normed, dv), tn(attn_ref[...], grad_ref[...])], axis=1
+        [nn(normed, dq), nn(normed, dk), nn(normed, dv), tn(attn_ref[...], grad_ref[...])], axis=1
     )
     sums = [jnp.sum(a.astype(F32), 0, keepdims=True) for a in (dq, dk, dv)] + [grad_proj_bias]
     small = jnp.concatenate(
@@ -246,15 +263,16 @@
     high = small.astype(BF).astype(F32)
     small = jnp.concatenate([high, small - high], axis=0)
     packed = jnp.concatenate([weights, small], axis=0)
-    for chunk in range(CHUNKS):
+    for chunk in range(50):
         tiles = []
-        for tile in range(5 * chunk, 5 * chunk + 5):
+        for tile in range(3 * chunk, 3 * chunk + 3):
             r, c = tile // 6, tile % 6
-            if r < 25:
-                tiles.append(packed[8 * r : 8 * r + 8, 128 * c : 128 * c + 128])
-            else:
-                tiles.append(jnp.zeros((8, 128), F32))
-        pack_ref[chunk] = jnp.concatenate(tiles, axis=0).astype(BF)
+            tiles.append(packed[8 * r : 8 * r + 8, 128 * c : 128 * c + 128])
+        pack_ref[chunk // 25, chunk % 25] = jnp.concatenate(tiles, axis=0).astype(BF)
+    pack_ref[:, 25:CHUNKS] = jnp.zeros((2, CHUNKS - 25, PACK, 128), BF)
+    core = core_ref[0]
+    mine_ref[...] = pack_ref[core]
+    other_ref[...] = pack_ref[1 - core]
 
 
 def add_up(ref, count):
@@ -270,31 +288,39 @@
         out_ref[i] = total
 
 
-def unpack_kernel(got_ref, w_ref, wb_ref, p_ref, pb_ref, ns_ref, nb_ref, table_ref, all_ref):
-    for tile in range(150):
-        r, c = tile // 6, tile % 6
-        if tile % 5 == 0:
-            chunk = got_ref[tile // 5].astype(F32)
-        part = 8 * (tile % 5)
-        all_ref[8 * r : 8 * r + 8, 128 * c : 128 * c + 128] = chunk[part : part + 8]
+def pair_kernel(mine_ref, got_ref, out_ref):
+    out_ref[...] = (mine_ref[...].astype(F32) + got_ref[...].astype(F32)).astype(BF)
+
+
+def unpack_kernel(
+    mine_ref, got_ref, core_ref, w_ref, wb_ref, p_ref, pb_ref, ns_ref, nb_ref, table_ref, half_ref, all_ref
+):
+    core = core_ref[0]
+    half_ref[core] = mine_ref[...]
+    half_ref[1 - core] = got_ref[...]
+    for chunk in range(50):
+        tiles = half_ref[chunk // 25, chunk % 25].astype(F32)
+        for tile in range(3 * chunk, 3 * chunk + 3):
+            r, c, part = tile // 6, tile % 6, 8 * (tile % 3)
+            all_ref[8 * r : 8 * r + 8, 128 * c : 128 * c + 128] = tiles[part : part + 8]
     w_ref[...] = all_ref[0:CHAN, 0 : 3 * CHAN]
     p_ref[...] = all_ref[0:CHAN, 3 * CHAN : 4 * CHAN]
     small = all_ref[CHAN : CHAN + 4, :] + all_ref[CHAN + 4 : CHAN + 8, :]
-    wb_ref[...] = small[0:1, 0 : 3 * CHAN]
-    pb_ref[...] = small[0:1, 3 * CHAN : 4 * CHAN]
-    ns_ref[...] = small[1:2, 0:CHAN]
-    nb_ref[...] = small[1:2, CHAN : 2 * CHAN]
-    lines = [small[2 + h // 3 : 3 + h // 3, OFF * (h % 3) : OFF * (h % 3) + OFF] for h in range(HEADS)]
-    lines += [jnp.zeros((1, OFF), F32)] * 2
-    table = jnp.concatenate(lines, axis=0).T
-    table_ref[...] = table[0:TABLE, 0:HEADS]
-
-
-def kernel_call(kernel, out_shape, scratch=(), flops=10**7):
+    wb_ref[...] = small[0, 0 : 3 * CHAN]
+    pb_ref[...] = small[0, 3 * CHAN : 4 * CHAN]
+    ns_ref[...] = small[1, 0:CHAN]
+    nb_ref[...] = small[1, CHAN : 2 * CHAN]
+    for h in range(HEADS):
+        place = OFF * (h % 3)
+        table_ref[h : h + 1, :] = small[2 + h // 3 : 3 + h // 3, place : place + TABLE]
+
+
+def kernel_call(kernel, out_shape, scratch=(), flops=10**7, **specs):
     return pl.pallas_call(
         kernel,
         out_shape=out_shape,
         scratch_shapes=scratch,
+        **specs,
         cost_estimate=pl.CostEstimate(flops=flops, bytes_accessed=10**6, transcendentals=0),
         compiler_params=pltpu.CompilerParams(vmem_limit_bytes=40 * 2**20),
     )
@@ -317,12 +343,25 @@
     return lax.ppermute(block, ROW + COL, pairs)
 
 
-def prepare(position_index, bias_table):
+SMALL = pl.BlockSpec(memory_space=pltpu.SMEM)
+WHOLE = pl.BlockSpec(memory_space=pltpu.VMEM)
+
+
+def prepare(position_index, bias_table, ls, lb, qb):
     return kernel_call(
         prepare_kernel,
-        (shape((TOK, HEADS * TOK)), shape((OFF, OFF))),
-        [pltpu.VMEM((OFF, 128), F32)],
-    )(position_index, bias_table)
+        (shape((TOK, HEADS * TOK)), shape((OFF, OFF), BF), shape((8, 3 * CHAN))),
+    )(position_index, bias_table.T, ls, lb, qb)
+
+
+def halos(x, g):
+    return kernel_call(
+        halo_kernel,
+        (
+            shape((2, SHIFT, COLS, CHAN), BF),
+            shape((2, SHIFT, SHIFT, CHAN), BF),
+        ),
+    )(x, g)
 
 
 def main(*args):
@@ -333,31 +372,43 @@
             shape((ROWS, COLS, CHAN)),
             shape((SHIFT, COLS, CHAN), BF),
             shape((CHUNKS, PACK, 128), BF),
+            shape((CHUNKS, PACK, 128), BF),
         ),
         [
+            pltpu.VMEM((2, CHUNKS, PACK, 128), BF),
             pltpu.VMEM((ROWS + 8, COLS + 8, CHAN), F32),
             pltpu.VMEM((tokens, CHAN), F32),
             pltpu.VMEM((tokens, 1), F32),
         ]
         + [pltpu.VMEM((tokens, CHAN), BF)] * 10,
         flops=10**9,
+        in_specs=[WHOLE] * (len(args) - 1) + [SMALL],
     )(*args)
 
 
-def unpack(gathered):
+def pair_sum(mine, got):
+    return kernel_call(pair_kernel, shape(mine.shape, BF))(mine, got)
+
+
+def chunk_sum(got, copies):
+    return kernel_call(sum_kernel, shape((copies,) + got.shape[1:], BF))(got)
+
+
+def unpack(mine, got, core):
     return kernel_call(
         unpack_kernel,
         (
             shape((CHAN, 3 * CHAN)),
-            shape((1, 3 * CHAN)),
+            shape((3 * CHAN,)),
             shape((CHAN, CHAN)),
-            shape((1, CHAN)),
-            shape((1, CHAN)),
-            shape((1, CHAN)),
-            shape((TABLE, HEADS)),
+            shape((CHAN,)),
+            shape((CHAN,)),
+            shape((CHAN,)),
+            shape((HEADS, TABLE)),
         ),
-        [pltpu.VMEM((CHAN + 8, 4 * CHAN), F32)],
-    )(gathered)
+        [pltpu.VMEM((2, CHUNKS, PACK, 128), BF), pltpu.VMEM((CHAN + 8, 4 * CHAN), F32)],
+        in_specs=[WHOLE, WHOLE, SMALL],
+    )(mine, got, core)
 
 
 def on_device(
@@ -373,37 +424,30 @@
     position_index,
 ):
     x, g = block_input[0], grad_out[0]
-    row = moved(jnp.stack([x[:SHIFT], g[:SHIFT]]), ROW, -1)
+    core = lax.axis_index("c").astype(jnp.int32)[None]
     col = moved(jnp.stack([x[:, :SHIFT], g[:, :SHIFT]]), COL, -1)
-    corner = moved_corner(jnp.stack([x[:SHIFT, :SHIFT], g[:SHIFT, :SHIFT]]))
-    bias, perm = prepare(position_index, bias_table)
-    d_shifted, edge, packed = main(
-        x,
-        g,
-        row,
-        col,
-        corner,
-        region_ids,
-        layernorm_scale[None],
-        layernorm_bias[None],
-        qkv_weight,
-        qkv_bias[None],
-        proj_weight,
-        bias,
-        perm,
-    )
+    row, corner = halos(x, g)
+    row, corner = moved(row, ROW, -1), moved_corner(corner)
+    bias, perm, rows = prepare(
+        position_index, bias_table, layernorm_scale, layernorm_bias, qkv_bias
+    )
+    d_shifted, edge, mine, other = main(
+        x, g, row, col, corner, region_ids, qkv_weight, proj_weight, bias, perm, rows, core
+    )
+    half = pair_sum(mine, lax.ppermute(other, "c", [(0, 1), (1, 0)]))
     above = moved(edge, ROW, 1)
-    got = lax.all_to_all(packed, FIRST, 0, 0, tiled=True)
-    part = kernel_call(sum_kernel, shape((16, PACK, 128), BF))(got)
+    got = lax.all_to_all(half, FIRST, 0, 0, tiled=True)
+    part = chunk_sum(got, 8)
+    got = lax.all_to_all(part, SECOND, 0, 0, tiled=True)
+    whole = chunk_sum(got, CHUNKS)
     back = jnp.concatenate([above.astype(F32), d_shifted[: ROWS - SHIFT]], axis=0)
     left = moved(back[:, COLS - SHIFT :].astype(BF), COL, 1)
-    got = lax.all_to_all(part, SECOND, 0, 0, tiled=True)
-    whole = kernel_call(sum_kernel, shape((CHUNKS, PACK, 128), BF))(got)
     back = jnp.concatenate([left.astype(F32), back[:, : COLS - SHIFT]], axis=1)
     grad_x = (g.astype(F32) + back).astype(BF)[None]
     gathered = lax.all_to_all(whole, FIRST, 0, 0, tiled=True)
-    w, wb, p, pb, ns, nb, table = unpack(gathered)
-    return (grad_x, w, wb[0], p, pb[0], ns[0], nb[0], table)
+    other = lax.ppermute(gathered, "c", [(0, 1), (1, 0)])
+    w, wb, p, pb, ns, nb, table = unpack(gathered, other, core)
+    return (grad_x, w, wb, p, pb, ns, nb, table.T)
 
 
 def solution(mesh):

time: 94 us -> 95 us (1.011); the launches traced: 92.4 us -> 94.4 us
  starting transfers between devices: 41.1 us -> 50.3 us
  waiting for transfers between devices: 14.2 us -> 10.2 us
  blocking collectives: 20.2 us -> 18.1 us
    ppermute x0 -> x2, starting transfers between devices: none -> 8.58 us  [the longest x1 5.97 us: on_device(): other = lax.ppermute(gathered, 'c', [(0, 1), (1, 0)])]
    all_to_all x1, waiting for transfers between devices: 4.19 us -> 0.01 us  [on_device(): got = lax.all_to_all(part, SECOND, 0, 0, tiled=True)]
    all_to_all x1, blocking collectives: 20.2 us -> 18.1 us  [on_device(): got = lax.all_to_all(half, FIRST, 0, 0, tiled=True)]
    ppermute x4, starting transfers between devices: 23.5 us -> 25.2 us  [moved(): lax.ppermute(block, axes, [((i - distance) % count, i) for i in range(cou...]
    unnamed x22 -> x24, local copies, waits for them, and re-layouts: 2.1 us -> 3.51 us
    ppermute x0 -> x2, waiting for transfers between devices: none -> 1.28 us  [the longest x1 1.05 us: on_device(): half = pair_sum(mine, lax.ppermute(other, 'c', [(0, 1), (1, 0)]))]
    all_to_all x1, starting transfers between devices: 8.48 us -> 7.3 us  [on_device(): got = lax.all_to_all(part, SECOND, 0, 0, tiled=True)]
    ppermute x4, waiting for transfers between devices: 9.95 us -> 8.93 us  [moved(): lax.ppermute(block, axes, [((i - distance) % count, i) for i in range(cou...]
  transfers between devices with their start and end apart: 7 -> 9, of which waited for: 4 -> 4; matrix products, arithmetic and copies ran while one was open for 2% -> 1% of each run, Pallas kernels for 1% -> 1%
where the time goes in v2:
time: 95 us; the launch traced here: 94.4 us
  starting transfers between devices  50.3 us (53%)
  blocking collectives  18.1 us (19%)
  Pallas kernels  10.4 us (11%)
  waiting for transfers between devices  10.2 us (11%)
  local copies, waits for them, and re-layouts  3.56 us (4%)
  other arithmetic  0.96 us (1%)
    ppermute x4, starting transfers between devices, moved(): lax.ppermute(block, axes, [((i - distance) % count, i) for i in range(cou...  25.2 us
    all_to_all x1, blocking collectives, on_device(): got = lax.all_to_all(half, FIRST, 0, 0, tiled=True)  18.1 us
    ppermute x4, waiting for transfers between devices, moved(): lax.ppermute(block, axes, [((i - distance) % count, i) for i in range(cou...  8.93 us
    all_to_all x1, starting transfers between devices, on_device(): got = lax.all_to_all(part, SECOND, 0, 0, tiled=True)  7.3 us
    pallas_call x1, Pallas kernels, main(): kernel_call(main_kernel, (shape((ROWS, COLS, CHAN)), shape((SHIFT, COLS,...  6.72 us
    ppermute x1, starting transfers between devices, on_device(): other = lax.ppermute(gathered, 'c', [(0, 1), (1, 0)])  5.97 us
    ppermute x1, starting transfers between devices, moved_corner(): return lax.ppermute(block, ROW + COL, pairs)  5.35 us
    all_to_all x1, starting transfers between devices, on_device(): gathered = lax.all_to_all(whole, FIRST, 0, 0, tiled=True)  3.87 us
  transfers between devices with their start and end apart: 9, of which 4 were waited for; matrix products, arithmetic and copies ran while one was open for 1% of the time, Pallas kernels for 1%

profile of v2, /device:TPU:1, one launch (start us, length us, event | category | flops | bytes accessed | tf_op | source)
XLA Modules:
  0.0 94.4 jit_solution(14359838522056031243)
XLA Ops:
  0.6 0.0 copy-start
  0.6 0.9 copy-done
  1.6 0.0 copy-start.2
  1.6 0.9 %copy-done.2 = bf16[1,16,32,192]{3,2,1,0:T(8,128)(2,1)S(1)} copy-done((bf16[1,16,32,192]{3,2,1,0:T(8,128)(2,1)S(1)}, bf16[1,16,32,192]{3,2,1,0:T(8,128)(2,1)}, u32[]{:S(2)}) %copy-start.2) | copy-done | bytes 196632
  2.5 0.0 copy-start.4
  2.5 0.0 copy-start.10
  2.6 0.0 copy-start.1
  2.6 8.9 %collective-permute-start = (bf16[2,4,32,192]{3,2,1,0:T(8,128)(2,1)S(1)}, bf16[2,4,32,192]{3,2,1,0:T(8,128)(2,1)S(1)}, u32[]{:S(2)}, u32[]{:S(2)}) collective-permute-start(bf16[2,4,32,192]{3,2,1,0:T(8,128)(2,1)S(1)} %get-tuple-element.24), channel_id=1, source_target_pairs={{8,0},{16,8},{24,16},{32,24},{40,32},{48,40},{56,48},{0,56},{9,1},... | collective-permute-start | bytes 294920 | tf_op jit(solution)/shard_map/ppermute | solution.py:336
  11.5 0.0 copy-start.6
  11.5 0.1 pad_maximum_fusion.1
  11.6 0.0 copy-start.5
  11.6 7.5 %collective-permute-start.1 = (bf16[2,16,4,192]{3,2,1,0:T(4,128)(2,1)S(1)}, bf16[2,16,4,192]{3,2,1,0:T(4,128)(2,1)S(1)}, u32[]{:S(2)}, u32[]{:S(2)}) collective-permute-start(bf16[2,16,4,192]{3,2,1,0:T(4,128)(2,1)S(1)} %pad_maximum_fusion.1), channel_id=1, source_target_pairs={{1,0},{2,1},{3,2},{4,3},{5,4},{6,5},{7,6},{0,7},{9,8},{10,9},{11,1... | collective-permute-start | bytes 147464 | tf_op jit(solution)/shard_map/ppermute | solution.py:336
  19.1 0.0 copy-start.8
  19.1 5.4 %collective-permute-start.2 = (bf16[2,4,4,192]{3,2,1,0:T(4,128)(2,1)S(1)}, bf16[2,4,4,192]{3,2,1,0:T(4,128)(2,1)S(1)}, u32[]{:S(2)}, u32[]{:S(2)}) collective-permute-start(bf16[2,4,4,192]{3,2,1,0:T(4,128)(2,1)S(1)} %get-tuple-element.25), channel_id=1, source_target_pairs={{9,0},{10,1},{11,2},{12,3},{13,4},{14,5},{15,6},{8,7},{17,8},{18,9... | collective-permute-start | bytes 36872 | tf_op jit(solution)/shard_map/ppermute | solution.py:343
  24.5 0.0 copy-start.7
  24.5 0.0 copy-done.4
  24.5 0.0 copy-done.6
  24.5 0.0 copy-done.5
  24.5 0.0 copy-done.8
  24.5 0.6 copy-done.7
  25.1 1.3 %shard_map.162 = (f32[64,384]{1,0:T(8,128)S(1)}, bf16[256,256]{1,0:T(8,128)(2,1)S(1)}, f32[8,576]{1,0:T(8,128)S(1)}) custom-call(s32[64,64]{1,0:T(8,128)S(1)} %copy-done.4, f32[6,225]{1,0:T(8,128)S(1)} %bitcast.20, f32[192]{0:T(256)S(1)} %copy-done.7, f32[192]{0:T(256)S(1)} %copy-done.8, f32[576]{0:T(1024)S(1)} %copy-done.6), custom_call_target="tpu_custom_call" | custom-call | flops 10000000 | bytes 1000000 | tf_op jit(solution)/shard_map/pallas_call | solution.py:351
  26.4 0.0 collective-permute-done.2.corner_ref
  26.5 0.0 collective-permute-done.1.col_ref
  26.5 0.0 collective-permute-done.row_ref
  26.5 0.0 copy-done.3
  26.5 0.0 copy-done.10
  26.5 0.0 copy-done.1
  26.5 0.0 copy-done.11
  26.5 0.0 copy-start.9
  26.5 0.9 copy-done.9
  27.5 6.7 %shard_map.163 = (f32[16,32,192]{2,1,0:T(8,128)S(1)}, bf16[4,32,192]{2,1,0:T(8,128)(2,1)S(1)}, bf16[32,24,128]{2,1,0:T(8,128)(2,1)S(1)}, bf16[32,24,128]{2,1,0:T(8,128)(2,1)S(1)}) custom-call(bf16[16,32,192]{2,1,0:T(8,128)(2,1)S(1)} %bitcast.19, bf16[16,32,192]{2,1,0:T(8,128)(2,1)S(1)} %bitcast.16, bf16[2,4,32,192]{3,2,1,0:T(8,128)(2,1)S(1)} %collective-permute-done.row_ref, ...), custom_call_target="tpu_custom_call" | custom-call | flops 1000000000 | bytes 1000000 | tf_op jit(solution)/shard_map/pallas_call | solution.py:369
  34.2 2.6 %collective-permute-start.5 = (bf16[32,24,128]{2,1,0:T(8,128)(2,1)S(1)}, bf16[32,24,128]{2,1,0:T(8,128)(2,1)S(1)}, u32[]{:S(2)}, u32[]{:S(2)}) collective-permute-start(bf16[32,24,128]{2,1,0:T(8,128)(2,1)S(1)} %get-tuple-element.32), channel_id=1, source_target_pairs={{0,8},{8,0},{1,9},{9,1},{2,10},{10,2},{3,11},{11,3},{4,12},{12,4},... | collective-permute-start | bytes 589832 | tf_op jit(solution)/shard_map/ppermute | solution.py:437
  36.8 1.0 %collective-permute-done.5.got_ref = bf16[32,24,128]{2,1,0:T(8,128)(2,1)S(1)} collective-permute-done((bf16[32,24,128]{2,1,0:T(8,128)(2,1)S(1)}, bf16[32,24,128]{2,1,0:T(8,128)(2,1)S(1)}, u32[]{:S(2)}, u32[]{:S(2)}) %collective-permute-start.5) | collective-permute-done | bytes 196640 | tf_op jit(solution)/shard_map/ppermute | solution.py:437
  37.9 18.1 %all_to_all.15.got_ref = bf16[32,24,128]{2,1,0:T(8,128)(2,1)S(1)} all-to-all(bf16[32,24,128]{2,1,0:T(8,128)(2,1)S(1)} %shard_map.164), channel_id=1, replica_groups=mesh['y'=8,'zl'=4,'c'=2,'zh'=2,'x'=4] {'y','x'}, dimensions={0} | all-to-all | bytes 393216 | tf_op jit(solution)/shard_map/all_to_all | solution.py:439
  56.0 0.7 shard_map.165
  56.7 7.3 %all-to-all-start.1 = ((bf16[8,24,128]{2,1,0:T(8,128)(2,1)}), bf16[8,24,128]{2,1,0:T(8,128)(2,1)S(1)}, u32[]{:S(2)}, u32[]{:S(2)}) async-start(bf16[8,24,128]{2,1,0:T(8,128)(2,1)} %shard_map.165), calls=%async_computation.1 | async-start | bytes 98304 | tf_op jit(solution)/shard_map/all_to_all | solution.py:441
  64.0 5.8 %collective-permute-start.3 = (bf16[4,32,192]{2,1,0:T(8,128)(2,1)S(1)}, bf16[4,32,192]{2,1,0:T(8,128)(2,1)S(1)}, u32[]{:S(2)}, u32[]{:S(2)}) collective-permute-start(bf16[4,32,192]{2,1,0:T(8,128)(2,1)S(1)} %get-tuple-element.29), channel_id=1, source_target_pairs={{56,0},{0,8},{8,16},{16,24},{24,32},{32,40},{40,48},{48,56},{57,1}... | collective-permute-start | bytes 147464 | tf_op jit(solution)/shard_map/ppermute | solution.py:336
  69.8 1.3 %collective-permute-done.3 = bf16[4,32,192]{2,1,0:T(8,128)(2,1)S(1)} collective-permute-done((bf16[4,32,192]{2,1,0:T(8,128)(2,1)S(1)}, bf16[4,32,192]{2,1,0:T(8,128)(2,1)S(1)}, u32[]{:S(2)}, u32[]{:S(2)}) %collective-permute-start.3) | collective-permute-done | bytes 49184 | tf_op jit(solution)/shard_map/ppermute | solution.py:336
  71.1 0.0 all-to-all-done.1.got_ref
  71.1 0.7 shard_map.166
  71.8 3.9 %all-to-all-start.2 = ((bf16[32,24,128]{2,1,0:T(8,128)(2,1)}), bf16[32,24,128]{2,1,0:T(8,128)(2,1)S(1)}, u32[]{:S(2)}, u32[]{:S(2)}) async-start(bf16[32,24,128]{2,1,0:T(8,128)(2,1)} %shard_map.166), calls=%async_computation.2 | async-start | bytes 393216 | tf_op jit(solution)/shard_map/all_to_all | solution.py:447
  75.7 3.0 %collective-permute-start.4 = (bf16[16,4,192]{2,1,0:T(4,128)(2,1)S(1)}, bf16[16,4,192]{2,1,0:T(4,128)(2,1)S(1)}, u32[]{:S(2)}, u32[]{:S(2)}) collective-permute-start(bf16[16,4,192]{2,1,0:T(4,128)(2,1)S(1)} %fusion.3), channel_id=1, source_target_pairs={{7,0},{0,1},{1,2},{2,3},{3,4},{4,5},{5,6},{6,7},{15,8},{8,9},{9,10... | collective-permute-start | bytes 73736 | tf_op jit(solution)/shard_map/ppermute | solution.py:336
  78.8 7.7 %collective-permute-done.4 = bf16[16,4,192]{2,1,0:T(4,128)(2,1)S(1)} collective-permute-done((bf16[16,4,192]{2,1,0:T(4,128)(2,1)S(1)}, bf16[16,4,192]{2,1,0:T(4,128)(2,1)S(1)}, u32[]{:S(2)}, u32[]{:S(2)}) %collective-permute-start.4) | collective-permute-done | bytes 24608 | tf_op jit(solution)/shard_map/ppermute | solution.py:336
  86.5 0.0 all-to-all-done.2.mine_ref
  86.5 6.0 %collective-permute-start.6 = (bf16[32,24,128]{2,1,0:T(8,128)(2,1)S(1)}, bf16[32,24,128]{2,1,0:T(8,128)(2,1)S(1)}, u32[]{:S(2)}, u32[]{:S(2)}) collective-permute-start(bf16[32,24,128]{2,1,0:T(8,128)(2,1)S(1)} %all-to-all-done.2.mine_ref), channel_id=1, source_target_pairs={{0,8},{8,0},{1,9},{9,1},{2,10},{10,2},{3,11},{11,3},{4,12},{12,4},... | collective-permute-start | bytes 589832 | tf_op jit(solution)/shard_map/ppermute | solution.py:448
  92.4 0.8 fusion.1
  93.3 0.2 collective-permute-done.6.got_ref
  93.5 0.9 shard_map.167
  (10 shorter events, 0.2 us)
Async XLA Ops:
  0.6 1.0 %copy-start = (bf16[1,16,32,192]{3,2,1,0:T(8,128)(2,1)S(1)}, bf16[1,16,32,192]{3,2,1,0:T(8,128)(2,1)}, u32[]{:S(2)}) copy-start(bf16[1,16,32,192]{3,2,1,0:T(8,128)(2,1)} %param.11) | copy-start | bytes 589828
  1.6 0.9 %copy-start.2 = (bf16[1,16,32,192]{3,2,1,0:T(8,128)(2,1)S(1)}, bf16[1,16,32,192]{3,2,1,0:T(8,128)(2,1)}, u32[]{:S(2)}) copy-start(bf16[1,16,32,192]{3,2,1,0:T(8,128)(2,1)} %param.10) | copy-start | bytes 589828
  2.5 21.9 %copy-start.4 = (s32[64,64]{1,0:T(8,128)S(1)}, s32[64,64]{1,0:T(8,128)}, u32[]{:S(2)}) copy-start(s32[64,64]{1,0:T(8,128)} %pos_ref.1) | copy-start | bytes 49156
  2.5 23.9 %copy-start.3 = (bf16[1,16,32,192]{3,2,1,0:T(8,128)(2,1)S(1)}, bf16[1,16,32,192]{3,2,1,0:T(8,128)(2,1)}, u32[]{:S(2)}) copy-start(bf16[1,16,32,192]{3,2,1,0:T(8,128)(2,1)} %param.10) | copy-start | bytes 589828
  2.5 23.9 %copy-start.10 = (bf16[192,192]{1,0:T(8,128)(2,1)S(1)}, bf16[192,192]{1,0:T(8,128)(2,1)}, u32[]{:S(2)}) copy-start(bf16[192,192]{1,0:T(8,128)(2,1)} %wp_ref.1) | copy-start | bytes 221188
  2.6 23.9 %copy-start.1 = (bf16[1,16,32,192]{3,2,1,0:T(8,128)(2,1)S(1)}, bf16[1,16,32,192]{3,2,1,0:T(8,128)(2,1)}, u32[]{:S(2)}) copy-start(bf16[1,16,32,192]{3,2,1,0:T(8,128)(2,1)} %param.11) | copy-start | bytes 589828
  2.6 23.9 %collective-permute-start = (bf16[2,4,32,192]{3,2,1,0:T(8,128)(2,1)S(1)}, bf16[2,4,32,192]{3,2,1,0:T(8,128)(2,1)S(1)}, u32[]{:S(2)}, u32[]{:S(2)}) collective-permute-start(bf16[2,4,32,192]{3,2,1,0:T(8,128)(2,1)S(1)} %get-tuple-element.24), channel_id=1, source_target_pairs={{8,0},{16,8},{24,16},{32,24},{40,32},{48,40},{56,48},{0,56},{9,1},... | collective-permute-start | bytes 294920 | tf_op jit(solution)/shard_map/ppermute | solution.py:336
  11.5 13.0 %copy-start.6 = (f32[576]{0:T(1024)S(1)}, f32[576]{0:T(1024)}, u32[]{:S(2)}) copy-start(f32[576]{0:T(1024)} %qb_ref.1) | copy-start | bytes 6916
  11.6 12.9 %copy-start.5 = (f32[225,6]{0,1:T(8,128)S(1)}, f32[225,6]{0,1:T(8,128)}, u32[]{:S(2)}) copy-start(f32[225,6]{0,1:T(8,128)} %param.18) | copy-start | bytes 16204
  11.6 14.8 %collective-permute-start.1 = (bf16[2,16,4,192]{3,2,1,0:T(4,128)(2,1)S(1)}, bf16[2,16,4,192]{3,2,1,0:T(4,128)(2,1)S(1)}, u32[]{:S(2)}, u32[]{:S(2)}) collective-permute-start(bf16[2,16,4,192]{3,2,1,0:T(4,128)(2,1)S(1)} %pad_maximum_fusion.1), channel_id=1, source_target_pairs={{1,0},{2,1},{3,2},{4,3},{5,4},{6,5},{7,6},{0,7},{9,8},{10,9},{11,1... | collective-permute-start | bytes 147464 | tf_op jit(solution)/shard_map/ppermute | solution.py:336
  19.1 5.4 %copy-start.8 = (f32[192]{0:T(256)S(1)}, f32[192]{0:T(256)}, u32[]{:S(2)}) copy-start(f32[192]{0:T(256)} %lb_ref.1) | copy-start | bytes 2308
  19.1 7.4 %collective-permute-start.2 = (bf16[2,4,4,192]{3,2,1,0:T(4,128)(2,1)S(1)}, bf16[2,4,4,192]{3,2,1,0:T(4,128)(2,1)S(1)}, u32[]{:S(2)}, u32[]{:S(2)}) collective-permute-start(bf16[2,4,4,192]{3,2,1,0:T(4,128)(2,1)S(1)} %get-tuple-element.25), channel_id=1, source_target_pairs={{9,0},{10,1},{11,2},{12,3},{13,4},{14,5},{15,6},{8,7},{17,8},{18,9... | collective-permute-start | bytes 36872 | tf_op jit(solution)/shard_map/ppermute | solution.py:343
  24.5 0.7 copy-start.7
  25.1 1.4 %copy-start.11 = (s32[16,32]{1,0:T(8,128)S(1)}, s32[16,32]{1,0:T(8,128)}, u32[]{:S(2)}) copy-start(s32[16,32]{1,0:T(8,128)} %ids_ref.1) | copy-start | bytes 6148
  26.5 0.9 %copy-start.9 = (bf16[192,576]{1,0:T(8,128)(2,1)S(1)}, bf16[192,576]{1,0:T(8,128)(2,1)}, u32[]{:S(2)}) copy-start(bf16[192,576]{1,0:T(8,128)(2,1)} %w_ref.1) | copy-start | bytes 663556
  34.2 3.7 %collective-permute-start.5 = (bf16[32,24,128]{2,1,0:T(8,128)(2,1)S(1)}, bf16[32,24,128]{2,1,0:T(8,128)(2,1)S(1)}, u32[]{:S(2)}, u32[]{:S(2)}) collective-permute-start(bf16[32,24,128]{2,1,0:T(8,128)(2,1)S(1)} %get-tuple-element.32), channel_id=1, source_target_pairs={{0,8},{8,0},{1,9},{9,1},{2,10},{10,2},{3,11},{11,3},{4,12},{12,4},... | collective-permute-start | bytes 589832 | tf_op jit(solution)/shard_map/ppermute | solution.py:437
  56.7 14.4 %all-to-all-start.1 = ((bf16[8,24,128]{2,1,0:T(8,128)(2,1)}), bf16[8,24,128]{2,1,0:T(8,128)(2,1)S(1)}, u32[]{:S(2)}, u32[]{:S(2)}) async-start(bf16[8,24,128]{2,1,0:T(8,128)(2,1)} %shard_map.165), calls=%async_computation.1 | async-start | bytes 98304 | tf_op jit(solution)/shard_map/all_to_all | solution.py:441
  64.0 7.1 %collective-permute-start.3 = (bf16[4,32,192]{2,1,0:T(8,128)(2,1)S(1)}, bf16[4,32,192]{2,1,0:T(8,128)(2,1)S(1)}, u32[]{:S(2)}, u32[]{:S(2)}) collective-permute-start(bf16[4,32,192]{2,1,0:T(8,128)(2,1)S(1)} %get-tuple-element.29), channel_id=1, source_target_pairs={{56,0},{0,8},{8,16},{16,24},{24,32},{32,40},{40,48},{48,56},{57,1}... | collective-permute-start | bytes 147464 | tf_op jit(solution)/shard_map/ppermute | solution.py:336
  71.8 14.7 %all-to-all-start.2 = ((bf16[32,24,128]{2,1,0:T(8,128)(2,1)}), bf16[32,24,128]{2,1,0:T(8,128)(2,1)S(1)}, u32[]{:S(2)}, u32[]{:S(2)}) async-start(bf16[32,24,128]{2,1,0:T(8,128)(2,1)} %shard_map.166), calls=%async_computation.2 | async-start | bytes 393216 | tf_op jit(solution)/shard_map/all_to_all | solution.py:447
  75.7 10.7 %collective-permute-start.4 = (bf16[16,4,192]{2,1,0:T(4,128)(2,1)S(1)}, bf16[16,4,192]{2,1,0:T(4,128)(2,1)S(1)}, u32[]{:S(2)}, u32[]{:S(2)}) collective-permute-start(bf16[16,4,192]{2,1,0:T(4,128)(2,1)S(1)} %fusion.3), channel_id=1, source_target_pairs={{7,0},{0,1},{1,2},{2,3},{3,4},{4,5},{5,6},{6,7},{15,8},{8,9},{9,10... | collective-permute-start | bytes 73736 | tf_op jit(solution)/shard_map/ppermute | solution.py:336
  86.5 7.0 %collective-permute-start.6 = (bf16[32,24,128]{2,1,0:T(8,128)(2,1)S(1)}, bf16[32,24,128]{2,1,0:T(8,128)(2,1)S(1)}, u32[]{:S(2)}, u32[]{:S(2)}) collective-permute-start(bf16[32,24,128]{2,1,0:T(8,128)(2,1)S(1)} %all-to-all-done.2.mine_ref), channel_id=1, source_target_pairs={{0,8},{8,0},{1,9},{9,1},{2,10},{10,2},{3,11},{11,3},{4,12},{12,4},... | collective-permute-start | bytes 589832 | tf_op jit(solution)/shard_map/ppermute | solution.py:448

commit v3 on v2

--- a/solution.py
+++ b/solution.py
@@ -69,10 +69,40 @@
     return jnp.sum(pltpu.roll(total, 0, 1, stride=1, stride_axis=0), 0, keepdims=True)
 
 
-def prepare_kernel(pos_ref, table_ref, ls_ref, lb_ref, qb_ref, bias_ref, perm_ref, rows_ref):
+def prepare_kernel(
+    pos_ref,
+    table_ref,
+    ids_ref,
+    w_ref,
+    ls_ref,
+    lb_ref,
+    qb_ref,
+    bias_ref,
+    perm_ref,
+    apart_ref,
+    parts_ref,
+    rows_ref,
+):
     rows_ref[0, 0:CHAN] = ls_ref[...]
     rows_ref[1, 0:CHAN] = lb_ref[...]
     rows_ref[2, :] = qb_ref[...]
+    w = w_ref[...]
+    for i in range(3):
+        parts_ref[i] = w[:, CHAN * i : CHAN * i + CHAN]
+
+    token, tile_row = iota((8 * TOK, ROWS), 0), iota((8 * TOK, ROWS), 1)
+    window, inside = token // TOK, token % TOK
+    pick_row = (tile_row == WIN * (window // 4) + inside // WIN).astype(BF)
+    spread_ids = nn(pick_row, ids_ref[...].astype(F32).astype(BF))
+    token, tile_col = iota((8 * TOK, COLS), 0), iota((8 * TOK, COLS), 1)
+    window, inside = token // TOK, token % TOK
+    pick_col = tile_col == WIN * (window % 4) + inside % WIN
+    ids = jnp.sum(jnp.where(pick_col, spread_ids, 0.0), -1, keepdims=True)
+    region = (ids == iota((8 * TOK, 16), 1).astype(F32)).astype(BF)
+    for win in range(8):
+        own = region[TOK * win : TOK * win + TOK]
+        apart_ref[win] = nt(own, jnp.concatenate([own, own], axis=0)) * 100.0 - 100.0
+
     pos = pos_ref[...]
     both = jnp.concatenate([pos, jnp.ones_like(pos)], axis=1).astype(F32).astype(BF)
     spread = nn(both, spread_pair())
@@ -116,11 +146,11 @@
     row_ref,
     col_ref,
     corner_ref,
-    ids_ref,
-    w_ref,
+    parts_ref,
     wp_ref,
     bias_ref,
     perm_ref,
+    apart_ref,
     rows_ref,
     core_ref,
     ds_ref,
@@ -141,6 +171,12 @@
     dq_ref,
     dk_ref,
     dv_ref,
+    qh_ref,
+    dah_ref,
+    p_ref,
+    dp_ref,
+    pb_ref,
+    dsb_ref,
 ):
     scale = DIM ** (-0.5)
 
@@ -169,22 +205,11 @@
     ls, lb, qb = rows_ref[0:1, 0:CHAN], rows_ref[1:2, 0:CHAN], rows_ref[2:3, :]
     normed = (xhat * ls + lb).astype(BF)
     normed_ref[...] = normed
-    w = w_ref[...]
-    w_q, w_k, w_v = w[:, 0:CHAN], w[:, CHAN : 2 * CHAN], w[:, 2 * CHAN : 3 * CHAN]
+    w_q, w_k, w_v = parts_ref[0], parts_ref[1], parts_ref[2]
     q_ref[...] = ((nn(normed, w_q) + qb[:, 0:CHAN]) * scale).astype(BF)
     k_ref[...] = (nn(normed, w_k) + qb[:, CHAN : 2 * CHAN]).astype(BF)
     v_ref[...] = (nn(normed, w_v) + qb[:, 2 * CHAN : 3 * CHAN]).astype(BF)
     da_ref[...] = nt(grad_ref[...], wp_ref[...]).astype(BF)
-
-    token, tile_row = iota((8 * TOK, ROWS), 0), iota((8 * TOK, ROWS), 1)
-    window, inside = token // TOK, token % TOK
-    pick_row = (tile_row == WIN * (window // 4) + inside // WIN).astype(BF)
-    spread_ids = nn(pick_row, ids_ref[...].astype(F32).astype(BF))
-    token, tile_col = iota((8 * TOK, COLS), 0), iota((8 * TOK, COLS), 1)
-    window, inside = token // TOK, token % TOK
-    pick_col = tile_col == WIN * (window % 4) + inside % WIN
-    ids = jnp.sum(jnp.where(pick_col, spread_ids, 0.0), -1, keepdims=True)
-    region = (ids == iota((8 * TOK, 16), 1).astype(F32)).astype(BF)
 
     head_of = iota((TOK, CHAN), 1) // DIM
 
@@ -198,27 +223,29 @@
             total = jnp.where(head_of == h, a[TOK * h : TOK * h + TOK], total)
         return total
 
+    windows = [slice(TOK * win, TOK * win + TOK) for win in range(8)]
+    for win, s in enumerate(windows):
+        qh_ref[win] = by_head(q_ref[s])
+        dah_ref[win] = by_head(da_ref[s])
+    for win, s in enumerate(windows):
+        apart = jnp.concatenate([apart_ref[win]] * 3, axis=1)
+        p_ref[win] = nt(k_ref[s], qh_ref[win]) + bias_ref[...] + apart
+        dp_ref[win] = nt(v_ref[s], dah_ref[win])
     d_sum = jnp.zeros((TOK, HEADS * TOK), F32)
     for win in range(8):
-        s = slice(TOK * win, TOK * win + TOK)
-        q_heads = by_head(q_ref[s])
-        key = k_ref[s]
-        value = v_ref[s]
-        apart = nt(region[s], jnp.concatenate([region[s]] * 2, axis=0)) * 100.0 - 100.0
-        scores = nt(key, q_heads) + bias_ref[...] + jnp.concatenate([apart] * 3, axis=1)
-        top = jnp.max(scores, 0, keepdims=True)
-        e = jnp.exp(scores - top)
+        scores = p_ref[win]
+        e = jnp.exp(scores - jnp.max(scores, 0, keepdims=True))
         p = e * (1.0 / jnp.sum(e, 0, keepdims=True))
-        pb = p.astype(BF)
-        attn_ref[s] = own_head(tn(pb, value)).astype(BF)
-        da_heads = by_head(da_ref[s])
-        d_p = nt(value, da_heads)
-        dv_ref[s] = nn(pb, da_heads).astype(BF)
+        pb_ref[win] = p.astype(BF)
+        d_p = dp_ref[win]
         d_s = p * (d_p - jnp.sum(d_p * p, 0, keepdims=True))
         d_sum += d_s
-        d_sb = d_s.astype(BF)
-        dq_ref[s] = (own_head(tn(d_sb, key)) * scale).astype(BF)
-        dk_ref[s] = nn(d_sb, q_heads).astype(BF)
+        dsb_ref[win] = d_s.astype(BF)
+    for win, s in enumerate(windows):
+        attn_ref[s] = own_head(tn(pb_ref[win], v_ref[s])).astype(BF)
+        dv_ref[s] = nn(pb_ref[win], dah_ref[win]).astype(BF)
+        dq_ref[s] = (own_head(tn(dsb_ref[win], k_ref[s])) * scale).astype(BF)
+        dk_ref[s] = nn(dsb_ref[win], qh_ref[win]).astype(BF)
 
     parts = [a for pair in range(3) for a in split(d_sum[:, 128 * pair : 128 * pair + 128])]
     spread = nn(jnp.concatenate(parts, axis=0), spread_pair())
@@ -282,10 +309,18 @@
     return total
 
 
-def sum_kernel(got_ref, out_ref):
+def sum_kernel(got_ref, after_ref, out_ref):
     total = add_up(got_ref, got_ref.shape[0]).astype(BF)
     for i in range(out_ref.shape[0]):
         out_ref[i] = total
+
+
+def sum_edge_kernel(got_ref, above_ref, ds_ref, out_ref, edge_ref):
+    total = add_up(got_ref, got_ref.shape[0]).astype(BF)
+    for i in range(out_ref.shape[0]):
+        out_ref[i] = total
+    edge_ref[0:SHIFT] = above_ref[:, COLS - SHIFT : COLS]
+    edge_ref[SHIFT:ROWS] = ds_ref[0 : ROWS - SHIFT, COLS - SHIFT : COLS].astype(BF)
 
 
 def pair_kernel(mine_ref, got_ref, out_ref):
@@ -347,11 +382,17 @@
 WHOLE = pl.BlockSpec(memory_space=pltpu.VMEM)
 
 
-def prepare(position_index, bias_table, ls, lb, qb):
+def prepare(*args):
     return kernel_call(
         prepare_kernel,
-        (shape((TOK, HEADS * TOK)), shape((OFF, OFF), BF), shape((8, 3 * CHAN))),
-    )(position_index, bias_table.T, ls, lb, qb)
+        (
+            shape((TOK, HEADS * TOK)),
+            shape((OFF, OFF), BF),
+            shape((8, TOK, 128)),
+            shape((3, CHAN, CHAN), BF),
+            shape((8, 3 * CHAN)),
+        ),
+    )(*args)
 
 
 def halos(x, g):
@@ -380,7 +421,10 @@
             pltpu.VMEM((tokens, CHAN), F32),
             pltpu.VMEM((tokens, 1), F32),
         ]
-        + [pltpu.VMEM((tokens, CHAN), BF)] * 10,
+        + [pltpu.VMEM((tokens, CHAN), BF)] * 10
+        + [pltpu.VMEM((8, HEADS * TOK, CHAN), BF)] * 2
+        + [pltpu.VMEM((8, TOK, HEADS * TOK), F32)] * 2
+        + [pltpu.VMEM((8, TOK, HEADS * TOK), BF)] * 2,
         flops=10**9,
         in_specs=[WHOLE] * (len(args) - 1) + [SMALL],
     )(*args)
@@ -390,8 +434,15 @@
     return kernel_call(pair_kernel, shape(mine.shape, BF))(mine, got)
 
 
-def chunk_sum(got, copies):
-    return kernel_call(sum_kernel, shape((copies,) + got.shape[1:], BF))(got)
+def chunk_sum(got, copies, after):
+    return kernel_call(sum_kernel, shape((copies,) + got.shape[1:], BF))(got, after)
+
+
+def chunk_sum_edge(got, copies, above, d_shifted):
+    return kernel_call(
+        sum_edge_kernel,
+        (shape((copies,) + got.shape[1:], BF), shape((ROWS, SHIFT, CHAN), BF)),
+    )(got, above, d_shifted)
 
 
 def unpack(mine, got, core):
@@ -428,23 +479,23 @@
     col = moved(jnp.stack([x[:, :SHIFT], g[:, :SHIFT]]), COL, -1)
     row, corner = halos(x, g)
     row, corner = moved(row, ROW, -1), moved_corner(corner)
-    bias, perm, rows = prepare(
-        position_index, bias_table, layernorm_scale, layernorm_bias, qkv_bias
+    bias, perm, apart, parts, rows = prepare(
+        position_index, bias_table.T, region_ids, qkv_weight, layernorm_scale, layernorm_bias, qkv_bias
     )
     d_shifted, edge, mine, other = main(
-        x, g, row, col, corner, region_ids, qkv_weight, proj_weight, bias, perm, rows, core
+        x, g, row, col, corner, parts, proj_weight, bias, perm, apart, rows, core
     )
     half = pair_sum(mine, lax.ppermute(other, "c", [(0, 1), (1, 0)]))
     above = moved(edge, ROW, 1)
     got = lax.all_to_all(half, FIRST, 0, 0, tiled=True)
-    part = chunk_sum(got, 8)
+    part = chunk_sum(got, 8, above)
     got = lax.all_to_all(part, SECOND, 0, 0, tiled=True)
-    whole = chunk_sum(got, CHUNKS)
+    whole, edge = chunk_sum_edge(got, CHUNKS, above, d_shifted)
+    left = moved(edge, COL, 1)
+    gathered = lax.all_to_all(whole, FIRST, 0, 0, tiled=True)
     back = jnp.concatenate([above.astype(F32), d_shifted[: ROWS - SHIFT]], axis=0)
-    left = moved(back[:, COLS - SHIFT :].astype(BF), COL, 1)
     back = jnp.concatenate([left.astype(F32), back[:, : COLS - SHIFT]], axis=1)
     grad_x = (g.astype(F32) + back).astype(BF)[None]
-    gathered = lax.all_to_all(whole, FIRST, 0, 0, tiled=True)
     other = lax.ppermute(gathered, "c", [(0, 1), (1, 0)])
     w, wb, p, pb, ns, nb, table = unpack(gathered, other, core)
     return (grad_x, w, wb, p, pb, ns, nb, table.T)

time: 95 us -> 92.9 us (0.978)
  waiting for transfers between devices: 10.2 us -> 17.5 us
  blocking collectives: 18.1 us -> 13.8 us
  Pallas kernels: 10.4 us -> 8.15 us
  local copies, waits for them, and re-layouts: 3.56 us -> 2 us
  starting transfers between devices: 50.3 us -> 49.1 us
    all_to_all x1, waiting for transfers between devices: 0.01 us -> 7.28 us  [on_device(): got = lax.all_to_all(half, FIRST, 0, 0, tiled=True)]
    all_to_all x1, blocking collectives: 18.1 us -> 13.8 us  [on_device(): got = lax.all_to_all(part, SECOND, 0, 0, tiled=True)]
    ppermute x4, starting transfers between devices: 25.2 us -> 21.6 us  [moved(): lax.ppermute(block, axes, [((i - distance) % count, i) for i in range(cou...]
    pallas_call x1, Pallas kernels: 6.72 us -> 4.09 us  [main(): kernel_call(main_kernel, (shape((ROWS, COLS, CHAN)), shape((SHIFT, COLS,...]
    unnamed x24, local copies, waits for them, and re-layouts: 3.51 us -> 1.95 us
    ppermute x1, starting transfers between devices: 5.97 us -> 7.52 us  [on_device(): other = lax.ppermute(gathered, 'c', [(0, 1), (1, 0)])]
  transfers between devices with their start and end apart: 9 -> 9, of which waited for: 4 -> 5; matrix products, arithmetic and copies ran while one was open for 1% -> 1% of each run, Pallas kernels for 1% -> 2%
where the time goes in v3:
time: 92.9 us; the launch traced here: 92.4 us
  starting transfers between devices  49.1 us (53%)
  waiting for transfers between devices  17.5 us (19%)
  blocking collectives  13.8 us (15%)
  Pallas kernels  8.15 us (9%)
  local copies, waits for them, and re-layouts  2 us (2%)
  between operations  0.95 us (1%)
    ppermute x4, starting transfers between devices, moved(): lax.ppermute(block, axes, [((i - distance) % count, i) for i in range(cou...  21.6 us
    all_to_all x1, blocking collectives, on_device(): got = lax.all_to_all(part, SECOND, 0, 0, tiled=True)  13.8 us
    ppermute x4, waiting for transfers between devices, moved(): lax.ppermute(block, axes, [((i - distance) % count, i) for i in range(cou...  8.93 us
    all_to_all x1, starting transfers between devices, on_device(): got = lax.all_to_all(half, FIRST, 0, 0, tiled=True)  7.75 us
    ppermute x1, starting transfers between devices, on_device(): other = lax.ppermute(gathered, 'c', [(0, 1), (1, 0)])  7.52 us
    all_to_all x1, waiting for transfers between devices, on_device(): got = lax.all_to_all(half, FIRST, 0, 0, tiled=True)  7.28 us
    ppermute x1, starting transfers between devices, moved_corner(): return lax.ppermute(block, ROW + COL, pairs)  5.35 us
    pallas_call x1, Pallas kernels, main(): kernel_call(main_kernel, (shape((ROWS, COLS, CHAN)), shape((SHIFT, COLS,...  4.09 us
  transfers between devices with their start and end apart: 9, of which 5 were waited for; matrix products, arithmetic and copies ran while one was open for 1% of the time, Pallas kernels for 2%

profile of v3, /device:TPU:1, one launch (start us, length us, event | category | flops | bytes accessed | tf_op | source)
XLA Modules:
  0.0 92.4 jit_solution(17887321898129262655)
XLA Ops:
  0.6 0.0 copy-start
  0.6 0.9 %copy-done = bf16[1,16,32,192]{3,2,1,0:T(8,128)(2,1)S(1)} copy-done((bf16[1,16,32,192]{3,2,1,0:T(8,128)(2,1)S(1)}, bf16[1,16,32,192]{3,2,1,0:T(8,128)(2,1)}, u32[]{:S(2)}) %copy-start) | copy-done | bytes 196632
  1.6 0.0 copy-start.2
  1.6 0.9 %copy-done.2 = bf16[1,16,32,192]{3,2,1,0:T(8,128)(2,1)S(1)} copy-done((bf16[1,16,32,192]{3,2,1,0:T(8,128)(2,1)S(1)}, bf16[1,16,32,192]{3,2,1,0:T(8,128)(2,1)}, u32[]{:S(2)}) %copy-start.2) | copy-done | bytes 196632
  2.5 0.0 copy-start.4
  2.5 0.0 copy-start.5
  2.5 0.0 copy-start.11
  2.6 0.0 copy-start.7
  2.6 8.9 %collective-permute-start = (bf16[2,4,32,192]{3,2,1,0:T(8,128)(2,1)S(1)}, bf16[2,4,32,192]{3,2,1,0:T(8,128)(2,1)S(1)}, u32[]{:S(2)}, u32[]{:S(2)}) collective-permute-start(bf16[2,4,32,192]{3,2,1,0:T(8,128)(2,1)S(1)} %get-tuple-element.28), channel_id=1, source_target_pairs={{8,0},{16,8},{24,16},{32,24},{40,32},{48,40},{56,48},{0,56},{9,1},... | collective-permute-start | bytes 294920 | tf_op jit(solution)/shard_map/ppermute | solution.py:371
  11.5 0.0 copy-start.6
  11.5 0.0 copy-start.9
  11.5 0.0 copy-start.3
  11.6 0.0 copy-start.1
  11.6 0.1 pad_maximum_fusion.1
  11.7 7.6 %collective-permute-start.1 = (bf16[2,16,4,192]{3,2,1,0:T(4,128)(2,1)S(1)}, bf16[2,16,4,192]{3,2,1,0:T(4,128)(2,1)S(1)}, u32[]{:S(2)}, u32[]{:S(2)}) collective-permute-start(bf16[2,16,4,192]{3,2,1,0:T(4,128)(2,1)S(1)} %pad_maximum_fusion.1), channel_id=1, source_target_pairs={{1,0},{2,1},{3,2},{4,3},{5,4},{6,5},{7,6},{0,7},{9,8},{10,9},{11,1... | collective-permute-start | bytes 147464 | tf_op jit(solution)/shard_map/ppermute | solution.py:371
  19.3 5.4 %collective-permute-start.2 = (bf16[2,4,4,192]{3,2,1,0:T(4,128)(2,1)S(1)}, bf16[2,4,4,192]{3,2,1,0:T(4,128)(2,1)S(1)}, u32[]{:S(2)}, u32[]{:S(2)}) collective-permute-start(bf16[2,4,4,192]{3,2,1,0:T(4,128)(2,1)S(1)} %get-tuple-element.29), channel_id=1, source_target_pairs={{9,0},{10,1},{11,2},{12,3},{13,4},{14,5},{15,6},{8,7},{17,8},{18,9... | collective-permute-start | bytes 36872 | tf_op jit(solution)/shard_map/ppermute | solution.py:378
  24.6 0.0 copy-done.4
  24.6 0.0 copy-done.5
  24.6 0.0 copy-done.8
  24.7 0.0 copy-done.10
  24.7 0.0 copy-done.7
  24.7 0.0 copy-done.6
  24.7 0.0 copy-done.9
  24.7 1.6 %shard_map.162 = (f32[64,384]{1,0:T(8,128)S(1)}, bf16[256,256]{1,0:T(8,128)(2,1)S(1)}, f32[8,64,128]{2,1,0:T(8,128)S(1)}, bf16[3,192,192]{2,1,0:T(8,128)(2,1)S(1)}, f32[8,576]{1,0:T(8,128)S(1)}) custom-call(s32[64,64]{1,0:T(8,128)S(1)} %copy-done.5, f32[6,225]{1,0:T(8,128)S(1)} %bitcast.20, s32[16,32]{1,0:T(8,128)S(1)} %copy-done.7, ...), custom_call_target="tpu_custom_call" | custom-call | flops 10000000 | bytes 1000000 | tf_op jit(solution)/shard_map/pallas_call | solution.py:386
  26.3 0.0 collective-permute-done.2.corner_ref
  26.4 0.0 collective-permute-done.1.col_ref
  26.4 0.0 collective-permute-done.row_ref
  26.4 0.0 copy-done.11
  26.4 0.0 copy-done.3
  26.4 0.0 copy-done.1
  26.4 4.1 %shard_map.163 = (f32[16,32,192]{2,1,0:T(8,128)S(1)}, bf16[4,32,192]{2,1,0:T(8,128)(2,1)S(1)}, bf16[32,24,128]{2,1,0:T(8,128)(2,1)S(1)}, bf16[32,24,128]{2,1,0:T(8,128)(2,1)S(1)}) custom-call(bf16[16,32,192]{2,1,0:T(8,128)(2,1)S(1)} %bitcast.19, bf16[16,32,192]{2,1,0:T(8,128)(2,1)S(1)} %bitcast.16, bf16[2,4,32,192]{3,2,1,0:T(8,128)(2,1)S(1)} %collective-permute-done.row_ref, ...), custom_call_target="tpu_custom_call" | custom-call | flops 1000000000 | bytes 1000000 | tf_op jit(solution)/shard_map/pallas_call | solution.py:410
  30.5 2.9 %collective-permute-start.3 = (bf16[32,24,128]{2,1,0:T(8,128)(2,1)S(1)}, bf16[32,24,128]{2,1,0:T(8,128)(2,1)S(1)}, u32[]{:S(2)}, u32[]{:S(2)}) collective-permute-start(bf16[32,24,128]{2,1,0:T(8,128)(2,1)S(1)} %get-tuple-element.36), channel_id=1, source_target_pairs={{0,8},{8,0},{1,9},{9,1},{2,10},{10,2},{3,11},{11,3},{4,12},{12,4},... | collective-permute-start | bytes 589832 | tf_op jit(solution)/shard_map/ppermute | solution.py:488
  33.4 1.0 %collective-permute-done.3.got_ref = bf16[32,24,128]{2,1,0:T(8,128)(2,1)S(1)} collective-permute-done((bf16[32,24,128]{2,1,0:T(8,128)(2,1)S(1)}, bf16[32,24,128]{2,1,0:T(8,128)(2,1)S(1)}, u32[]{:S(2)}, u32[]{:S(2)}) %collective-permute-start.3) | collective-permute-done | bytes 196640 | tf_op jit(solution)/shard_map/ppermute | solution.py:488
  34.4 0.7 shard_map.164
  35.1 7.7 %all-to-all-start = ((bf16[32,24,128]{2,1,0:T(8,128)(2,1)}), bf16[32,24,128]{2,1,0:T(8,128)(2,1)S(1)}, u32[]{:S(2)}, u32[]{:S(2)}) async-start(bf16[32,24,128]{2,1,0:T(8,128)(2,1)} %shard_map.164), calls=%async_computation | async-start | bytes 393216 | tf_op jit(solution)/shard_map/all_to_all | solution.py:490
  42.9 1.9 %collective-permute-start.4 = (bf16[4,32,192]{2,1,0:T(8,128)(2,1)S(1)}, bf16[4,32,192]{2,1,0:T(8,128)(2,1)S(1)}, u32[]{:S(2)}, u32[]{:S(2)}) collective-permute-start(bf16[4,32,192]{2,1,0:T(8,128)(2,1)S(1)} %get-tuple-element.37), channel_id=1, source_target_pairs={{56,0},{0,8},{8,16},{16,24},{24,32},{32,40},{40,48},{48,56},{57,1}... | collective-permute-start | bytes 147464 | tf_op jit(solution)/shard_map/ppermute | solution.py:371
  44.8 1.4 %collective-permute-done.4.after_ref.above_ref = bf16[4,32,192]{2,1,0:T(8,128)(2,1)S(1)} collective-permute-done((bf16[4,32,192]{2,1,0:T(8,128)(2,1)S(1)}, bf16[4,32,192]{2,1,0:T(8,128)(2,1)S(1)}, u32[]{:S(2)}, u32[]{:S(2)}) %collective-permute-start.4) | collective-permute-done | bytes 49184 | tf_op jit(solution)/shard_map/ppermute | solution.py:371
  46.2 7.3 %all-to-all-done.got_ref = bf16[32,24,128]{2,1,0:T(8,128)(2,1)S(1)} async-done(((bf16[32,24,128]{2,1,0:T(8,128)(2,1)}), bf16[32,24,128]{2,1,0:T(8,128)(2,1)S(1)}, u32[]{:S(2)}, u32[]{:S(2)}) %all-to-all-start) | async-done | bytes 196640 | tf_op jit(solution)/shard_map/all_to_all | solution.py:490
  53.5 13.8 %all_to_all.15.got_ref = bf16[8,24,128]{2,1,0:T(8,128)(2,1)S(1)} all-to-all(bf16[8,24,128]{2,1,0:T(8,128)(2,1)S(1)} %shard_map.165), channel_id=1, replica_groups=mesh['y'=8,'zl'=4,'c'=2,'zh'=2,'x'=4] {'zl','zh'}, dimensions={0} | all-to-all | bytes 98304 | tf_op jit(solution)/shard_map/all_to_all | solution.py:492
  67.3 0.7 shard_map.166
  68.0 4.0 %all-to-all-start.2 = ((bf16[32,24,128]{2,1,0:T(8,128)(2,1)}), bf16[32,24,128]{2,1,0:T(8,128)(2,1)S(1)}, u32[]{:S(2)}, u32[]{:S(2)}) async-start(bf16[32,24,128]{2,1,0:T(8,128)(2,1)} %get-tuple-element.40), calls=%async_computation.2 | async-start | bytes 393216 | tf_op jit(solution)/shard_map/all_to_all | solution.py:495
  72.1 3.1 %collective-permute-start.5 = (bf16[16,4,192]{2,1,0:T(4,128)(2,1)S(1)}, bf16[16,4,192]{2,1,0:T(4,128)(2,1)S(1)}, u32[]{:S(2)}, u32[]{:S(2)}) collective-permute-start(bf16[16,4,192]{2,1,0:T(4,128)(2,1)S(1)} %get-tuple-element.39), channel_id=1, source_target_pairs={{7,0},{0,1},{1,2},{2,3},{3,4},{4,5},{5,6},{6,7},{15,8},{8,9},{9,10... | collective-permute-start | bytes 73736 | tf_op jit(solution)/shard_map/ppermute | solution.py:371
  75.3 7.6 %collective-permute-done.5 = bf16[16,4,192]{2,1,0:T(4,128)(2,1)S(1)} collective-permute-done((bf16[16,4,192]{2,1,0:T(4,128)(2,1)S(1)}, bf16[16,4,192]{2,1,0:T(4,128)(2,1)S(1)}, u32[]{:S(2)}, u32[]{:S(2)}) %collective-permute-start.5) | collective-permute-done | bytes 24608 | tf_op jit(solution)/shard_map/ppermute | solution.py:371
  82.9 0.0 all-to-all-done.2.mine_ref
  82.9 7.5 %collective-permute-start.6 = (bf16[32,24,128]{2,1,0:T(8,128)(2,1)S(1)}, bf16[32,24,128]{2,1,0:T(8,128)(2,1)S(1)}, u32[]{:S(2)}, u32[]{:S(2)}) collective-permute-start(bf16[32,24,128]{2,1,0:T(8,128)(2,1)S(1)} %all-to-all-done.2.mine_ref), channel_id=1, source_target_pairs={{0,8},{8,0},{1,9},{9,1},{2,10},{10,2},{3,11},{11,3},{4,12},{12,4},... | collective-permute-start | bytes 589832 | tf_op jit(solution)/shard_map/ppermute | solution.py:499
  90.4 0.8 fusion.1
  91.2 0.2 collective-permute-done.6.got_ref
  91.5 0.9 %shard_map.167 = (f32[192,576]{1,0:T(8,128)}, f32[576]{0:T(1024)}, f32[192,192]{1,0:T(8,128)}, f32[192]{0:T(256)}, f32[192]{0:T(256)}, /*index=5*/f32[192]{0:T(256)}, f32[6,225]{1,0:T(8,128)}) custom-call(bf16[32,24,128]{2,1,0:T(8,128)(2,1)S(1)} %all-to-all-done.2.mine_ref, bf16[32,24,128]{2,1,0:T(8,128)(2,1)S(1)} %collective-permute-done.6.got_ref, ...), custom_call_target="tpu_custom_call" | custom-call | flops 10000000 | bytes 1000000 | tf_op jit(solution)/shard_map/pallas_call | solution.py:449
  (9 shorter events, 0.2 us)
Async XLA Ops:
  0.6 1.0 %copy-start = (bf16[1,16,32,192]{3,2,1,0:T(8,128)(2,1)S(1)}, bf16[1,16,32,192]{3,2,1,0:T(8,128)(2,1)}, u32[]{:S(2)}) copy-start(bf16[1,16,32,192]{3,2,1,0:T(8,128)(2,1)} %param.11) | copy-start | bytes 589828
  1.6 0.9 %copy-start.2 = (bf16[1,16,32,192]{3,2,1,0:T(8,128)(2,1)S(1)}, bf16[1,16,32,192]{3,2,1,0:T(8,128)(2,1)}, u32[]{:S(2)}) copy-start(bf16[1,16,32,192]{3,2,1,0:T(8,128)(2,1)} %param.10) | copy-start | bytes 589828
  2.5 22.1 %copy-start.4 = (bf16[192,576]{1,0:T(8,128)(2,1)S(1)}, bf16[192,576]{1,0:T(8,128)(2,1)}, u32[]{:S(2)}) copy-start(bf16[192,576]{1,0:T(8,128)(2,1)} %w_ref.1) | copy-start | bytes 663556
  2.5 22.1 %copy-start.5 = (s32[64,64]{1,0:T(8,128)S(1)}, s32[64,64]{1,0:T(8,128)}, u32[]{:S(2)}) copy-start(s32[64,64]{1,0:T(8,128)} %pos_ref.1) | copy-start | bytes 49156
  2.5 22.1 %copy-start.8 = (f32[576]{0:T(1024)S(1)}, f32[576]{0:T(1024)}, u32[]{:S(2)}) copy-start(f32[576]{0:T(1024)} %qb_ref.1) | copy-start | bytes 6916
  2.5 22.1 %copy-start.10 = (f32[192]{0:T(256)S(1)}, f32[192]{0:T(256)}, u32[]{:S(2)}) copy-start(f32[192]{0:T(256)} %lb_ref.1) | copy-start | bytes 2308
  2.5 23.8 %copy-start.11 = (bf16[192,192]{1,0:T(8,128)(2,1)S(1)}, bf16[192,192]{1,0:T(8,128)(2,1)}, u32[]{:S(2)}) copy-start(bf16[192,192]{1,0:T(8,128)(2,1)} %wp_ref.1) | copy-start | bytes 221188
  2.6 22.1 %copy-start.7 = (s32[16,32]{1,0:T(8,128)S(1)}, s32[16,32]{1,0:T(8,128)}, u32[]{:S(2)}) copy-start(s32[16,32]{1,0:T(8,128)} %ids_ref.1) | copy-start | bytes 6148
  2.6 23.8 %collective-permute-start = (bf16[2,4,32,192]{3,2,1,0:T(8,128)(2,1)S(1)}, bf16[2,4,32,192]{3,2,1,0:T(8,128)(2,1)S(1)}, u32[]{:S(2)}, u32[]{:S(2)}) collective-permute-start(bf16[2,4,32,192]{3,2,1,0:T(8,128)(2,1)S(1)} %get-tuple-element.28), channel_id=1, source_target_pairs={{8,0},{16,8},{24,16},{32,24},{40,32},{48,40},{56,48},{0,56},{9,1},... | collective-permute-start | bytes 294920 | tf_op jit(solution)/shard_map/ppermute | solution.py:371
  11.5 13.2 %copy-start.6 = (f32[225,6]{0,1:T(8,128)S(1)}, f32[225,6]{0,1:T(8,128)}, u32[]{:S(2)}) copy-start(f32[225,6]{0,1:T(8,128)} %param.18) | copy-start | bytes 16204
  11.5 13.2 %copy-start.9 = (f32[192]{0:T(256)S(1)}, f32[192]{0:T(256)}, u32[]{:S(2)}) copy-start(f32[192]{0:T(256)} %ls_ref.1) | copy-start | bytes 2308
  11.5 14.8 %copy-start.3 = (bf16[1,16,32,192]{3,2,1,0:T(8,128)(2,1)S(1)}, bf16[1,16,32,192]{3,2,1,0:T(8,128)(2,1)}, u32[]{:S(2)}) copy-start(bf16[1,16,32,192]{3,2,1,0:T(8,128)(2,1)} %param.10) | copy-start | bytes 589828
  11.6 14.8 %copy-start.1 = (bf16[1,16,32,192]{3,2,1,0:T(8,128)(2,1)S(1)}, bf16[1,16,32,192]{3,2,1,0:T(8,128)(2,1)}, u32[]{:S(2)}) copy-start(bf16[1,16,32,192]{3,2,1,0:T(8,128)(2,1)} %param.11) | copy-start | bytes 589828
  11.7 14.7 %collective-permute-start.1 = (bf16[2,16,4,192]{3,2,1,0:T(4,128)(2,1)S(1)}, bf16[2,16,4,192]{3,2,1,0:T(4,128)(2,1)S(1)}, u32[]{:S(2)}, u32[]{:S(2)}) collective-permute-start(bf16[2,16,4,192]{3,2,1,0:T(4,128)(2,1)S(1)} %pad_maximum_fusion.1), channel_id=1, source_target_pairs={{1,0},{2,1},{3,2},{4,3},{5,4},{6,5},{7,6},{0,7},{9,8},{10,9},{11,1... | collective-permute-start | bytes 147464 | tf_op jit(solution)/shard_map/ppermute | solution.py:371
  19.3 7.1 %collective-permute-start.2 = (bf16[2,4,4,192]{3,2,1,0:T(4,128)(2,1)S(1)}, bf16[2,4,4,192]{3,2,1,0:T(4,128)(2,1)S(1)}, u32[]{:S(2)}, u32[]{:S(2)}) collective-permute-start(bf16[2,4,4,192]{3,2,1,0:T(4,128)(2,1)S(1)} %get-tuple-element.29), channel_id=1, source_target_pairs={{9,0},{10,1},{11,2},{12,3},{13,4},{14,5},{15,6},{8,7},{17,8},{18,9... | collective-permute-start | bytes 36872 | tf_op jit(solution)/shard_map/ppermute | solution.py:378
  30.5 3.9 %collective-permute-start.3 = (bf16[32,24,128]{2,1,0:T(8,128)(2,1)S(1)}, bf16[32,24,128]{2,1,0:T(8,128)(2,1)S(1)}, u32[]{:S(2)}, u32[]{:S(2)}) collective-permute-start(bf16[32,24,128]{2,1,0:T(8,128)(2,1)S(1)} %get-tuple-element.36), channel_id=1, source_target_pairs={{0,8},{8,0},{1,9},{9,1},{2,10},{10,2},{3,11},{11,3},{4,12},{12,4},... | collective-permute-start | bytes 589832 | tf_op jit(solution)/shard_map/ppermute | solution.py:488
  35.1 18.3 %all-to-all-start = ((bf16[32,24,128]{2,1,0:T(8,128)(2,1)}), bf16[32,24,128]{2,1,0:T(8,128)(2,1)S(1)}, u32[]{:S(2)}, u32[]{:S(2)}) async-start(bf16[32,24,128]{2,1,0:T(8,128)(2,1)} %shard_map.164), calls=%async_computation | async-start | bytes 393216 | tf_op jit(solution)/shard_map/all_to_all | solution.py:490
  42.9 3.3 %collective-permute-start.4 = (bf16[4,32,192]{2,1,0:T(8,128)(2,1)S(1)}, bf16[4,32,192]{2,1,0:T(8,128)(2,1)S(1)}, u32[]{:S(2)}, u32[]{:S(2)}) collective-permute-start(bf16[4,32,192]{2,1,0:T(8,128)(2,1)S(1)} %get-tuple-element.37), channel_id=1, source_target_pairs={{56,0},{0,8},{8,16},{16,24},{24,32},{32,40},{40,48},{48,56},{57,1}... | collective-permute-start | bytes 147464 | tf_op jit(solution)/shard_map/ppermute | solution.py:371
  68.0 14.8 %all-to-all-start.2 = ((bf16[32,24,128]{2,1,0:T(8,128)(2,1)}), bf16[32,24,128]{2,1,0:T(8,128)(2,1)S(1)}, u32[]{:S(2)}, u32[]{:S(2)}) async-start(bf16[32,24,128]{2,1,0:T(8,128)(2,1)} %get-tuple-element.40), calls=%async_computation.2 | async-start | bytes 393216 | tf_op jit(solution)/shard_map/all_to_all | solution.py:495
  72.1 10.7 %collective-permute-start.5 = (bf16[16,4,192]{2,1,0:T(4,128)(2,1)S(1)}, bf16[16,4,192]{2,1,0:T(4,128)(2,1)S(1)}, u32[]{:S(2)}, u32[]{:S(2)}) collective-permute-start(bf16[16,4,192]{2,1,0:T(4,128)(2,1)S(1)} %get-tuple-element.39), channel_id=1, source_target_pairs={{7,0},{0,1},{1,2},{2,3},{3,4},{4,5},{5,6},{6,7},{15,8},{8,9},{9,10... | collective-permute-start | bytes 73736 | tf_op jit(solution)/shard_map/ppermute | solution.py:371
  82.9 8.6 %collective-permute-start.6 = (bf16[32,24,128]{2,1,0:T(8,128)(2,1)S(1)}, bf16[32,24,128]{2,1,0:T(8,128)(2,1)S(1)}, u32[]{:S(2)}, u32[]{:S(2)}) collective-permute-start(bf16[32,24,128]{2,1,0:T(8,128)(2,1)S(1)} %all-to-all-done.2.mine_ref), channel_id=1, source_target_pairs={{0,8},{8,0},{1,9},{9,1},{2,10},{10,2},{3,11},{11,3},{4,12},{12,4},... | collective-permute-start | bytes 589832 | tf_op jit(solution)/shard_map/ppermute | solution.py:499

commit v4 on v3

--- a/solution.py
+++ b/solution.py
@@ -16,13 +16,13 @@
 TABLE = 225
 OFF = 256
 CHUNKS = 32
-PACK = 24
+PACK = 40
 BF = jnp.bfloat16
 F32 = jnp.float32
 HIGH = lax.Precision.HIGHEST
 
 FIRST = ("y", "x")
-SECOND = ("zl", "zh")
+SECOND = ("zl", "c", "zh")
 ROW = ("zl", "c")
 COL = ("zh", "x")
 
@@ -152,11 +152,8 @@
     perm_ref,
     apart_ref,
     rows_ref,
-    core_ref,
     ds_ref,
     edge_ref,
-    mine_ref,
-    other_ref,
     pack_ref,
     ext_ref,
     xhat_ref,
@@ -290,16 +287,13 @@
     high = small.astype(BF).astype(F32)
     small = jnp.concatenate([high, small - high], axis=0)
     packed = jnp.concatenate([weights, small], axis=0)
-    for chunk in range(50):
+    for chunk in range(30):
         tiles = []
-        for tile in range(3 * chunk, 3 * chunk + 3):
+        for tile in range(5 * chunk, 5 * chunk + 5):
             r, c = tile // 6, tile % 6
             tiles.append(packed[8 * r : 8 * r + 8, 128 * c : 128 * c + 128])
-        pack_ref[chunk // 25, chunk % 25] = jnp.concatenate(tiles, axis=0).astype(BF)
-    pack_ref[:, 25:CHUNKS] = jnp.zeros((2, CHUNKS - 25, PACK, 128), BF)
-    core = core_ref[0]
-    mine_ref[...] = pack_ref[core]
-    other_ref[...] = pack_ref[1 - core]
+        pack_ref[chunk] = jnp.concatenate(tiles, axis=0).astype(BF)
+    pack_ref[30:CHUNKS] = jnp.zeros((CHUNKS - 30, PACK, 128), BF)
 
 
 def add_up(ref, count):
@@ -323,20 +317,13 @@
     edge_ref[SHIFT:ROWS] = ds_ref[0 : ROWS - SHIFT, COLS - SHIFT : COLS].astype(BF)
 
 
-def pair_kernel(mine_ref, got_ref, out_ref):
-    out_ref[...] = (mine_ref[...].astype(F32) + got_ref[...].astype(F32)).astype(BF)
-
-
 def unpack_kernel(
-    mine_ref, got_ref, core_ref, w_ref, wb_ref, p_ref, pb_ref, ns_ref, nb_ref, table_ref, half_ref, all_ref
+    got_ref, w_ref, wb_ref, p_ref, pb_ref, ns_ref, nb_ref, table_ref, all_ref
 ):
-    core = core_ref[0]
-    half_ref[core] = mine_ref[...]
-    half_ref[1 - core] = got_ref[...]
-    for chunk in range(50):
-        tiles = half_ref[chunk // 25, chunk % 25].astype(F32)
-        for tile in range(3 * chunk, 3 * chunk + 3):
-            r, c, part = tile // 6, tile % 6, 8 * (tile % 3)
+    for chunk in range(30):
+        tiles = got_ref[chunk].astype(F32)
+        for tile in range(5 * chunk, 5 * chunk + 5):
+            r, c, part = tile // 6, tile % 6, 8 * (tile % 5)
             all_ref[8 * r : 8 * r + 8, 128 * c : 128 * c + 128] = tiles[part : part + 8]
     w_ref[...] = all_ref[0:CHAN, 0 : 3 * CHAN]
     p_ref[...] = all_ref[0:CHAN, 3 * CHAN : 4 * CHAN]
@@ -378,10 +365,6 @@
     return lax.ppermute(block, ROW + COL, pairs)
 
 
-SMALL = pl.BlockSpec(memory_space=pltpu.SMEM)
-WHOLE = pl.BlockSpec(memory_space=pltpu.VMEM)
-
-
 def prepare(*args):
     return kernel_call(
         prepare_kernel,
@@ -413,10 +396,8 @@
             shape((ROWS, COLS, CHAN)),
             shape((SHIFT, COLS, CHAN), BF),
             shape((CHUNKS, PACK, 128), BF),
-            shape((CHUNKS, PACK, 128), BF),
         ),
         [
-            pltpu.VMEM((2, CHUNKS, PACK, 128), BF),
             pltpu.VMEM((ROWS + 8, COLS + 8, CHAN), F32),
             pltpu.VMEM((tokens, CHAN), F32),
             pltpu.VMEM((tokens, 1), F32),
@@ -426,12 +407,7 @@
         + [pltpu.VMEM((8, TOK, HEADS * TOK), F32)] * 2
         + [pltpu.VMEM((8, TOK, HEADS * TOK), BF)] * 2,
         flops=10**9,
-        in_specs=[WHOLE] * (len(args) - 1) + [SMALL],
     )(*args)
-
-
-def pair_sum(mine, got):
-    return kernel_call(pair_kernel, shape(mine.shape, BF))(mine, got)
 
 
 def chunk_sum(got, copies, after):
@@ -445,7 +421,7 @@
     )(got, above, d_shifted)
 
 
-def unpack(mine, got, core):
+def unpack(got):
     return kernel_call(
         unpack_kernel,
         (
@@ -457,9 +433,8 @@
             shape((CHAN,)),
             shape((HEADS, TABLE)),
         ),
-        [pltpu.VMEM((2, CHUNKS, PACK, 128), BF), pltpu.VMEM((CHAN + 8, 4 * CHAN), F32)],
-        in_specs=[WHOLE, WHOLE, SMALL],
-    )(mine, got, core)
+        [pltpu.VMEM((CHAN + 8, 4 * CHAN), F32)],
+    )(got)
 
 
 def on_device(
@@ -475,20 +450,18 @@
     position_index,
 ):
     x, g = block_input[0], grad_out[0]
-    core = lax.axis_index("c").astype(jnp.int32)[None]
     col = moved(jnp.stack([x[:, :SHIFT], g[:, :SHIFT]]), COL, -1)
     row, corner = halos(x, g)
     row, corner = moved(row, ROW, -1), moved_corner(corner)
     bias, perm, apart, parts, rows = prepare(
         position_index, bias_table.T, region_ids, qkv_weight, layernorm_scale, layernorm_bias, qkv_bias
     )
-    d_shifted, edge, mine, other = main(
-        x, g, row, col, corner, parts, proj_weight, bias, perm, apart, rows, core
-    )
-    half = pair_sum(mine, lax.ppermute(other, "c", [(0, 1), (1, 0)]))
+    d_shifted, edge, packed = main(
+        x, g, row, col, corner, parts, proj_weight, bias, perm, apart, rows
+    )
     above = moved(edge, ROW, 1)
-    got = lax.all_to_all(half, FIRST, 0, 0, tiled=True)
-    part = chunk_sum(got, 8, above)
+    got = lax.all_to_all(packed, FIRST, 0, 0, tiled=True)
+    part = chunk_sum(got, 16, above)
     got = lax.all_to_all(part, SECOND, 0, 0, tiled=True)
     whole, edge = chunk_sum_edge(got, CHUNKS, above, d_shifted)
     left = moved(edge, COL, 1)
@@ -496,8 +469,7 @@
     back = jnp.concatenate([above.astype(F32), d_shifted[: ROWS - SHIFT]], axis=0)
     back = jnp.concatenate([left.astype(F32), back[:, : COLS - SHIFT]], axis=1)
     grad_x = (g.astype(F32) + back).astype(BF)[None]
-    other = lax.ppermute(gathered, "c", [(0, 1), (1, 0)])
-    w, wb, p, pb, ns, nb, table = unpack(gathered, other, core)
+    w, wb, p, pb, ns, nb, table = unpack(gathered)
     return (grad_x, w, wb, p, pb, ns, nb, table.T)
 
 

time: 92.9 us -> 89.2 us (0.960)
  starting transfers between devices: 49.1 us -> 39.3 us
  blocking collectives: 13.8 us -> 17.8 us
  waiting for transfers between devices: 17.5 us -> 19.2 us
    ppermute x2 -> x0, starting transfers between devices: 10.4 us -> none  [the longest x1 7.52 us: on_device(): other = lax.ppermute(gathered, 'c', [(0, 1), (1, 0)])]
    all_to_all x1, blocking collectives: 13.8 us -> 17.8 us  [on_device(): got = lax.all_to_all(part, SECOND, 0, 0, tiled=True)]
    all_to_all x1, waiting for transfers between devices: 7.28 us -> 8.77 us  [on_device(): got = lax.all_to_all(packed, FIRST, 0, 0, tiled=True)]
    ppermute x2 -> x0, waiting for transfers between devices: 1.28 us -> none  [the longest x1 1.05 us: on_device(): half = pair_sum(mine, lax.ppermute(other, 'c', [(0, 1), (1, 0)]))]
  transfers between devices with their start and end apart: 9 -> 7, of which waited for: 5 -> 4; matrix products, arithmetic and copies ran while one was open for 1% -> 1% of each run, Pallas kernels for 2% -> 2%
where the time goes in v4:
time: 89.2 us; the launch traced here: 88.3 us
  starting transfers between devices  39.3 us (44%)
  waiting for transfers between devices  19.2 us (22%)
  blocking collectives  17.8 us (20%)
  Pallas kernels  8.15 us (9%)
  local copies, waits for them, and re-layouts  1.99 us (2%)
  other arithmetic  0.93 us (1%)
  between operations  0.92 us (1%)
    ppermute x4, starting transfers between devices, moved(): lax.ppermute(block, axes, [((i - distance) % count, i) for i in range(cou...  21.4 us
    all_to_all x1, blocking collectives, on_device(): got = lax.all_to_all(part, SECOND, 0, 0, tiled=True)  17.8 us
    ppermute x4, waiting for transfers between devices, moved(): lax.ppermute(block, axes, [((i - distance) % count, i) for i in range(cou...  9.6 us
    all_to_all x1, waiting for transfers between devices, on_device(): got = lax.all_to_all(packed, FIRST, 0, 0, tiled=True)  8.77 us
    all_to_all x1, starting transfers between devices, on_device(): got = lax.all_to_all(packed, FIRST, 0, 0, tiled=True)  7.85 us
    ppermute x1, starting transfers between devices, moved_corner(): return lax.ppermute(block, ROW + COL, pairs)  5.35 us
    pallas_call x1, Pallas kernels, main(): kernel_call(main_kernel, (shape((ROWS, COLS, CHAN)), shape((SHIFT, COLS,...  4.76 us
    all_to_all x1, starting transfers between devices, on_device(): gathered = lax.all_to_all(whole, FIRST, 0, 0, tiled=True)  4.7 us
  transfers between devices with their start and end apart: 7, of which 4 were waited for; matrix products, arithmetic and copies ran while one was open for 1% of the time, Pallas kernels for 2%

profile of v4, /device:TPU:1, one launch (start us, length us, event | category | flops | bytes accessed | tf_op | source)
XLA Modules:
  0.0 88.3 jit_solution(11036494468910318344)
XLA Ops:
  0.6 0.0 copy-start
  0.6 0.9 %copy-done = bf16[1,16,32,192]{3,2,1,0:T(8,128)(2,1)S(1)} copy-done((bf16[1,16,32,192]{3,2,1,0:T(8,128)(2,1)S(1)}, bf16[1,16,32,192]{3,2,1,0:T(8,128)(2,1)}, u32[]{:S(2)}) %copy-start) | copy-done | bytes 196632
  1.6 0.0 copy-start.2
  1.6 0.9 %copy-done.2 = bf16[1,16,32,192]{3,2,1,0:T(8,128)(2,1)S(1)} copy-done((bf16[1,16,32,192]{3,2,1,0:T(8,128)(2,1)S(1)}, bf16[1,16,32,192]{3,2,1,0:T(8,128)(2,1)}, u32[]{:S(2)}) %copy-start.2) | copy-done | bytes 196632
  2.5 0.0 copy-start.4
  2.5 0.0 copy-start.5
  2.5 0.0 copy-start.6
  2.5 0.0 copy-start.7
  2.6 0.0 copy-start.8
  2.6 0.0 copy-start.9
  2.6 0.0 copy-start.10
  2.6 0.0 copy-start.11
  2.6 0.0 copy-start.1
  2.6 0.0 copy-start.3
  2.6 8.9 %collective-permute-start = (bf16[2,4,32,192]{3,2,1,0:T(8,128)(2,1)S(1)}, bf16[2,4,32,192]{3,2,1,0:T(8,128)(2,1)S(1)}, u32[]{:S(2)}, u32[]{:S(2)}) collective-permute-start(bf16[2,4,32,192]{3,2,1,0:T(8,128)(2,1)S(1)} %get-tuple-element.27), channel_id=1, source_target_pairs={{8,0},{16,8},{24,16},{32,24},{40,32},{48,40},{56,48},{0,56},{9,1},... | collective-permute-start | bytes 294920 | tf_op jit(solution)/shard_map/ppermute | solution.py:358
  11.6 0.1 pad_maximum_fusion.1
  11.7 7.5 %collective-permute-start.1 = (bf16[2,16,4,192]{3,2,1,0:T(4,128)(2,1)S(1)}, bf16[2,16,4,192]{3,2,1,0:T(4,128)(2,1)S(1)}, u32[]{:S(2)}, u32[]{:S(2)}) collective-permute-start(bf16[2,16,4,192]{3,2,1,0:T(4,128)(2,1)S(1)} %pad_maximum_fusion.1), channel_id=1, source_target_pairs={{1,0},{2,1},{3,2},{4,3},{5,4},{6,5},{7,6},{0,7},{9,8},{10,9},{11,1... | collective-permute-start | bytes 147464 | tf_op jit(solution)/shard_map/ppermute | solution.py:358
  19.1 5.4 %collective-permute-start.2 = (bf16[2,4,4,192]{3,2,1,0:T(4,128)(2,1)S(1)}, bf16[2,4,4,192]{3,2,1,0:T(4,128)(2,1)S(1)}, u32[]{:S(2)}, u32[]{:S(2)}) collective-permute-start(bf16[2,4,4,192]{3,2,1,0:T(4,128)(2,1)S(1)} %get-tuple-element.28), channel_id=1, source_target_pairs={{9,0},{10,1},{11,2},{12,3},{13,4},{14,5},{15,6},{8,7},{17,8},{18,9... | collective-permute-start | bytes 36872 | tf_op jit(solution)/shard_map/ppermute | solution.py:365
  24.5 0.0 copy-done.4
  24.5 0.0 copy-done.5
  24.5 0.0 copy-done.6
  24.5 0.0 copy-done.7
  24.5 0.0 copy-done.8
  24.5 0.0 copy-done.9
  24.5 0.0 copy-done.10
  24.6 1.6 %shard_map.162 = (f32[64,384]{1,0:T(8,128)S(1)}, bf16[256,256]{1,0:T(8,128)(2,1)S(1)}, f32[8,64,128]{2,1,0:T(8,128)S(1)}, bf16[3,192,192]{2,1,0:T(8,128)(2,1)S(1)}, f32[8,576]{1,0:T(8,128)S(1)}) custom-call(s32[64,64]{1,0:T(8,128)S(1)} %copy-done.5, f32[6,225]{1,0:T(8,128)S(1)} %bitcast.19, s32[16,32]{1,0:T(8,128)S(1)} %copy-done.7, ...), custom_call_target="tpu_custom_call" | custom-call | flops 10000000 | bytes 1000000 | tf_op jit(solution)/shard_map/pallas_call | solution.py:369
  26.2 0.0 collective-permute-done.2.corner_ref
  26.2 0.0 collective-permute-done.1.col_ref
  26.2 0.0 collective-permute-done.row_ref
  26.2 0.0 copy-done.11
  26.2 0.0 copy-done.1
  26.3 0.0 copy-done.3
  26.3 4.8 %shard_map.163 = (f32[16,32,192]{2,1,0:T(8,128)S(1)}, bf16[4,32,192]{2,1,0:T(8,128)(2,1)S(1)}, bf16[32,40,128]{2,1,0:T(8,128)(2,1)}) custom-call(bf16[16,32,192]{2,1,0:T(8,128)(2,1)S(1)} %bitcast.18, bf16[16,32,192]{2,1,0:T(8,128)(2,1)S(1)} %bitcast.15, bf16[2,4,32,192]{3,2,1,0:T(8,128)(2,1)S(1)} %collective-permute-done.row_ref, ...), custom_call_target="tpu_custom_call" | custom-call | flops 1000000000 | bytes 1000000 | tf_op jit(solution)/shard_map/pallas_call | solution.py:393
  31.0 7.8 %all-to-all-start = ((bf16[32,40,128]{2,1,0:T(8,128)(2,1)}), bf16[32,40,128]{2,1,0:T(8,128)(2,1)S(1)}, u32[]{:S(2)}, u32[]{:S(2)}) async-start(bf16[32,40,128]{2,1,0:T(8,128)(2,1)} %get-tuple-element.34), calls=%async_computation | async-start | bytes 655360 | tf_op jit(solution)/shard_map/all_to_all | solution.py:463
  38.9 1.9 %collective-permute-start.3 = (bf16[4,32,192]{2,1,0:T(8,128)(2,1)S(1)}, bf16[4,32,192]{2,1,0:T(8,128)(2,1)S(1)}, u32[]{:S(2)}, u32[]{:S(2)}) collective-permute-start(bf16[4,32,192]{2,1,0:T(8,128)(2,1)S(1)} %get-tuple-element.35), channel_id=1, source_target_pairs={{56,0},{0,8},{8,16},{16,24},{24,32},{32,40},{40,48},{48,56},{57,1}... | collective-permute-start | bytes 147464 | tf_op jit(solution)/shard_map/ppermute | solution.py:358
  40.8 1.9 %collective-permute-done.3.after_ref.above_ref = bf16[4,32,192]{2,1,0:T(8,128)(2,1)S(1)} collective-permute-done((bf16[4,32,192]{2,1,0:T(8,128)(2,1)S(1)}, bf16[4,32,192]{2,1,0:T(8,128)(2,1)S(1)}, u32[]{:S(2)}, u32[]{:S(2)}) %collective-permute-start.3) | collective-permute-done | bytes 49184 | tf_op jit(solution)/shard_map/ppermute | solution.py:358
  42.7 8.8 %all-to-all-done.got_ref = bf16[32,40,128]{2,1,0:T(8,128)(2,1)S(1)} async-done(((bf16[32,40,128]{2,1,0:T(8,128)(2,1)}), bf16[32,40,128]{2,1,0:T(8,128)(2,1)S(1)}, u32[]{:S(2)}, u32[]{:S(2)}) %all-to-all-start) | async-done | bytes 327712 | tf_op jit(solution)/shard_map/all_to_all | solution.py:463
  51.4 0.1 shard_map.164
  51.5 17.8 %all_to_all.15.got_ref = bf16[16,40,128]{2,1,0:T(8,128)(2,1)S(1)} all-to-all(bf16[16,40,128]{2,1,0:T(8,128)(2,1)S(1)} %shard_map.164), channel_id=1, replica_groups=mesh['y'=8,'zl'=4,'c'=2,'zh'=2,'x'=4] {'zl','c','zh'}, dimensions={0} | all-to-all | bytes 327680 | tf_op jit(solution)/shard_map/all_to_all | solution.py:465
  69.3 0.8 shard_map.165
  70.0 4.7 %all-to-all-start.2 = ((bf16[32,40,128]{2,1,0:T(8,128)(2,1)}), bf16[32,40,128]{2,1,0:T(8,128)(2,1)S(1)}, u32[]{:S(2)}, u32[]{:S(2)}) async-start(bf16[32,40,128]{2,1,0:T(8,128)(2,1)} %get-tuple-element.38), calls=%async_computation.2 | async-start | bytes 655360 | tf_op jit(solution)/shard_map/all_to_all | solution.py:468
  74.8 3.1 %collective-permute-start.4 = (bf16[16,4,192]{2,1,0:T(4,128)(2,1)S(1)}, bf16[16,4,192]{2,1,0:T(4,128)(2,1)S(1)}, u32[]{:S(2)}, u32[]{:S(2)}) collective-permute-start(bf16[16,4,192]{2,1,0:T(4,128)(2,1)S(1)} %get-tuple-element.37), channel_id=1, source_target_pairs={{7,0},{0,1},{1,2},{2,3},{3,4},{4,5},{5,6},{6,7},{15,8},{8,9},{9,10... | collective-permute-start | bytes 73736 | tf_op jit(solution)/shard_map/ppermute | solution.py:358
  78.0 7.7 %collective-permute-done.4 = bf16[16,4,192]{2,1,0:T(4,128)(2,1)S(1)} collective-permute-done((bf16[16,4,192]{2,1,0:T(4,128)(2,1)S(1)}, bf16[16,4,192]{2,1,0:T(4,128)(2,1)S(1)}, u32[]{:S(2)}, u32[]{:S(2)}) %collective-permute-start.4) | collective-permute-done | bytes 24608 | tf_op jit(solution)/shard_map/ppermute | solution.py:358
  85.7 0.8 fusion.1
  86.6 0.8 all-to-all-done.2.got_ref
  87.4 0.9 %shard_map.166 = (f32[192,576]{1,0:T(8,128)}, f32[576]{0:T(1024)}, f32[192,192]{1,0:T(8,128)}, f32[192]{0:T(256)}, f32[192]{0:T(256)}, /*index=5*/f32[192]{0:T(256)}, f32[6,225]{1,0:T(8,128)}) custom-call(bf16[32,40,128]{2,1,0:T(8,128)(2,1)S(1)} %all-to-all-done.2.got_ref), custom_call_target="tpu_custom_call" | custom-call | flops 10000000 | bytes 1000000 | tf_op jit(solution)/shard_map/pallas_call | solution.py:425
  (6 shorter events, 0.1 us)
Async XLA Ops:
  0.6 1.0 %copy-start = (bf16[1,16,32,192]{3,2,1,0:T(8,128)(2,1)S(1)}, bf16[1,16,32,192]{3,2,1,0:T(8,128)(2,1)}, u32[]{:S(2)}) copy-start(bf16[1,16,32,192]{3,2,1,0:T(8,128)(2,1)} %param.11) | copy-start | bytes 589828
  1.6 0.9 %copy-start.2 = (bf16[1,16,32,192]{3,2,1,0:T(8,128)(2,1)S(1)}, bf16[1,16,32,192]{3,2,1,0:T(8,128)(2,1)}, u32[]{:S(2)}) copy-start(bf16[1,16,32,192]{3,2,1,0:T(8,128)(2,1)} %param.10) | copy-start | bytes 589828
  2.5 21.9 %copy-start.4 = (bf16[192,576]{1,0:T(8,128)(2,1)S(1)}, bf16[192,576]{1,0:T(8,128)(2,1)}, u32[]{:S(2)}) copy-start(bf16[192,576]{1,0:T(8,128)(2,1)} %w_ref.1) | copy-start | bytes 663556
  2.5 22.0 %copy-start.5 = (s32[64,64]{1,0:T(8,128)S(1)}, s32[64,64]{1,0:T(8,128)}, u32[]{:S(2)}) copy-start(s32[64,64]{1,0:T(8,128)} %pos_ref.1) | copy-start | bytes 49156
  2.5 22.0 %copy-start.6 = (f32[225,6]{0,1:T(8,128)S(1)}, f32[225,6]{0,1:T(8,128)}, u32[]{:S(2)}) copy-start(f32[225,6]{0,1:T(8,128)} %param.18) | copy-start | bytes 16204
  2.5 22.0 %copy-start.7 = (s32[16,32]{1,0:T(8,128)S(1)}, s32[16,32]{1,0:T(8,128)}, u32[]{:S(2)}) copy-start(s32[16,32]{1,0:T(8,128)} %ids_ref.1) | copy-start | bytes 6148
  2.6 22.0 %copy-start.8 = (f32[576]{0:T(1024)S(1)}, f32[576]{0:T(1024)}, u32[]{:S(2)}) copy-start(f32[576]{0:T(1024)} %qb_ref.1) | copy-start | bytes 6916
  2.6 22.0 %copy-start.9 = (f32[192]{0:T(256)S(1)}, f32[192]{0:T(256)}, u32[]{:S(2)}) copy-start(f32[192]{0:T(256)} %ls_ref.1) | copy-start | bytes 2308
  2.6 22.0 %copy-start.10 = (f32[192]{0:T(256)S(1)}, f32[192]{0:T(256)}, u32[]{:S(2)}) copy-start(f32[192]{0:T(256)} %lb_ref.1) | copy-start | bytes 2308
  2.6 23.7 %copy-start.11 = (bf16[192,192]{1,0:T(8,128)(2,1)S(1)}, bf16[192,192]{1,0:T(8,128)(2,1)}, u32[]{:S(2)}) copy-start(bf16[192,192]{1,0:T(8,128)(2,1)} %wp_ref.1) | copy-start | bytes 221188
  2.6 23.6 %copy-start.1 = (bf16[1,16,32,192]{3,2,1,0:T(8,128)(2,1)S(1)}, bf16[1,16,32,192]{3,2,1,0:T(8,128)(2,1)}, u32[]{:S(2)}) copy-start(bf16[1,16,32,192]{3,2,1,0:T(8,128)(2,1)} %param.11) | copy-start | bytes 589828
  2.6 23.6 %copy-start.3 = (bf16[1,16,32,192]{3,2,1,0:T(8,128)(2,1)S(1)}, bf16[1,16,32,192]{3,2,1,0:T(8,128)(2,1)}, u32[]{:S(2)}) copy-start(bf16[1,16,32,192]{3,2,1,0:T(8,128)(2,1)} %param.10) | copy-start | bytes 589828
  2.6 23.6 %collective-permute-start = (bf16[2,4,32,192]{3,2,1,0:T(8,128)(2,1)S(1)}, bf16[2,4,32,192]{3,2,1,0:T(8,128)(2,1)S(1)}, u32[]{:S(2)}, u32[]{:S(2)}) collective-permute-start(bf16[2,4,32,192]{3,2,1,0:T(8,128)(2,1)S(1)} %get-tuple-element.27), channel_id=1, source_target_pairs={{8,0},{16,8},{24,16},{32,24},{40,32},{48,40},{56,48},{0,56},{9,1},... | collective-permute-start | bytes 294920 | tf_op jit(solution)/shard_map/ppermute | solution.py:358
  11.7 14.6 %collective-permute-start.1 = (bf16[2,16,4,192]{3,2,1,0:T(4,128)(2,1)S(1)}, bf16[2,16,4,192]{3,2,1,0:T(4,128)(2,1)S(1)}, u32[]{:S(2)}, u32[]{:S(2)}) collective-permute-start(bf16[2,16,4,192]{3,2,1,0:T(4,128)(2,1)S(1)} %pad_maximum_fusion.1), channel_id=1, source_target_pairs={{1,0},{2,1},{3,2},{4,3},{5,4},{6,5},{7,6},{0,7},{9,8},{10,9},{11,1... | collective-permute-start | bytes 147464 | tf_op jit(solution)/shard_map/ppermute | solution.py:358
  19.1 7.1 %collective-permute-start.2 = (bf16[2,4,4,192]{3,2,1,0:T(4,128)(2,1)S(1)}, bf16[2,4,4,192]{3,2,1,0:T(4,128)(2,1)S(1)}, u32[]{:S(2)}, u32[]{:S(2)}) collective-permute-start(bf16[2,4,4,192]{3,2,1,0:T(4,128)(2,1)S(1)} %get-tuple-element.28), channel_id=1, source_target_pairs={{9,0},{10,1},{11,2},{12,3},{13,4},{14,5},{15,6},{8,7},{17,8},{18,9... | collective-permute-start | bytes 36872 | tf_op jit(solution)/shard_map/ppermute | solution.py:365
  31.0 20.4 %all-to-all-start = ((bf16[32,40,128]{2,1,0:T(8,128)(2,1)}), bf16[32,40,128]{2,1,0:T(8,128)(2,1)S(1)}, u32[]{:S(2)}, u32[]{:S(2)}) async-start(bf16[32,40,128]{2,1,0:T(8,128)(2,1)} %get-tuple-element.34), calls=%async_computation | async-start | bytes 655360 | tf_op jit(solution)/shard_map/all_to_all | solution.py:463
  38.9 3.8 %collective-permute-start.3 = (bf16[4,32,192]{2,1,0:T(8,128)(2,1)S(1)}, bf16[4,32,192]{2,1,0:T(8,128)(2,1)S(1)}, u32[]{:S(2)}, u32[]{:S(2)}) collective-permute-start(bf16[4,32,192]{2,1,0:T(8,128)(2,1)S(1)} %get-tuple-element.35), channel_id=1, source_target_pairs={{56,0},{0,8},{8,16},{16,24},{24,32},{32,40},{40,48},{48,56},{57,1}... | collective-permute-start | bytes 147464 | tf_op jit(solution)/shard_map/ppermute | solution.py:358
  70.0 17.3 %all-to-all-start.2 = ((bf16[32,40,128]{2,1,0:T(8,128)(2,1)}), bf16[32,40,128]{2,1,0:T(8,128)(2,1)S(1)}, u32[]{:S(2)}, u32[]{:S(2)}) async-start(bf16[32,40,128]{2,1,0:T(8,128)(2,1)} %get-tuple-element.38), calls=%async_computation.2 | async-start | bytes 655360 | tf_op jit(solution)/shard_map/all_to_all | solution.py:468
  74.8 10.9 %collective-permute-start.4 = (bf16[16,4,192]{2,1,0:T(4,128)(2,1)S(1)}, bf16[16,4,192]{2,1,0:T(4,128)(2,1)S(1)}, u32[]{:S(2)}, u32[]{:S(2)}) collective-permute-start(bf16[16,4,192]{2,1,0:T(4,128)(2,1)S(1)} %get-tuple-element.37), channel_id=1, source_target_pairs={{7,0},{0,1},{1,2},{2,3},{3,4},{4,5},{5,6},{6,7},{15,8},{8,9},{9,10... | collective-permute-start | bytes 73736 | tf_op jit(solution)/shard_map/ppermute | solution.py:358

commit v5 on v4

--- a/solution.py
+++ b/solution.py
@@ -153,7 +153,6 @@
     apart_ref,
     rows_ref,
     ds_ref,
-    edge_ref,
     pack_ref,
     ext_ref,
     xhat_ref,
@@ -268,7 +267,6 @@
         wr, wc = win // 4, win % 4
         block = d_shifted[TOK * win : TOK * win + TOK].reshape(WIN, WIN, CHAN)
         ds_ref[WIN * wr : WIN * wr + WIN, WIN * wc : WIN * wc + WIN, :] = block
-    edge_ref[...] = ds_ref[ROWS - SHIFT : ROWS].astype(BF)
 
     normed = normed_ref[...].T
     weights = jnp.concatenate(
@@ -303,14 +301,27 @@
     return total
 
 
-def sum_kernel(got_ref, after_ref, out_ref):
-    total = add_up(got_ref, got_ref.shape[0]).astype(BF)
+def part_sum(got_ref, place_ref):
+    total = add_up(got_ref, got_ref.shape[0])
+    tiles = []
+    for i in range(PACK // 8):
+        tile = total[8 * i : 8 * i + 8]
+        whole = tile + pltpu.roll(tile, 4, 0)
+        high = whole.astype(BF).astype(F32)
+        parts = jnp.where(iota((8, 128), 0) < 4, high, whole - high)
+        tiles.append(jnp.where(place_ref[0] * (PACK // 8) + i >= 6 * CHAN // 8, parts, tile))
+    return jnp.concatenate(tiles, axis=0).astype(BF)
+
+
+def sum_kernel(got_ref, ds_ref, place_ref, out_ref, edge_ref):
+    total = part_sum(got_ref, place_ref)
     for i in range(out_ref.shape[0]):
         out_ref[i] = total
-
-
-def sum_edge_kernel(got_ref, above_ref, ds_ref, out_ref, edge_ref):
-    total = add_up(got_ref, got_ref.shape[0]).astype(BF)
+    edge_ref[...] = ds_ref[ROWS - SHIFT : ROWS].astype(BF)
+
+
+def sum_edge_kernel(got_ref, above_ref, ds_ref, place_ref, out_ref, edge_ref):
+    total = part_sum(got_ref, place_ref)
     for i in range(out_ref.shape[0]):
         out_ref[i] = total
     edge_ref[0:SHIFT] = above_ref[:, COLS - SHIFT : COLS]
@@ -394,7 +405,6 @@
         main_kernel,
         (
             shape((ROWS, COLS, CHAN)),
-            shape((SHIFT, COLS, CHAN), BF),
             shape((CHUNKS, PACK, 128), BF),
         ),
         [
@@ -410,15 +420,24 @@
     )(*args)
 
 
-def chunk_sum(got, copies, after):
-    return kernel_call(sum_kernel, shape((copies,) + got.shape[1:], BF))(got, after)
-
-
-def chunk_sum_edge(got, copies, above, d_shifted):
+SMALL = pl.BlockSpec(memory_space=pltpu.SMEM)
+WHOLE = pl.BlockSpec(memory_space=pltpu.VMEM)
+
+
+def chunk_sum(got, copies, d_shifted, place):
+    return kernel_call(
+        sum_kernel,
+        (shape((copies,) + got.shape[1:], BF), shape((SHIFT, COLS, CHAN), BF)),
+        in_specs=[WHOLE, WHOLE, SMALL],
+    )(got, d_shifted, place)
+
+
+def chunk_sum_edge(got, copies, above, d_shifted, place):
     return kernel_call(
         sum_edge_kernel,
         (shape((copies,) + got.shape[1:], BF), shape((ROWS, SHIFT, CHAN), BF)),
-    )(got, above, d_shifted)
+        in_specs=[WHOLE, WHOLE, WHOLE, SMALL],
+    )(got, above, d_shifted, place)
 
 
 def unpack(got):
@@ -456,14 +475,16 @@
     bias, perm, apart, parts, rows = prepare(
         position_index, bias_table.T, region_ids, qkv_weight, layernorm_scale, layernorm_bias, qkv_bias
     )
-    d_shifted, edge, packed = main(
+    place = lax.axis_index(FIRST).astype(jnp.int32)[None]
+    rows, place = lax.optimization_barrier((rows, place))
+    d_shifted, packed = main(
         x, g, row, col, corner, parts, proj_weight, bias, perm, apart, rows
     )
+    got = lax.all_to_all(packed, FIRST, 0, 0, tiled=True)
+    part, edge = chunk_sum(got, 16, d_shifted, place)
     above = moved(edge, ROW, 1)
-    got = lax.all_to_all(packed, FIRST, 0, 0, tiled=True)
-    part = chunk_sum(got, 16, above)
     got = lax.all_to_all(part, SECOND, 0, 0, tiled=True)
-    whole, edge = chunk_sum_edge(got, CHUNKS, above, d_shifted)
+    whole, edge = chunk_sum_edge(got, CHUNKS, above, d_shifted, place)
     left = moved(edge, COL, 1)
     gathered = lax.all_to_all(whole, FIRST, 0, 0, tiled=True)
     back = jnp.concatenate([above.astype(F32), d_shifted[: ROWS - SHIFT]], axis=0)

time: 89.2 us -> 88.7 us (level)
  waiting for transfers between devices: 19.2 us -> 14.7 us
  blocking collectives: 17.8 us -> 20.2 us
  starting transfers between devices: 39.3 us -> 40.6 us
    all_to_all x1, waiting for transfers between devices: 8.77 us -> 4.21 us  [on_device(): got = lax.all_to_all(part, SECOND, 0, 0, tiled=True)]
    all_to_all x1, blocking collectives: 17.8 us -> 20.2 us  [on_device(): got = lax.all_to_all(packed, FIRST, 0, 0, tiled=True)]
    ppermute x4, starting transfers between devices: 21.4 us -> 23.1 us  [moved(): lax.ppermute(block, axes, [((i - distance) % count, i) for i in range(cou...]
where the time goes in v5:
time: 88.7 us; the launch traced here: 87.5 us
  starting transfers between devices  40.6 us (46%)
  blocking collectives  20.2 us (23%)
  waiting for transfers between devices  14.7 us (17%)
  Pallas kernels  8.1 us (9%)
  local copies, waits for them, and re-layouts  1.99 us (2%)
  other arithmetic  0.93 us (1%)
  between operations  0.92 us (1%)
    ppermute x4, starting transfers between devices, moved(): lax.ppermute(block, axes, [((i - distance) % count, i) for i in range(cou...  23.1 us
    all_to_all x1, blocking collectives, on_device(): got = lax.all_to_all(packed, FIRST, 0, 0, tiled=True)  20.2 us
    ppermute x4, waiting for transfers between devices, moved(): lax.ppermute(block, axes, [((i - distance) % count, i) for i in range(cou...  10.2 us
    all_to_all x1, starting transfers between devices, on_device(): got = lax.all_to_all(part, SECOND, 0, 0, tiled=True)  8.34 us
    ppermute x1, starting transfers between devices, moved_corner(): return lax.ppermute(block, ROW + COL, pairs)  5.35 us
    all_to_all x1, waiting for transfers between devices, on_device(): got = lax.all_to_all(part, SECOND, 0, 0, tiled=True)  4.21 us
    pallas_call x1, Pallas kernels, main(): kernel_call(main_kernel, (shape((ROWS, COLS, CHAN)), shape((CHUNKS, PACK,...  4.02 us
    all_to_all x1, starting transfers between devices, on_device(): gathered = lax.all_to_all(whole, FIRST, 0, 0, tiled=True)  3.87 us
  transfers between devices with their start and end apart: 7, of which 4 were waited for; matrix products, arithmetic and copies ran while one was open for 1% of the time, Pallas kernels for 2%

profile of v5, /device:TPU:1, one launch (start us, length us, event | category | flops | bytes accessed | tf_op | source)
XLA Modules:
  0.0 87.5 jit_solution(13248626484866766335)
XLA Ops:
  0.6 0.0 copy-start
  0.6 0.9 %copy-done = bf16[1,16,32,192]{3,2,1,0:T(8,128)(2,1)S(1)} copy-done((bf16[1,16,32,192]{3,2,1,0:T(8,128)(2,1)S(1)}, bf16[1,16,32,192]{3,2,1,0:T(8,128)(2,1)}, u32[]{:S(2)}) %copy-start) | copy-done | bytes 196632
  1.6 0.0 copy-start.2
  1.6 0.9 %copy-done.2 = bf16[1,16,32,192]{3,2,1,0:T(8,128)(2,1)S(1)} copy-done((bf16[1,16,32,192]{3,2,1,0:T(8,128)(2,1)S(1)}, bf16[1,16,32,192]{3,2,1,0:T(8,128)(2,1)}, u32[]{:S(2)}) %copy-start.2) | copy-done | bytes 196632
  2.5 0.0 copy-start.4
  2.5 0.0 copy-start.6
  2.5 0.0 copy-start.7
  2.5 0.0 copy-start.8
  2.6 0.0 copy-start.9
  2.6 0.0 copy-start.10
  2.6 0.0 copy-start.11
  2.6 0.0 copy-start.5
  2.6 8.9 %collective-permute-start = (bf16[2,4,32,192]{3,2,1,0:T(8,128)(2,1)S(1)}, bf16[2,4,32,192]{3,2,1,0:T(8,128)(2,1)S(1)}, u32[]{:S(2)}, u32[]{:S(2)}) collective-permute-start(bf16[2,4,32,192]{3,2,1,0:T(8,128)(2,1)S(1)} %get-tuple-element.30), channel_id=1, source_target_pairs={{8,0},{16,8},{24,16},{32,24},{40,32},{48,40},{56,48},{0,56},{9,1},... | collective-permute-start | bytes 294920 | tf_op jit(solution)/shard_map/ppermute | solution.py:369
  11.5 0.0 copy-start.3
  11.6 0.0 copy-start.1
  11.6 0.1 pad_maximum_fusion.1
  11.7 7.6 %collective-permute-start.1 = (bf16[2,16,4,192]{3,2,1,0:T(4,128)(2,1)S(1)}, bf16[2,16,4,192]{3,2,1,0:T(4,128)(2,1)S(1)}, u32[]{:S(2)}, u32[]{:S(2)}) collective-permute-start(bf16[2,16,4,192]{3,2,1,0:T(4,128)(2,1)S(1)} %pad_maximum_fusion.1), channel_id=1, source_target_pairs={{1,0},{2,1},{3,2},{4,3},{5,4},{6,5},{7,6},{0,7},{9,8},{10,9},{11,1... | collective-permute-start | bytes 147464 | tf_op jit(solution)/shard_map/ppermute | solution.py:369
  19.3 5.4 %collective-permute-start.2 = (bf16[2,4,4,192]{3,2,1,0:T(4,128)(2,1)S(1)}, bf16[2,4,4,192]{3,2,1,0:T(4,128)(2,1)S(1)}, u32[]{:S(2)}, u32[]{:S(2)}) collective-permute-start(bf16[2,4,4,192]{3,2,1,0:T(4,128)(2,1)S(1)} %get-tuple-element.31), channel_id=1, source_target_pairs={{9,0},{10,1},{11,2},{12,3},{13,4},{14,5},{15,6},{8,7},{17,8},{18,9... | collective-permute-start | bytes 36872 | tf_op jit(solution)/shard_map/ppermute | solution.py:376
  24.6 0.0 copy-done.4
  24.6 0.0 copy-done.6
  24.6 0.0 copy-done.7
  24.7 0.0 copy-done.8
  24.7 0.0 copy-done.9
  24.7 0.0 copy-done.10
  24.7 0.0 copy-done.5
  24.7 1.6 %shard_map.162 = (f32[64,384]{1,0:T(8,128)S(1)}, bf16[256,256]{1,0:T(8,128)(2,1)S(1)}, f32[8,64,128]{2,1,0:T(8,128)S(1)}, bf16[3,192,192]{2,1,0:T(8,128)(2,1)S(1)}, f32[8,576]{1,0:T(8,128)S(1)}) custom-call(s32[64,64]{1,0:T(8,128)S(1)} %copy-done.5, f32[6,225]{1,0:T(8,128)S(1)} %bitcast.20, s32[16,32]{1,0:T(8,128)S(1)} %copy-done.7, ...), custom_call_target="tpu_custom_call" | custom-call | flops 10000000 | bytes 1000000 | tf_op jit(solution)/shard_map/pallas_call | solution.py:380
  26.3 0.0 collective-permute-done.2.corner_ref
  26.4 0.0 collective-permute-done.1.col_ref
  26.4 0.0 collective-permute-done.row_ref
  26.4 0.0 copy-done.11
  26.4 0.0 copy-done.3
  26.4 0.0 copy-done.1
  26.4 4.0 %shard_map.163 = (f32[16,32,192]{2,1,0:T(8,128)S(1)}, bf16[32,40,128]{2,1,0:T(8,128)(2,1)S(1)}) custom-call(bf16[16,32,192]{2,1,0:T(8,128)(2,1)S(1)} %bitcast.19, bf16[16,32,192]{2,1,0:T(8,128)(2,1)S(1)} %bitcast.16, bf16[2,4,32,192]{3,2,1,0:T(8,128)(2,1)S(1)} %collective-permute-done.row_ref, bf16[2,16,4,192]{3,2,1,0:T(4,128)(2,1)S(1)} %collective-permute-done.1.col_ref, ...), custom_call_target="tpu_custom_call" | custom-call | flops 1000000000 | bytes 1000000 | tf_op jit(solution)/shard_map/pallas_call | solution.py:404
  30.4 20.2 %all_to_all.15.got_ref = bf16[32,40,128]{2,1,0:T(8,128)(2,1)S(1)} all-to-all(bf16[32,40,128]{2,1,0:T(8,128)(2,1)S(1)} %get-tuple-element.38), channel_id=1, replica_groups=mesh['y'=8,'zl'=4,'c'=2,'zh'=2,'x'=4] {'y','x'}, dimensions={0} | all-to-all | bytes 655360 | tf_op jit(solution)/shard_map/all_to_all | solution.py:483
  50.7 0.7 shard_map.164
  51.4 8.3 %all-to-all-start.1 = ((bf16[16,40,128]{2,1,0:T(8,128)(2,1)}), bf16[16,40,128]{2,1,0:T(8,128)(2,1)S(1)}, u32[]{:S(2)}, u32[]{:S(2)}) async-start(bf16[16,40,128]{2,1,0:T(8,128)(2,1)} %get-tuple-element.41), calls=%async_computation.1 | async-start | bytes 327680 | tf_op jit(solution)/shard_map/all_to_all | solution.py:486
  59.7 3.5 %collective-permute-start.3 = (bf16[4,32,192]{2,1,0:T(8,128)(2,1)S(1)}, bf16[4,32,192]{2,1,0:T(8,128)(2,1)S(1)}, u32[]{:S(2)}, u32[]{:S(2)}) collective-permute-start(bf16[4,32,192]{2,1,0:T(8,128)(2,1)S(1)} %get-tuple-element.42), channel_id=1, source_target_pairs={{56,0},{0,8},{8,16},{16,24},{24,32},{32,40},{40,48},{48,56},{57,1}... | collective-permute-start | bytes 147464 | tf_op jit(solution)/shard_map/ppermute | solution.py:369
  63.3 2.1 %collective-permute-done.3.above_ref = bf16[4,32,192]{2,1,0:T(8,128)(2,1)S(1)} collective-permute-done((bf16[4,32,192]{2,1,0:T(8,128)(2,1)S(1)}, bf16[4,32,192]{2,1,0:T(8,128)(2,1)S(1)}, u32[]{:S(2)}, u32[]{:S(2)}) %collective-permute-start.3) | collective-permute-done | bytes 49184 | tf_op jit(solution)/shard_map/ppermute | solution.py:369
  65.3 4.2 %all-to-all-done.1.got_ref = bf16[16,40,128]{2,1,0:T(8,128)(2,1)S(1)} async-done(((bf16[16,40,128]{2,1,0:T(8,128)(2,1)}), bf16[16,40,128]{2,1,0:T(8,128)(2,1)S(1)}, u32[]{:S(2)}, u32[]{:S(2)}) %all-to-all-start.1) | async-done | bytes 163872 | tf_op jit(solution)/shard_map/all_to_all | solution.py:486
  69.5 0.8 shard_map.165
  70.3 3.9 %all-to-all-start.2 = ((bf16[32,40,128]{2,1,0:T(8,128)(2,1)}), bf16[32,40,128]{2,1,0:T(8,128)(2,1)S(1)}, u32[]{:S(2)}, u32[]{:S(2)}) async-start(bf16[32,40,128]{2,1,0:T(8,128)(2,1)} %get-tuple-element.44), calls=%async_computation.2 | async-start | bytes 655360 | tf_op jit(solution)/shard_map/all_to_all | solution.py:489
  74.2 3.0 %collective-permute-start.4 = (bf16[16,4,192]{2,1,0:T(4,128)(2,1)S(1)}, bf16[16,4,192]{2,1,0:T(4,128)(2,1)S(1)}, u32[]{:S(2)}, u32[]{:S(2)}) collective-permute-start(bf16[16,4,192]{2,1,0:T(4,128)(2,1)S(1)} %get-tuple-element.43), channel_id=1, source_target_pairs={{7,0},{0,1},{1,2},{2,3},{3,4},{4,5},{5,6},{6,7},{15,8},{8,9},{9,10... | collective-permute-start | bytes 73736 | tf_op jit(solution)/shard_map/ppermute | solution.py:369
  77.3 8.1 %collective-permute-done.4 = bf16[16,4,192]{2,1,0:T(4,128)(2,1)S(1)} collective-permute-done((bf16[16,4,192]{2,1,0:T(4,128)(2,1)S(1)}, bf16[16,4,192]{2,1,0:T(4,128)(2,1)S(1)}, u32[]{:S(2)}, u32[]{:S(2)}) %collective-permute-start.4) | collective-permute-done | bytes 24608 | tf_op jit(solution)/shard_map/ppermute | solution.py:369
  85.5 0.8 fusion.1
  86.3 0.3 all-to-all-done.2.got_ref
  86.6 0.9 %shard_map.166 = (f32[192,576]{1,0:T(8,128)}, f32[576]{0:T(1024)}, f32[192,192]{1,0:T(8,128)}, f32[192]{0:T(256)}, f32[192]{0:T(256)}, /*index=5*/f32[192]{0:T(256)}, f32[6,225]{1,0:T(8,128)}) custom-call(bf16[32,40,128]{2,1,0:T(8,128)(2,1)S(1)} %all-to-all-done.2.got_ref), custom_call_target="tpu_custom_call" | custom-call | flops 10000000 | bytes 1000000 | tf_op jit(solution)/shard_map/pallas_call | solution.py:444
  (6 shorter events, 0.1 us)
Async XLA Ops:
  0.6 1.0 %copy-start = (bf16[1,16,32,192]{3,2,1,0:T(8,128)(2,1)S(1)}, bf16[1,16,32,192]{3,2,1,0:T(8,128)(2,1)}, u32[]{:S(2)}) copy-start(bf16[1,16,32,192]{3,2,1,0:T(8,128)(2,1)} %param.11) | copy-start | bytes 589828
  1.6 0.9 %copy-start.2 = (bf16[1,16,32,192]{3,2,1,0:T(8,128)(2,1)S(1)}, bf16[1,16,32,192]{3,2,1,0:T(8,128)(2,1)}, u32[]{:S(2)}) copy-start(bf16[1,16,32,192]{3,2,1,0:T(8,128)(2,1)} %param.10) | copy-start | bytes 589828
  2.5 22.1 %copy-start.4 = (bf16[192,576]{1,0:T(8,128)(2,1)S(1)}, bf16[192,576]{1,0:T(8,128)(2,1)}, u32[]{:S(2)}) copy-start(bf16[192,576]{1,0:T(8,128)(2,1)} %w_ref.1) | copy-start | bytes 663556
  2.5 22.1 %copy-start.6 = (f32[225,6]{0,1:T(8,128)S(1)}, f32[225,6]{0,1:T(8,128)}, u32[]{:S(2)}) copy-start(f32[225,6]{0,1:T(8,128)} %param.18) | copy-start | bytes 16204
  2.5 22.1 %copy-start.7 = (s32[16,32]{1,0:T(8,128)S(1)}, s32[16,32]{1,0:T(8,128)}, u32[]{:S(2)}) copy-start(s32[16,32]{1,0:T(8,128)} %ids_ref.1) | copy-start | bytes 6148
  2.5 22.1 %copy-start.8 = (f32[576]{0:T(1024)S(1)}, f32[576]{0:T(1024)}, u32[]{:S(2)}) copy-start(f32[576]{0:T(1024)} %qb_ref.1) | copy-start | bytes 6916
  2.6 22.1 %copy-start.9 = (f32[192]{0:T(256)S(1)}, f32[192]{0:T(256)}, u32[]{:S(2)}) copy-start(f32[192]{0:T(256)} %ls_ref.1) | copy-start | bytes 2308
  2.6 22.1 %copy-start.10 = (f32[192]{0:T(256)S(1)}, f32[192]{0:T(256)}, u32[]{:S(2)}) copy-start(f32[192]{0:T(256)} %lb_ref.1) | copy-start | bytes 2308
  2.6 23.8 %copy-start.11 = (bf16[192,192]{1,0:T(8,128)(2,1)S(1)}, bf16[192,192]{1,0:T(8,128)(2,1)}, u32[]{:S(2)}) copy-start(bf16[192,192]{1,0:T(8,128)(2,1)} %wp_ref.1) | copy-start | bytes 221188
  2.6 22.1 %copy-start.5 = (s32[64,64]{1,0:T(8,128)S(1)}, s32[64,64]{1,0:T(8,128)}, u32[]{:S(2)}) copy-start(s32[64,64]{1,0:T(8,128)} %pos_ref.1) | copy-start | bytes 49156
  2.6 23.8 %collective-permute-start = (bf16[2,4,32,192]{3,2,1,0:T(8,128)(2,1)S(1)}, bf16[2,4,32,192]{3,2,1,0:T(8,128)(2,1)S(1)}, u32[]{:S(2)}, u32[]{:S(2)}) collective-permute-start(bf16[2,4,32,192]{3,2,1,0:T(8,128)(2,1)S(1)} %get-tuple-element.30), channel_id=1, source_target_pairs={{8,0},{16,8},{24,16},{32,24},{40,32},{48,40},{56,48},{0,56},{9,1},... | collective-permute-start | bytes 294920 | tf_op jit(solution)/shard_map/ppermute | solution.py:369
  11.5 14.8 %copy-start.3 = (bf16[1,16,32,192]{3,2,1,0:T(8,128)(2,1)S(1)}, bf16[1,16,32,192]{3,2,1,0:T(8,128)(2,1)}, u32[]{:S(2)}) copy-start(bf16[1,16,32,192]{3,2,1,0:T(8,128)(2,1)} %param.10) | copy-start | bytes 589828
  11.6 14.8 %copy-start.1 = (bf16[1,16,32,192]{3,2,1,0:T(8,128)(2,1)S(1)}, bf16[1,16,32,192]{3,2,1,0:T(8,128)(2,1)}, u32[]{:S(2)}) copy-start(bf16[1,16,32,192]{3,2,1,0:T(8,128)(2,1)} %param.11) | copy-start | bytes 589828
  11.7 14.7 %collective-permute-start.1 = (bf16[2,16,4,192]{3,2,1,0:T(4,128)(2,1)S(1)}, bf16[2,16,4,192]{3,2,1,0:T(4,128)(2,1)S(1)}, u32[]{:S(2)}, u32[]{:S(2)}) collective-permute-start(bf16[2,16,4,192]{3,2,1,0:T(4,128)(2,1)S(1)} %pad_maximum_fusion.1), channel_id=1, source_target_pairs={{1,0},{2,1},{3,2},{4,3},{5,4},{6,5},{7,6},{0,7},{9,8},{10,9},{11,1... | collective-permute-start | bytes 147464 | tf_op jit(solution)/shard_map/ppermute | solution.py:369
  19.3 7.1 %collective-permute-start.2 = (bf16[2,4,4,192]{3,2,1,0:T(4,128)(2,1)S(1)}, bf16[2,4,4,192]{3,2,1,0:T(4,128)(2,1)S(1)}, u32[]{:S(2)}, u32[]{:S(2)}) collective-permute-start(bf16[2,4,4,192]{3,2,1,0:T(4,128)(2,1)S(1)} %get-tuple-element.31), channel_id=1, source_target_pairs={{9,0},{10,1},{11,2},{12,3},{13,4},{14,5},{15,6},{8,7},{17,8},{18,9... | collective-permute-start | bytes 36872 | tf_op jit(solution)/shard_map/ppermute | solution.py:376
  51.4 18.1 %all-to-all-start.1 = ((bf16[16,40,128]{2,1,0:T(8,128)(2,1)}), bf16[16,40,128]{2,1,0:T(8,128)(2,1)S(1)}, u32[]{:S(2)}, u32[]{:S(2)}) async-start(bf16[16,40,128]{2,1,0:T(8,128)(2,1)} %get-tuple-element.41), calls=%async_computation.1 | async-start | bytes 327680 | tf_op jit(solution)/shard_map/all_to_all | solution.py:486
  59.7 5.6 %collective-permute-start.3 = (bf16[4,32,192]{2,1,0:T(8,128)(2,1)S(1)}, bf16[4,32,192]{2,1,0:T(8,128)(2,1)S(1)}, u32[]{:S(2)}, u32[]{:S(2)}) collective-permute-start(bf16[4,32,192]{2,1,0:T(8,128)(2,1)S(1)} %get-tuple-element.42), channel_id=1, source_target_pairs={{56,0},{0,8},{8,16},{16,24},{24,32},{32,40},{40,48},{48,56},{57,1}... | collective-permute-start | bytes 147464 | tf_op jit(solution)/shard_map/ppermute | solution.py:369
  70.3 16.3 %all-to-all-start.2 = ((bf16[32,40,128]{2,1,0:T(8,128)(2,1)}), bf16[32,40,128]{2,1,0:T(8,128)(2,1)S(1)}, u32[]{:S(2)}, u32[]{:S(2)}) async-start(bf16[32,40,128]{2,1,0:T(8,128)(2,1)} %get-tuple-element.44), calls=%async_computation.2 | async-start | bytes 655360 | tf_op jit(solution)/shard_map/all_to_all | solution.py:489
  74.2 11.2 %collective-permute-start.4 = (bf16[16,4,192]{2,1,0:T(4,128)(2,1)S(1)}, bf16[16,4,192]{2,1,0:T(4,128)(2,1)S(1)}, u32[]{:S(2)}, u32[]{:S(2)}) collective-permute-start(bf16[16,4,192]{2,1,0:T(4,128)(2,1)S(1)} %get-tuple-element.43), channel_id=1, source_target_pairs={{7,0},{0,1},{1,2},{2,3},{3,4},{4,5},{5,6},{6,7},{15,8},{8,9},{9,10... | collective-permute-start | bytes 73736 | tf_op jit(solution)/shard_map/ppermute | solution.py:369

commit v6 on v5

--- a/solution.py
+++ b/solution.py
@@ -152,11 +152,11 @@
     perm_ref,
     apart_ref,
     rows_ref,
-    ds_ref,
+    dn_ref,
+    xhat_ref,
+    rstd_ref,
     pack_ref,
     ext_ref,
-    xhat_ref,
-    rstd_ref,
     normed_ref,
     grad_ref,
     q_ref,
@@ -259,14 +259,7 @@
     xhat = xhat_ref[...]
     norm_scale = jnp.sum(d_normed * xhat, 0, keepdims=True)
     norm_bias = jnp.sum(d_normed, 0, keepdims=True)
-    d_hat = d_normed * ls
-    mean_hat = jnp.sum(d_hat, -1, keepdims=True) * (1.0 / CHAN)
-    mean_mix = jnp.sum(d_hat * xhat, -1, keepdims=True) * (1.0 / CHAN)
-    d_shifted = rstd_ref[...] * (d_hat - mean_hat - xhat * mean_mix)
-    for win in range(8):
-        wr, wc = win // 4, win % 4
-        block = d_shifted[TOK * win : TOK * win + TOK].reshape(WIN, WIN, CHAN)
-        ds_ref[WIN * wr : WIN * wr + WIN, WIN * wc : WIN * wc + WIN, :] = block
+    dn_ref[...] = d_normed
 
     normed = normed_ref[...].T
     weights = jnp.concatenate(
@@ -313,11 +306,24 @@
     return jnp.concatenate(tiles, axis=0).astype(BF)
 
 
-def sum_kernel(got_ref, ds_ref, place_ref, out_ref, edge_ref):
+def finish_kernel(dn_ref, xhat_ref, rstd_ref, rows_ref, mark_ref, ds_ref, edge_ref):
+    xhat = xhat_ref[...]
+    d_hat = dn_ref[...] * rows_ref[0:1, 0:CHAN]
+    mean_hat = jnp.sum(d_hat, -1, keepdims=True) * (1.0 / CHAN)
+    mean_mix = jnp.sum(d_hat * xhat, -1, keepdims=True) * (1.0 / CHAN)
+    d_shifted = rstd_ref[...] * (d_hat - mean_hat - xhat * mean_mix)
+    for win in range(8):
+        wr, wc = win // 4, win % 4
+        block = d_shifted[TOK * win : TOK * win + TOK].reshape(WIN, WIN, CHAN)
+        ds_ref[WIN * wr : WIN * wr + WIN, WIN * wc : WIN * wc + WIN, :] = block
+    edge_ref[...] = ds_ref[ROWS - SHIFT : ROWS].astype(BF)
+
+
+def sum_kernel(got_ref, place_ref, out_ref, mark_ref):
+    mark_ref[...] = jnp.zeros_like(mark_ref)
     total = part_sum(got_ref, place_ref)
     for i in range(out_ref.shape[0]):
         out_ref[i] = total
-    edge_ref[...] = ds_ref[ROWS - SHIFT : ROWS].astype(BF)
 
 
 def sum_edge_kernel(got_ref, above_ref, ds_ref, place_ref, out_ref, edge_ref):
@@ -404,13 +410,13 @@
     return kernel_call(
         main_kernel,
         (
-            shape((ROWS, COLS, CHAN)),
+            shape((tokens, CHAN)),
+            shape((tokens, CHAN)),
+            shape((tokens, 1)),
             shape((CHUNKS, PACK, 128), BF),
         ),
         [
             pltpu.VMEM((ROWS + 8, COLS + 8, CHAN), F32),
-            pltpu.VMEM((tokens, CHAN), F32),
-            pltpu.VMEM((tokens, 1), F32),
         ]
         + [pltpu.VMEM((tokens, CHAN), BF)] * 10
         + [pltpu.VMEM((8, HEADS * TOK, CHAN), BF)] * 2
@@ -424,12 +430,18 @@
 WHOLE = pl.BlockSpec(memory_space=pltpu.VMEM)
 
 
-def chunk_sum(got, copies, d_shifted, place):
+def chunk_sum(got, copies, place):
     return kernel_call(
         sum_kernel,
-        (shape((copies,) + got.shape[1:], BF), shape((SHIFT, COLS, CHAN), BF)),
-        in_specs=[WHOLE, WHOLE, SMALL],
-    )(got, d_shifted, place)
+        (shape((copies,) + got.shape[1:], BF), shape((8, 128))),
+        in_specs=[WHOLE, SMALL],
+    )(got, place)
+
+
+def finish(*args):
+    return kernel_call(
+        finish_kernel, (shape((ROWS, COLS, CHAN)), shape((SHIFT, COLS, CHAN), BF))
+    )(*args)
 
 
 def chunk_sum_edge(got, copies, above, d_shifted, place):
@@ -477,11 +489,12 @@
     )
     place = lax.axis_index(FIRST).astype(jnp.int32)[None]
     rows, place = lax.optimization_barrier((rows, place))
-    d_shifted, packed = main(
+    d_normed, xhat, rstd, packed = main(
         x, g, row, col, corner, parts, proj_weight, bias, perm, apart, rows
     )
     got = lax.all_to_all(packed, FIRST, 0, 0, tiled=True)
-    part, edge = chunk_sum(got, 16, d_shifted, place)
+    part, mark = chunk_sum(got, 16, place)
+    d_shifted, edge = finish(d_normed, xhat, rstd, rows, mark)
     above = moved(edge, ROW, 1)
     got = lax.all_to_all(part, SECOND, 0, 0, tiled=True)
     whole, edge = chunk_sum_edge(got, CHUNKS, above, d_shifted, place)

time: 88.7 us -> 88.4 us (level)
    pallas_call x2 -> x3, Pallas kernels: 4.76 us -> 4.96 us  [the longest x1 3.89 us: main(): kernel_call(main_kernel, (shape((tokens, CHAN)), shape((tokens, CHAN)), s...]
where the time goes in v6:
time: 88.4 us; the launch traced here: 87.2 us
  starting transfers between devices  40.6 us (46%)
  blocking collectives  20.2 us (23%)
  waiting for transfers between devices  14.2 us (16%)
  Pallas kernels  8.3 us (9%)
  local copies, waits for them, and re-layouts  1.99 us (2%)
  other arithmetic  0.93 us (1%)
  between operations  0.93 us (1%)
    ppermute x4, starting transfers between devices, moved(): lax.ppermute(block, axes, [((i - distance) % count, i) for i in range(cou...  23.1 us
    all_to_all x1, blocking collectives, on_device(): got = lax.all_to_all(packed, FIRST, 0, 0, tiled=True)  20.2 us
    ppermute x4, waiting for transfers between devices, moved(): lax.ppermute(block, axes, [((i - distance) % count, i) for i in range(cou...  9.78 us
    all_to_all x1, starting transfers between devices, on_device(): got = lax.all_to_all(part, SECOND, 0, 0, tiled=True)  8.32 us
    ppermute x1, starting transfers between devices, moved_corner(): return lax.ppermute(block, ROW + COL, pairs)  5.35 us
    pallas_call x1, Pallas kernels, main(): kernel_call(main_kernel, (shape((tokens, CHAN)), shape((tokens, CHAN)), s...  3.89 us
    all_to_all x1, starting transfers between devices, on_device(): gathered = lax.all_to_all(whole, FIRST, 0, 0, tiled=True)  3.88 us
    all_to_all x1, waiting for transfers between devices, on_device(): got = lax.all_to_all(part, SECOND, 0, 0, tiled=True)  3.85 us
  transfers between devices with their start and end apart: 7, of which 4 were waited for; matrix products, arithmetic and copies ran while one was open for 1% of the time, Pallas kernels for 2%

profile of v6, /device:TPU:1, one launch (start us, length us, event | category | flops | bytes accessed | tf_op | source)
XLA Modules:
  0.0 87.2 jit_solution(8395089825397324074)
XLA Ops:
  0.6 0.0 copy-start
  0.6 0.9 %copy-done = bf16[1,16,32,192]{3,2,1,0:T(8,128)(2,1)S(1)} copy-done((bf16[1,16,32,192]{3,2,1,0:T(8,128)(2,1)S(1)}, bf16[1,16,32,192]{3,2,1,0:T(8,128)(2,1)}, u32[]{:S(2)}) %copy-start) | copy-done | bytes 196632
  1.6 0.0 copy-start.2
  1.6 0.9 %copy-done.2 = bf16[1,16,32,192]{3,2,1,0:T(8,128)(2,1)S(1)} copy-done((bf16[1,16,32,192]{3,2,1,0:T(8,128)(2,1)S(1)}, bf16[1,16,32,192]{3,2,1,0:T(8,128)(2,1)}, u32[]{:S(2)}) %copy-start.2) | copy-done | bytes 196632
  2.5 0.0 copy-start.4
  2.5 0.0 copy-start.6
  2.5 0.0 copy-start.7
  2.5 0.0 copy-start.8
  2.6 0.0 copy-start.9
  2.6 0.0 copy-start.10
  2.6 0.0 copy-start.11
  2.6 0.0 copy-start.5
  2.6 8.9 %collective-permute-start = (bf16[2,4,32,192]{3,2,1,0:T(8,128)(2,1)S(1)}, bf16[2,4,32,192]{3,2,1,0:T(8,128)(2,1)S(1)}, u32[]{:S(2)}, u32[]{:S(2)}) collective-permute-start(bf16[2,4,32,192]{3,2,1,0:T(8,128)(2,1)S(1)} %get-tuple-element.34), channel_id=1, source_target_pairs={{8,0},{16,8},{24,16},{32,24},{40,32},{48,40},{56,48},{0,56},{9,1},... | collective-permute-start | bytes 294920 | tf_op jit(solution)/shard_map/ppermute | solution.py:375
  11.5 0.0 copy-start.3
  11.6 0.0 copy-start.1
  11.6 0.1 pad_maximum_fusion.1
  11.7 7.6 %collective-permute-start.1 = (bf16[2,16,4,192]{3,2,1,0:T(4,128)(2,1)S(1)}, bf16[2,16,4,192]{3,2,1,0:T(4,128)(2,1)S(1)}, u32[]{:S(2)}, u32[]{:S(2)}) collective-permute-start(bf16[2,16,4,192]{3,2,1,0:T(4,128)(2,1)S(1)} %pad_maximum_fusion.1), channel_id=1, source_target_pairs={{1,0},{2,1},{3,2},{4,3},{5,4},{6,5},{7,6},{0,7},{9,8},{10,9},{11,1... | collective-permute-start | bytes 147464 | tf_op jit(solution)/shard_map/ppermute | solution.py:375
  19.3 5.4 %collective-permute-start.2 = (bf16[2,4,4,192]{3,2,1,0:T(4,128)(2,1)S(1)}, bf16[2,4,4,192]{3,2,1,0:T(4,128)(2,1)S(1)}, u32[]{:S(2)}, u32[]{:S(2)}) collective-permute-start(bf16[2,4,4,192]{3,2,1,0:T(4,128)(2,1)S(1)} %get-tuple-element.35), channel_id=1, source_target_pairs={{9,0},{10,1},{11,2},{12,3},{13,4},{14,5},{15,6},{8,7},{17,8},{18,9... | collective-permute-start | bytes 36872 | tf_op jit(solution)/shard_map/ppermute | solution.py:382
  24.6 0.0 copy-done.4
  24.6 0.0 copy-done.6
  24.6 0.0 copy-done.7
  24.7 0.0 copy-done.8
  24.7 0.0 copy-done.9
  24.7 0.0 copy-done.10
  24.7 0.0 copy-done.5
  24.7 1.6 %shard_map.162 = (f32[64,384]{1,0:T(8,128)S(1)}, bf16[256,256]{1,0:T(8,128)(2,1)S(1)}, f32[8,64,128]{2,1,0:T(8,128)S(1)}, bf16[3,192,192]{2,1,0:T(8,128)(2,1)S(1)}, f32[8,576]{1,0:T(8,128)S(1)}) custom-call(s32[64,64]{1,0:T(8,128)S(1)} %copy-done.5, f32[6,225]{1,0:T(8,128)S(1)} %bitcast.20, s32[16,32]{1,0:T(8,128)S(1)} %copy-done.7, ...), custom_call_target="tpu_custom_call" | custom-call | flops 10000000 | bytes 1000000 | tf_op jit(solution)/shard_map/pallas_call | solution.py:386
  26.3 0.0 collective-permute-done.2.corner_ref
  26.4 0.0 collective-permute-done.1.col_ref
  26.4 0.0 collective-permute-done.row_ref
  26.4 0.0 copy-done.11
  26.4 0.0 copy-done.3
  26.4 0.0 copy-done.1
  26.4 3.9 %shard_map.163 = (f32[512,192]{1,0:T(8,128)S(1)}, f32[512,192]{1,0:T(8,128)S(1)}, f32[512,1]{1,0:T(8,128)S(1)}, bf16[32,40,128]{2,1,0:T(8,128)(2,1)S(1)}) custom-call(bf16[16,32,192]{2,1,0:T(8,128)(2,1)S(1)} %bitcast.19, bf16[16,32,192]{2,1,0:T(8,128)(2,1)S(1)} %bitcast.16, bf16[2,4,32,192]{3,2,1,0:T(8,128)(2,1)S(1)} %collective-permute-done.row_ref, ...), custom_call_target="tpu_custom_call" | custom-call | flops 1000000000 | bytes 1000000 | tf_op jit(solution)/shard_map/pallas_call | solution.py:410
  30.3 20.2 %all_to_all.15.got_ref = bf16[32,40,128]{2,1,0:T(8,128)(2,1)S(1)} all-to-all(bf16[32,40,128]{2,1,0:T(8,128)(2,1)S(1)} %get-tuple-element.42), channel_id=1, replica_groups=mesh['y'=8,'zl'=4,'c'=2,'zh'=2,'x'=4] {'y','x'}, dimensions={0} | all-to-all | bytes 655360 | tf_op jit(solution)/shard_map/all_to_all | solution.py:495
  50.6 0.7 shard_map.164
  51.3 8.3 %all-to-all-start.1 = ((bf16[16,40,128]{2,1,0:T(8,128)(2,1)}), bf16[16,40,128]{2,1,0:T(8,128)(2,1)S(1)}, u32[]{:S(2)}, u32[]{:S(2)}) async-start(bf16[16,40,128]{2,1,0:T(8,128)(2,1)} %get-tuple-element.44), calls=%async_computation.1 | async-start | bytes 327680 | tf_op jit(solution)/shard_map/all_to_all | solution.py:499
  59.6 0.3 shard_map.165
  60.0 3.5 %collective-permute-start.3 = (bf16[4,32,192]{2,1,0:T(8,128)(2,1)S(1)}, bf16[4,32,192]{2,1,0:T(8,128)(2,1)S(1)}, u32[]{:S(2)}, u32[]{:S(2)}) collective-permute-start(bf16[4,32,192]{2,1,0:T(8,128)(2,1)S(1)} %get-tuple-element.49), channel_id=1, source_target_pairs={{56,0},{0,8},{8,16},{16,24},{24,32},{32,40},{40,48},{48,56},{57,1}... | collective-permute-start | bytes 147464 | tf_op jit(solution)/shard_map/ppermute | solution.py:375
  63.5 1.9 %collective-permute-done.3.above_ref = bf16[4,32,192]{2,1,0:T(8,128)(2,1)S(1)} collective-permute-done((bf16[4,32,192]{2,1,0:T(8,128)(2,1)S(1)}, bf16[4,32,192]{2,1,0:T(8,128)(2,1)S(1)}, u32[]{:S(2)}, u32[]{:S(2)}) %collective-permute-start.3) | collective-permute-done | bytes 49184 | tf_op jit(solution)/shard_map/ppermute | solution.py:375
  65.4 3.8 %all-to-all-done.1.got_ref = bf16[16,40,128]{2,1,0:T(8,128)(2,1)S(1)} async-done(((bf16[16,40,128]{2,1,0:T(8,128)(2,1)}), bf16[16,40,128]{2,1,0:T(8,128)(2,1)S(1)}, u32[]{:S(2)}, u32[]{:S(2)}) %all-to-all-start.1) | async-done | bytes 163872 | tf_op jit(solution)/shard_map/all_to_all | solution.py:499
  69.3 0.8 shard_map.166
  70.1 3.9 %all-to-all-start.2 = ((bf16[32,40,128]{2,1,0:T(8,128)(2,1)}), bf16[32,40,128]{2,1,0:T(8,128)(2,1)S(1)}, u32[]{:S(2)}, u32[]{:S(2)}) async-start(bf16[32,40,128]{2,1,0:T(8,128)(2,1)} %get-tuple-element.52), calls=%async_computation.2 | async-start | bytes 655360 | tf_op jit(solution)/shard_map/all_to_all | solution.py:502
  74.0 3.0 %collective-permute-start.4 = (bf16[16,4,192]{2,1,0:T(4,128)(2,1)S(1)}, bf16[16,4,192]{2,1,0:T(4,128)(2,1)S(1)}, u32[]{:S(2)}, u32[]{:S(2)}) collective-permute-start(bf16[16,4,192]{2,1,0:T(4,128)(2,1)S(1)} %get-tuple-element.51), channel_id=1, source_target_pairs={{7,0},{0,1},{1,2},{2,3},{3,4},{4,5},{5,6},{6,7},{15,8},{8,9},{9,10... | collective-permute-start | bytes 73736 | tf_op jit(solution)/shard_map/ppermute | solution.py:375
  77.1 7.8 %collective-permute-done.4 = bf16[16,4,192]{2,1,0:T(4,128)(2,1)S(1)} collective-permute-done((bf16[16,4,192]{2,1,0:T(4,128)(2,1)S(1)}, bf16[16,4,192]{2,1,0:T(4,128)(2,1)S(1)}, u32[]{:S(2)}, u32[]{:S(2)}) %collective-permute-start.4) | collective-permute-done | bytes 24608 | tf_op jit(solution)/shard_map/ppermute | solution.py:375
  84.9 0.8 fusion.1
  85.8 0.5 all-to-all-done.2.got_ref
  86.3 0.9 %shard_map.167 = (f32[192,576]{1,0:T(8,128)}, f32[576]{0:T(1024)}, f32[192,192]{1,0:T(8,128)}, f32[192]{0:T(256)}, f32[192]{0:T(256)}, /*index=5*/f32[192]{0:T(256)}, f32[6,225]{1,0:T(8,128)}) custom-call(bf16[32,40,128]{2,1,0:T(8,128)(2,1)S(1)} %all-to-all-done.2.got_ref), custom_call_target="tpu_custom_call" | custom-call | flops 10000000 | bytes 1000000 | tf_op jit(solution)/shard_map/pallas_call | solution.py:456
  (6 shorter events, 0.1 us)
Async XLA Ops:
  0.6 1.0 %copy-start = (bf16[1,16,32,192]{3,2,1,0:T(8,128)(2,1)S(1)}, bf16[1,16,32,192]{3,2,1,0:T(8,128)(2,1)}, u32[]{:S(2)}) copy-start(bf16[1,16,32,192]{3,2,1,0:T(8,128)(2,1)} %param.11) | copy-start | bytes 589828
  1.6 0.9 %copy-start.2 = (bf16[1,16,32,192]{3,2,1,0:T(8,128)(2,1)S(1)}, bf16[1,16,32,192]{3,2,1,0:T(8,128)(2,1)}, u32[]{:S(2)}) copy-start(bf16[1,16,32,192]{3,2,1,0:T(8,128)(2,1)} %param.10) | copy-start | bytes 589828
  2.5 22.1 %copy-start.4 = (bf16[192,576]{1,0:T(8,128)(2,1)S(1)}, bf16[192,576]{1,0:T(8,128)(2,1)}, u32[]{:S(2)}) copy-start(bf16[192,576]{1,0:T(8,128)(2,1)} %w_ref.1) | copy-start | bytes 663556
  2.5 22.1 %copy-start.6 = (f32[225,6]{0,1:T(8,128)S(1)}, f32[225,6]{0,1:T(8,128)}, u32[]{:S(2)}) copy-start(f32[225,6]{0,1:T(8,128)} %param.18) | copy-start | bytes 16204
  2.5 22.1 %copy-start.7 = (s32[16,32]{1,0:T(8,128)S(1)}, s32[16,32]{1,0:T(8,128)}, u32[]{:S(2)}) copy-start(s32[16,32]{1,0:T(8,128)} %ids_ref.1) | copy-start | bytes 6148
  2.5 22.1 %copy-start.8 = (f32[576]{0:T(1024)S(1)}, f32[576]{0:T(1024)}, u32[]{:S(2)}) copy-start(f32[576]{0:T(1024)} %qb_ref.1) | copy-start | bytes 6916
  2.6 22.1 %copy-start.9 = (f32[192]{0:T(256)S(1)}, f32[192]{0:T(256)}, u32[]{:S(2)}) copy-start(f32[192]{0:T(256)} %ls_ref.1) | copy-start | bytes 2308
  2.6 22.1 %copy-start.10 = (f32[192]{0:T(256)S(1)}, f32[192]{0:T(256)}, u32[]{:S(2)}) copy-start(f32[192]{0:T(256)} %lb_ref.1) | copy-start | bytes 2308
  2.6 23.8 %copy-start.11 = (bf16[192,192]{1,0:T(8,128)(2,1)S(1)}, bf16[192,192]{1,0:T(8,128)(2,1)}, u32[]{:S(2)}) copy-start(bf16[192,192]{1,0:T(8,128)(2,1)} %wp_ref.1) | copy-start | bytes 221188
  2.6 22.1 %copy-start.5 = (s32[64,64]{1,0:T(8,128)S(1)}, s32[64,64]{1,0:T(8,128)}, u32[]{:S(2)}) copy-start(s32[64,64]{1,0:T(8,128)} %pos_ref.1) | copy-start | bytes 49156
  2.6 23.8 %collective-permute-start = (bf16[2,4,32,192]{3,2,1,0:T(8,128)(2,1)S(1)}, bf16[2,4,32,192]{3,2,1,0:T(8,128)(2,1)S(1)}, u32[]{:S(2)}, u32[]{:S(2)}) collective-permute-start(bf16[2,4,32,192]{3,2,1,0:T(8,128)(2,1)S(1)} %get-tuple-element.34), channel_id=1, source_target_pairs={{8,0},{16,8},{24,16},{32,24},{40,32},{48,40},{56,48},{0,56},{9,1},... | collective-permute-start | bytes 294920 | tf_op jit(solution)/shard_map/ppermute | solution.py:375
  11.5 14.8 %copy-start.3 = (bf16[1,16,32,192]{3,2,1,0:T(8,128)(2,1)S(1)}, bf16[1,16,32,192]{3,2,1,0:T(8,128)(2,1)}, u32[]{:S(2)}) copy-start(bf16[1,16,32,192]{3,2,1,0:T(8,128)(2,1)} %param.10) | copy-start | bytes 589828
  11.6 14.8 %copy-start.1 = (bf16[1,16,32,192]{3,2,1,0:T(8,128)(2,1)S(1)}, bf16[1,16,32,192]{3,2,1,0:T(8,128)(2,1)}, u32[]{:S(2)}) copy-start(bf16[1,16,32,192]{3,2,1,0:T(8,128)(2,1)} %param.11) | copy-start | bytes 589828
  11.7 14.7 %collective-permute-start.1 = (bf16[2,16,4,192]{3,2,1,0:T(4,128)(2,1)S(1)}, bf16[2,16,4,192]{3,2,1,0:T(4,128)(2,1)S(1)}, u32[]{:S(2)}, u32[]{:S(2)}) collective-permute-start(bf16[2,16,4,192]{3,2,1,0:T(4,128)(2,1)S(1)} %pad_maximum_fusion.1), channel_id=1, source_target_pairs={{1,0},{2,1},{3,2},{4,3},{5,4},{6,5},{7,6},{0,7},{9,8},{10,9},{11,1... | collective-permute-start | bytes 147464 | tf_op jit(solution)/shard_map/ppermute | solution.py:375
  19.3 7.1 %collective-permute-start.2 = (bf16[2,4,4,192]{3,2,1,0:T(4,128)(2,1)S(1)}, bf16[2,4,4,192]{3,2,1,0:T(4,128)(2,1)S(1)}, u32[]{:S(2)}, u32[]{:S(2)}) collective-permute-start(bf16[2,4,4,192]{3,2,1,0:T(4,128)(2,1)S(1)} %get-tuple-element.35), channel_id=1, source_target_pairs={{9,0},{10,1},{11,2},{12,3},{13,4},{14,5},{15,6},{8,7},{17,8},{18,9... | collective-permute-start | bytes 36872 | tf_op jit(solution)/shard_map/ppermute | solution.py:382
  51.3 18.0 %all-to-all-start.1 = ((bf16[16,40,128]{2,1,0:T(8,128)(2,1)}), bf16[16,40,128]{2,1,0:T(8,128)(2,1)S(1)}, u32[]{:S(2)}, u32[]{:S(2)}) async-start(bf16[16,40,128]{2,1,0:T(8,128)(2,1)} %get-tuple-element.44), calls=%async_computation.1 | async-start | bytes 327680 | tf_op jit(solution)/shard_map/all_to_all | solution.py:499
  60.0 5.5 %collective-permute-start.3 = (bf16[4,32,192]{2,1,0:T(8,128)(2,1)S(1)}, bf16[4,32,192]{2,1,0:T(8,128)(2,1)S(1)}, u32[]{:S(2)}, u32[]{:S(2)}) collective-permute-start(bf16[4,32,192]{2,1,0:T(8,128)(2,1)S(1)} %get-tuple-element.49), channel_id=1, source_target_pairs={{56,0},{0,8},{8,16},{16,24},{24,32},{32,40},{40,48},{48,56},{57,1}... | collective-permute-start | bytes 147464 | tf_op jit(solution)/shard_map/ppermute | solution.py:375
  70.1 16.2 %all-to-all-start.2 = ((bf16[32,40,128]{2,1,0:T(8,128)(2,1)}), bf16[32,40,128]{2,1,0:T(8,128)(2,1)S(1)}, u32[]{:S(2)}, u32[]{:S(2)}) async-start(bf16[32,40,128]{2,1,0:T(8,128)(2,1)} %get-tuple-element.52), calls=%async_computation.2 | async-start | bytes 655360 | tf_op jit(solution)/shard_map/all_to_all | solution.py:502
  74.0 10.9 %collective-permute-start.4 = (bf16[16,4,192]{2,1,0:T(4,128)(2,1)S(1)}, bf16[16,4,192]{2,1,0:T(4,128)(2,1)S(1)}, u32[]{:S(2)}, u32[]{:S(2)}) collective-permute-start(bf16[16,4,192]{2,1,0:T(4,128)(2,1)S(1)} %get-tuple-element.51), channel_id=1, source_target_pairs={{7,0},{0,1},{1,2},{2,3},{3,4},{4,5},{5,6},{6,7},{15,8},{8,9},{9,10... | collective-permute-start | bytes 73736 | tf_op jit(solution)/shard_map/ppermute | solution.py:375

commit v7 on v6

--- a/solution.py
+++ b/solution.py
@@ -335,8 +335,26 @@
 
 
 def unpack_kernel(
-    got_ref, w_ref, wb_ref, p_ref, pb_ref, ns_ref, nb_ref, table_ref, all_ref
+    got_ref,
+    g_ref,
+    ds_ref,
+    above_ref,
+    left_ref,
+    gx_ref,
+    w_ref,
+    wb_ref,
+    p_ref,
+    pb_ref,
+    ns_ref,
+    nb_ref,
+    table_ref,
+    all_ref,
+    back_ref,
 ):
+    back_ref[:, 0:SHIFT] = left_ref[...].astype(F32)
+    back_ref[0:SHIFT, SHIFT:COLS] = above_ref[:, 0 : COLS - SHIFT].astype(F32)
+    back_ref[SHIFT:ROWS, SHIFT:COLS] = ds_ref[0 : ROWS - SHIFT, 0 : COLS - SHIFT]
+    gx_ref[...] = (g_ref[...].astype(F32) + back_ref[...]).astype(BF)
     for chunk in range(30):
         tiles = got_ref[chunk].astype(F32)
         for tile in range(5 * chunk, 5 * chunk + 5):
@@ -452,10 +470,11 @@
     )(got, above, d_shifted, place)
 
 
-def unpack(got):
+def unpack(*args):
     return kernel_call(
         unpack_kernel,
         (
+            shape((ROWS, COLS, CHAN), BF),
             shape((CHAN, 3 * CHAN)),
             shape((3 * CHAN,)),
             shape((CHAN, CHAN)),
@@ -464,8 +483,8 @@
             shape((CHAN,)),
             shape((HEADS, TABLE)),
         ),
-        [pltpu.VMEM((CHAN + 8, 4 * CHAN), F32)],
-    )(got)
+        [pltpu.VMEM((CHAN + 8, 4 * CHAN), F32), pltpu.VMEM((ROWS, COLS, CHAN), F32)],
+    )(*args)
 
 
 def on_device(
@@ -500,11 +519,8 @@
     whole, edge = chunk_sum_edge(got, CHUNKS, above, d_shifted, place)
     left = moved(edge, COL, 1)
     gathered = lax.all_to_all(whole, FIRST, 0, 0, tiled=True)
-    back = jnp.concatenate([above.astype(F32), d_shifted[: ROWS - SHIFT]], axis=0)
-    back = jnp.concatenate([left.astype(F32), back[:, : COLS - SHIFT]], axis=1)
-    grad_x = (g.astype(F32) + back).astype(BF)[None]
-    w, wb, p, pb, ns, nb, table = unpack(gathered)
-    return (grad_x, w, wb, p, pb, ns, nb, table.T)
+    grad_x, w, wb, p, pb, ns, nb, table = unpack(gathered, g, d_shifted, above, left)
+    return (grad_x[None], w, wb, p, pb, ns, nb, table.T)
 
 
 def solution(mesh):

time: 88.4 us -> 88.5 us (level)
  waiting for transfers between devices: 14.2 us -> 15.1 us
    all_to_all x1, waiting for transfers between devices: 0.53 us -> 1.44 us  [on_device(): gathered = lax.all_to_all(whole, FIRST, 0, 0, tiled=True)]
  transfers between devices with their start and end apart: 7 -> 7, of which waited for: 4 -> 4; matrix products, arithmetic and copies ran while one was open for 1% -> 0% of each run, Pallas kernels for 2% -> 2%
where the time goes in v7:
time: 88.5 us; the launch traced here: 87.3 us
  starting transfers between devices  40.6 us (46%)
  blocking collectives  20.2 us (23%)
  waiting for transfers between devices  15.1 us (17%)
  Pallas kernels  8.4 us (9%)
  local copies, waits for them, and re-layouts  1.97 us (2%)
  between operations  0.9 us (1%)
    ppermute x4, starting transfers between devices, moved(): lax.ppermute(block, axes, [((i - distance) % count, i) for i in range(cou...  23.1 us
    all_to_all x1, blocking collectives, on_device(): got = lax.all_to_all(packed, FIRST, 0, 0, tiled=True)  20.2 us
    ppermute x4, waiting for transfers between devices, moved(): lax.ppermute(block, axes, [((i - distance) % count, i) for i in range(cou...  9.81 us
    all_to_all x1, starting transfers between devices, on_device(): got = lax.all_to_all(part, SECOND, 0, 0, tiled=True)  8.32 us
    ppermute x1, starting transfers between devices, moved_corner(): return lax.ppermute(block, ROW + COL, pairs)  5.35 us
    pallas_call x1, Pallas kernels, main(): kernel_call(main_kernel, (shape((tokens, CHAN)), shape((tokens, CHAN)), s...  3.89 us
    all_to_all x1, starting transfers between devices, on_device(): gathered = lax.all_to_all(whole, FIRST, 0, 0, tiled=True)  3.87 us
    all_to_all x1, waiting for transfers between devices, on_device(): got = lax.all_to_all(part, SECOND, 0, 0, tiled=True)  3.85 us
  transfers between devices with their start and end apart: 7, of which 4 were waited for; matrix products, arithmetic and copies ran while one was open for 0% of the time, Pallas kernels for 2%

profile of v7, /device:TPU:1, one launch (start us, length us, event | category | flops | bytes accessed | tf_op | source)
XLA Modules:
  0.0 87.3 jit_solution(4515634677299908796)
XLA Ops:
  0.6 0.0 copy-start
  0.6 0.9 %copy-done = bf16[1,16,32,192]{3,2,1,0:T(8,128)(2,1)S(1)} copy-done((bf16[1,16,32,192]{3,2,1,0:T(8,128)(2,1)S(1)}, bf16[1,16,32,192]{3,2,1,0:T(8,128)(2,1)}, u32[]{:S(2)}) %copy-start) | copy-done | bytes 196632
  1.6 0.0 copy-start.2
  1.6 0.9 %copy-done.2 = bf16[1,16,32,192]{3,2,1,0:T(8,128)(2,1)S(1)} copy-done((bf16[1,16,32,192]{3,2,1,0:T(8,128)(2,1)S(1)}, bf16[1,16,32,192]{3,2,1,0:T(8,128)(2,1)}, u32[]{:S(2)}) %copy-start.2) | copy-done | bytes 196632
  2.5 0.0 copy-start.4
  2.5 0.0 copy-start.6
  2.5 0.0 copy-start.7
  2.5 0.0 copy-start.8
  2.6 0.0 copy-start.9
  2.6 0.0 copy-start.10
  2.6 0.0 copy-start.11
  2.6 0.0 copy-start.5
  2.6 8.9 %collective-permute-start = (bf16[2,4,32,192]{3,2,1,0:T(8,128)(2,1)S(1)}, bf16[2,4,32,192]{3,2,1,0:T(8,128)(2,1)S(1)}, u32[]{:S(2)}, u32[]{:S(2)}) collective-permute-start(bf16[2,4,32,192]{3,2,1,0:T(8,128)(2,1)S(1)} %get-tuple-element.35), channel_id=1, source_target_pairs={{8,0},{16,8},{24,16},{32,24},{40,32},{48,40},{56,48},{0,56},{9,1},... | collective-permute-start | bytes 294920 | tf_op jit(solution)/shard_map/ppermute | solution.py:393
  11.5 0.0 copy-start.3
  11.6 0.0 copy-start.1
  11.6 0.1 pad_maximum_fusion
  11.7 7.6 %collective-permute-start.1 = (bf16[2,16,4,192]{3,2,1,0:T(4,128)(2,1)S(1)}, bf16[2,16,4,192]{3,2,1,0:T(4,128)(2,1)S(1)}, u32[]{:S(2)}, u32[]{:S(2)}) collective-permute-start(bf16[2,16,4,192]{3,2,1,0:T(4,128)(2,1)S(1)} %pad_maximum_fusion), channel_id=1, source_target_pairs={{1,0},{2,1},{3,2},{4,3},{5,4},{6,5},{7,6},{0,7},{9,8},{10,9},{11,1... | collective-permute-start | bytes 147464 | tf_op jit(solution)/shard_map/ppermute | solution.py:393
  19.3 5.4 %collective-permute-start.2 = (bf16[2,4,4,192]{3,2,1,0:T(4,128)(2,1)S(1)}, bf16[2,4,4,192]{3,2,1,0:T(4,128)(2,1)S(1)}, u32[]{:S(2)}, u32[]{:S(2)}) collective-permute-start(bf16[2,4,4,192]{3,2,1,0:T(4,128)(2,1)S(1)} %get-tuple-element.36), channel_id=1, source_target_pairs={{9,0},{10,1},{11,2},{12,3},{13,4},{14,5},{15,6},{8,7},{17,8},{18,9... | collective-permute-start | bytes 36872 | tf_op jit(solution)/shard_map/ppermute | solution.py:400
  24.6 0.0 copy-done.4
  24.6 0.0 copy-done.6
  24.6 0.0 copy-done.7
  24.7 0.0 copy-done.8
  24.7 0.0 copy-done.9
  24.7 0.0 copy-done.10
  24.7 0.0 copy-done.5
  24.7 1.6 %shard_map.162 = (f32[64,384]{1,0:T(8,128)S(1)}, bf16[256,256]{1,0:T(8,128)(2,1)S(1)}, f32[8,64,128]{2,1,0:T(8,128)S(1)}, bf16[3,192,192]{2,1,0:T(8,128)(2,1)S(1)}, f32[8,576]{1,0:T(8,128)S(1)}) custom-call(s32[64,64]{1,0:T(8,128)S(1)} %copy-done.5, f32[6,225]{1,0:T(8,128)S(1)} %bitcast.17, s32[16,32]{1,0:T(8,128)S(1)} %copy-done.7, ...), custom_call_target="tpu_custom_call" | custom-call | flops 10000000 | bytes 1000000 | tf_op jit(solution)/shard_map/pallas_call | solution.py:404
  26.3 0.0 collective-permute-done.2.corner_ref
  26.4 0.0 collective-permute-done.1.col_ref
  26.4 0.0 collective-permute-done.row_ref
  26.4 0.0 copy-done.11
  26.4 0.0 copy-done.3
  26.4 0.0 copy-done.1
  26.4 3.9 %shard_map.163 = (f32[512,192]{1,0:T(8,128)S(1)}, f32[512,192]{1,0:T(8,128)S(1)}, f32[512,1]{1,0:T(8,128)S(1)}, bf16[32,40,128]{2,1,0:T(8,128)(2,1)S(1)}) custom-call(bf16[16,32,192]{2,1,0:T(8,128)(2,1)S(1)} %bitcast.16, bf16[16,32,192]{2,1,0:T(8,128)(2,1)S(1)} %bitcast.12, bf16[2,4,32,192]{3,2,1,0:T(8,128)(2,1)S(1)} %collective-permute-done.row_ref, ...), custom_call_target="tpu_custom_call" | custom-call | flops 1000000000 | bytes 1000000 | tf_op jit(solution)/shard_map/pallas_call | solution.py:428
  30.3 20.2 %all_to_all.15.got_ref = bf16[32,40,128]{2,1,0:T(8,128)(2,1)S(1)} all-to-all(bf16[32,40,128]{2,1,0:T(8,128)(2,1)S(1)} %get-tuple-element.43), channel_id=1, replica_groups=mesh['y'=8,'zl'=4,'c'=2,'zh'=2,'x'=4] {'y','x'}, dimensions={0} | all-to-all | bytes 655360 | tf_op jit(solution)/shard_map/all_to_all | solution.py:514
  50.6 0.7 shard_map.164
  51.3 8.3 %all-to-all-start.1 = ((bf16[16,40,128]{2,1,0:T(8,128)(2,1)}), bf16[16,40,128]{2,1,0:T(8,128)(2,1)S(1)}, u32[]{:S(2)}, u32[]{:S(2)}) async-start(bf16[16,40,128]{2,1,0:T(8,128)(2,1)} %get-tuple-element.45), calls=%async_computation.1 | async-start | bytes 327680 | tf_op jit(solution)/shard_map/all_to_all | solution.py:518
  59.6 0.3 shard_map.165
  60.0 3.5 %collective-permute-start.3 = (bf16[4,32,192]{2,1,0:T(8,128)(2,1)S(1)}, bf16[4,32,192]{2,1,0:T(8,128)(2,1)S(1)}, u32[]{:S(2)}, u32[]{:S(2)}) collective-permute-start(bf16[4,32,192]{2,1,0:T(8,128)(2,1)S(1)} %get-tuple-element.50), channel_id=1, source_target_pairs={{56,0},{0,8},{8,16},{16,24},{24,32},{32,40},{40,48},{48,56},{57,1}... | collective-permute-start | bytes 147464 | tf_op jit(solution)/shard_map/ppermute | solution.py:393
  63.5 1.9 %collective-permute-done.3.above_ref = bf16[4,32,192]{2,1,0:T(8,128)(2,1)S(1)} collective-permute-done((bf16[4,32,192]{2,1,0:T(8,128)(2,1)S(1)}, bf16[4,32,192]{2,1,0:T(8,128)(2,1)S(1)}, u32[]{:S(2)}, u32[]{:S(2)}) %collective-permute-start.3) | collective-permute-done | bytes 49184 | tf_op jit(solution)/shard_map/ppermute | solution.py:393
  65.4 3.8 %all-to-all-done.1.got_ref = bf16[16,40,128]{2,1,0:T(8,128)(2,1)S(1)} async-done(((bf16[16,40,128]{2,1,0:T(8,128)(2,1)}), bf16[16,40,128]{2,1,0:T(8,128)(2,1)S(1)}, u32[]{:S(2)}, u32[]{:S(2)}) %all-to-all-start.1) | async-done | bytes 163872 | tf_op jit(solution)/shard_map/all_to_all | solution.py:518
  69.3 0.8 shard_map.166
  70.1 3.9 %all-to-all-start.2 = ((bf16[32,40,128]{2,1,0:T(8,128)(2,1)}), bf16[32,40,128]{2,1,0:T(8,128)(2,1)S(1)}, u32[]{:S(2)}, u32[]{:S(2)}) async-start(bf16[32,40,128]{2,1,0:T(8,128)(2,1)} %get-tuple-element.52), calls=%async_computation.2 | async-start | bytes 655360 | tf_op jit(solution)/shard_map/all_to_all | solution.py:521
  73.9 3.0 %collective-permute-start.4 = (bf16[16,4,192]{2,1,0:T(4,128)(2,1)S(1)}, bf16[16,4,192]{2,1,0:T(4,128)(2,1)S(1)}, u32[]{:S(2)}, u32[]{:S(2)}) collective-permute-start(bf16[16,4,192]{2,1,0:T(4,128)(2,1)S(1)} %get-tuple-element.53), channel_id=1, source_target_pairs={{7,0},{0,1},{1,2},{2,3},{3,4},{4,5},{5,6},{6,7},{15,8},{8,9},{9,10... | collective-permute-start | bytes 73736 | tf_op jit(solution)/shard_map/ppermute | solution.py:393
  77.0 7.9 %collective-permute-done.4.left_ref = bf16[16,4,192]{2,1,0:T(4,128)(2,1)S(1)} collective-permute-done((bf16[16,4,192]{2,1,0:T(4,128)(2,1)S(1)}, bf16[16,4,192]{2,1,0:T(4,128)(2,1)S(1)}, u32[]{:S(2)}, u32[]{:S(2)}) %collective-permute-start.4) | collective-permute-done | bytes 24608 | tf_op jit(solution)/shard_map/ppermute | solution.py:393
  84.8 1.4 %all-to-all-done.2.got_ref = bf16[32,40,128]{2,1,0:T(8,128)(2,1)S(1)} async-done(((bf16[32,40,128]{2,1,0:T(8,128)(2,1)}), bf16[32,40,128]{2,1,0:T(8,128)(2,1)S(1)}, u32[]{:S(2)}, u32[]{:S(2)}) %all-to-all-start.2) | async-done | bytes 327712 | tf_op jit(solution)/shard_map/all_to_all | solution.py:521
  86.3 1.0 %shard_map.167 = (bf16[16,32,192]{2,1,0:T(8,128)(2,1)}, f32[192,576]{1,0:T(8,128)}, f32[576]{0:T(1024)}, f32[192,192]{1,0:T(8,128)}, f32[192]{0:T(256)}, /*index...) custom-call(bf16[32,40,128]{2,1,0:T(8,128)(2,1)S(1)} %all-to-all-done.2.got_ref, bf16[16,32,192]{2,1,0:T(8,128)(2,1)S(1)} %bitcast.13, ...), custom_call_target="tpu_custom_call" | custom-call | flops 10000000 | bytes 1000000 | tf_op jit(solution)/shard_map/pallas_call | solution.py:474
  (2 shorter events, 0.0 us)
Async XLA Ops:
  0.6 1.0 %copy-start = (bf16[1,16,32,192]{3,2,1,0:T(8,128)(2,1)S(1)}, bf16[1,16,32,192]{3,2,1,0:T(8,128)(2,1)}, u32[]{:S(2)}) copy-start(bf16[1,16,32,192]{3,2,1,0:T(8,128)(2,1)} %param.11) | copy-start | bytes 589828
  1.6 0.9 %copy-start.2 = (bf16[1,16,32,192]{3,2,1,0:T(8,128)(2,1)S(1)}, bf16[1,16,32,192]{3,2,1,0:T(8,128)(2,1)}, u32[]{:S(2)}) copy-start(bf16[1,16,32,192]{3,2,1,0:T(8,128)(2,1)} %param.10) | copy-start | bytes 589828
  2.5 22.1 %copy-start.4 = (bf16[192,576]{1,0:T(8,128)(2,1)S(1)}, bf16[192,576]{1,0:T(8,128)(2,1)}, u32[]{:S(2)}) copy-start(bf16[192,576]{1,0:T(8,128)(2,1)} %w_ref.1) | copy-start | bytes 663556
  2.5 22.1 %copy-start.6 = (f32[225,6]{0,1:T(8,128)S(1)}, f32[225,6]{0,1:T(8,128)}, u32[]{:S(2)}) copy-start(f32[225,6]{0,1:T(8,128)} %param.18) | copy-start | bytes 16204
  2.5 22.1 %copy-start.7 = (s32[16,32]{1,0:T(8,128)S(1)}, s32[16,32]{1,0:T(8,128)}, u32[]{:S(2)}) copy-start(s32[16,32]{1,0:T(8,128)} %ids_ref.1) | copy-start | bytes 6148
  2.5 22.1 %copy-start.8 = (f32[576]{0:T(1024)S(1)}, f32[576]{0:T(1024)}, u32[]{:S(2)}) copy-start(f32[576]{0:T(1024)} %qb_ref.1) | copy-start | bytes 6916
  2.6 22.1 %copy-start.9 = (f32[192]{0:T(256)S(1)}, f32[192]{0:T(256)}, u32[]{:S(2)}) copy-start(f32[192]{0:T(256)} %ls_ref.1) | copy-start | bytes 2308
  2.6 22.1 %copy-start.10 = (f32[192]{0:T(256)S(1)}, f32[192]{0:T(256)}, u32[]{:S(2)}) copy-start(f32[192]{0:T(256)} %lb_ref.1) | copy-start | bytes 2308
  2.6 23.8 %copy-start.11 = (bf16[192,192]{1,0:T(8,128)(2,1)S(1)}, bf16[192,192]{1,0:T(8,128)(2,1)}, u32[]{:S(2)}) copy-start(bf16[192,192]{1,0:T(8,128)(2,1)} %wp_ref.1) | copy-start | bytes 221188
  2.6 22.1 %copy-start.5 = (s32[64,64]{1,0:T(8,128)S(1)}, s32[64,64]{1,0:T(8,128)}, u32[]{:S(2)}) copy-start(s32[64,64]{1,0:T(8,128)} %pos_ref.1) | copy-start | bytes 49156
  2.6 23.8 %collective-permute-start = (bf16[2,4,32,192]{3,2,1,0:T(8,128)(2,1)S(1)}, bf16[2,4,32,192]{3,2,1,0:T(8,128)(2,1)S(1)}, u32[]{:S(2)}, u32[]{:S(2)}) collective-permute-start(bf16[2,4,32,192]{3,2,1,0:T(8,128)(2,1)S(1)} %get-tuple-element.35), channel_id=1, source_target_pairs={{8,0},{16,8},{24,16},{32,24},{40,32},{48,40},{56,48},{0,56},{9,1},... | collective-permute-start | bytes 294920 | tf_op jit(solution)/shard_map/ppermute | solution.py:393
  11.5 14.8 %copy-start.3 = (bf16[1,16,32,192]{3,2,1,0:T(8,128)(2,1)S(1)}, bf16[1,16,32,192]{3,2,1,0:T(8,128)(2,1)}, u32[]{:S(2)}) copy-start(bf16[1,16,32,192]{3,2,1,0:T(8,128)(2,1)} %param.10) | copy-start | bytes 589828
  11.6 14.8 %copy-start.1 = (bf16[1,16,32,192]{3,2,1,0:T(8,128)(2,1)S(1)}, bf16[1,16,32,192]{3,2,1,0:T(8,128)(2,1)}, u32[]{:S(2)}) copy-start(bf16[1,16,32,192]{3,2,1,0:T(8,128)(2,1)} %param.11) | copy-start | bytes 589828
  11.7 14.7 %collective-permute-start.1 = (bf16[2,16,4,192]{3,2,1,0:T(4,128)(2,1)S(1)}, bf16[2,16,4,192]{3,2,1,0:T(4,128)(2,1)S(1)}, u32[]{:S(2)}, u32[]{:S(2)}) collective-permute-start(bf16[2,16,4,192]{3,2,1,0:T(4,128)(2,1)S(1)} %pad_maximum_fusion), channel_id=1, source_target_pairs={{1,0},{2,1},{3,2},{4,3},{5,4},{6,5},{7,6},{0,7},{9,8},{10,9},{11,1... | collective-permute-start | bytes 147464 | tf_op jit(solution)/shard_map/ppermute | solution.py:393
  19.3 7.1 %collective-permute-start.2 = (bf16[2,4,4,192]{3,2,1,0:T(4,128)(2,1)S(1)}, bf16[2,4,4,192]{3,2,1,0:T(4,128)(2,1)S(1)}, u32[]{:S(2)}, u32[]{:S(2)}) collective-permute-start(bf16[2,4,4,192]{3,2,1,0:T(4,128)(2,1)S(1)} %get-tuple-element.36), channel_id=1, source_target_pairs={{9,0},{10,1},{11,2},{12,3},{13,4},{14,5},{15,6},{8,7},{17,8},{18,9... | collective-permute-start | bytes 36872 | tf_op jit(solution)/shard_map/ppermute | solution.py:400
  51.3 18.0 %all-to-all-start.1 = ((bf16[16,40,128]{2,1,0:T(8,128)(2,1)}), bf16[16,40,128]{2,1,0:T(8,128)(2,1)S(1)}, u32[]{:S(2)}, u32[]{:S(2)}) async-start(bf16[16,40,128]{2,1,0:T(8,128)(2,1)} %get-tuple-element.45), calls=%async_computation.1 | async-start | bytes 327680 | tf_op jit(solution)/shard_map/all_to_all | solution.py:518
  60.0 5.5 %collective-permute-start.3 = (bf16[4,32,192]{2,1,0:T(8,128)(2,1)S(1)}, bf16[4,32,192]{2,1,0:T(8,128)(2,1)S(1)}, u32[]{:S(2)}, u32[]{:S(2)}) collective-permute-start(bf16[4,32,192]{2,1,0:T(8,128)(2,1)S(1)} %get-tuple-element.50), channel_id=1, source_target_pairs={{56,0},{0,8},{8,16},{16,24},{24,32},{32,40},{40,48},{48,56},{57,1}... | collective-permute-start | bytes 147464 | tf_op jit(solution)/shard_map/ppermute | solution.py:393
  70.1 16.2 %all-to-all-start.2 = ((bf16[32,40,128]{2,1,0:T(8,128)(2,1)}), bf16[32,40,128]{2,1,0:T(8,128)(2,1)S(1)}, u32[]{:S(2)}, u32[]{:S(2)}) async-start(bf16[32,40,128]{2,1,0:T(8,128)(2,1)} %get-tuple-element.52), calls=%async_computation.2 | async-start | bytes 655360 | tf_op jit(solution)/shard_map/all_to_all | solution.py:521
  73.9 10.9 %collective-permute-start.4 = (bf16[16,4,192]{2,1,0:T(4,128)(2,1)S(1)}, bf16[16,4,192]{2,1,0:T(4,128)(2,1)S(1)}, u32[]{:S(2)}, u32[]{:S(2)}) collective-permute-start(bf16[16,4,192]{2,1,0:T(4,128)(2,1)S(1)} %get-tuple-element.53), channel_id=1, source_target_pairs={{7,0},{0,1},{1,2},{2,3},{3,4},{4,5},{5,6},{6,7},{15,8},{8,9},{9,10... | collective-permute-start | bytes 73736 | tf_op jit(solution)/shard_map/ppermute | solution.py:393
